TPU v7x, 32 devices: a whole 2x2x4 slice. The times are simulated.
32 devices in a mesh: dp: 4 (over y, x), fsdp: 8 (over z, core).
Axes of the slice: x: 2, y: 2, z: 4, core: 2. Of those that a mesh axis runs over, the one named last changes fastest.
Arguments:
- tokens: float32 [12288, 1536], P(('dp', 'fsdp')), may hold values from -6 to 6
- segment: int32 [12288], P(('dp', 'fsdp')), may hold values from 0 to 4, as said below
- timestep: int32 [128], P(('dp', 'fsdp')), may hold values from 0 to 999
- ada_weight: bfloat16 [1536, 4608], P('fsdp', 'dp'), may hold values from -0.15625 to 0.15625
- ada_bias: bfloat16 [4608], P(('dp', 'fsdp')), may hold values from -3 to 3
- in_weight: bfloat16 [1536, 6144], P('fsdp', 'dp'), may hold values from -1 to 1
- conv_weight: bfloat16 [3072, 4], P(('dp', 'fsdp')), may hold values from -3 to 3
- convolution_bias: bfloat16 [3072], P(('dp', 'fsdp')), may hold values from -3 to 3
- xproj_weight: bfloat16 [3072, 128], P(('dp', 'fsdp')), may hold values from -0.4375 to 0.4375
- dtproj_weight: bfloat16 [3072, 96], P(('dp', 'fsdp')), may hold values from -0.3125 to 0.3125
- dt_bias: bfloat16 [3072], P(('dp', 'fsdp')), may hold values from -6.1875 to -3.1875
- a_log: bfloat16 [3072, 16], P(('dp', 'fsdp')), may hold values from -3 to 0
- d_skip: bfloat16 [3072], P(('dp', 'fsdp')), may hold values from 0.5 to 1.5
- out_weight: bfloat16 [3072, 1536], P('fsdp', 'dp'), may hold values from -0.21875 to 0.21875
- cotangent: float32 [12288, 1536], P(('dp', 'fsdp')), may hold values from -6 to 6
Outputs:
- layer_out: float32 [12288, 1536], P(('dp', 'fsdp'))
- grad_tokens: float32 [12288, 1536], P(('dp', 'fsdp'))
- grad_ada_weight: float32 [1536, 4608], P('fsdp', 'dp')
- grad_ada_bias: float32 [4608], P(('dp', 'fsdp'))
- grad_in_weight: float32 [1536, 6144], P('fsdp', 'dp')
- grad_conv_weight: float32 [3072, 4], P(('dp', 'fsdp'))
- grad_conv_bias: float32 [3072], P(('dp', 'fsdp'))
- grad_xproj_weight: float32 [3072, 128], P(('dp', 'fsdp'))
- grad_dtproj_weight: float32 [3072, 96], P(('dp', 'fsdp'))
- grad_dt_bias: float32 [3072], P(('dp', 'fsdp'))
- grad_a_log: float32 [3072, 16], P(('dp', 'fsdp'))
- grad_d_skip: float32 [3072], P(('dp', 'fsdp'))
- grad_out_weight: float32 [3072, 1536], P('fsdp', 'dp')
- out_rms: float32 [], replicated
- grad_rms: float32 [], replicated
Inputs may be any that keep to these rules, and one draw needn't show every extreme that they name: On each device the tokens form either one sequence of 384 tokens (segment 0 throughout) or two to 4 sequences of 96 tokens numbered 0, 1, ... in order, followed by padding marked 4; some device holds one whole sequence and some device has padding in every draw.
All inputs are finite; a program needn't handle non-finite values.
Results may differ from a plain program's by a relative error of at most 0.019.
Values may be sent and summed in bfloat16 or wider, within the bound.
No kernel may reach another device: no remote copies, remote signals or barrier semaphores. Data moves between devices by JAX's collectives and lax.ppermute only.
A program may use at most 320 MiB of HBM per device.

v0:
```python
import math

import jax
import jax.numpy as jnp
from jax import lax
from jax.sharding import PartitionSpec as P

maximal_precision = lax.Precision.HIGHEST


def embed_columns(time_values, column_count, model_width):
    half_width = model_width // 2
    column = jnp.arange(column_count, dtype=jnp.int32)
    lower_half = column < half_width
    freq_index = jnp.where(lower_half, column, column - half_width).astype(jnp.float32)
    frequency = jnp.exp(freq_index * (-math.log(10000.0) / half_width))
    angles = time_values.astype(jnp.float32)[:, None] * frequency[None, :]
    return jax.nn.silu(jnp.where(lower_half[None, :], jnp.cos(angles), jnp.sin(angles)))


def conv_series(values, segment, conv_w, conv_b, direction):
    length = values.shape[0]
    taps = conv_w.shape[1]
    result = conv_b[None, :] + conv_w[:, taps - 1][None, :] * values
    for offset in range(1, taps):
        zero_rows = jnp.zeros((offset, values.shape[1]), values.dtype)
        edge_seg = jnp.full((offset,), -1, jnp.int32)
        if direction > 0:
            moved = jnp.concatenate([zero_rows, values[: length - offset]], axis=0)
            moved_seg = jnp.concatenate([edge_seg, segment[: length - offset]])
        else:
            moved = jnp.concatenate([values[offset:], zero_rows], axis=0)
            moved_seg = jnp.concatenate([segment[offset:], edge_seg])
        matched = (moved_seg == segment).astype(values.dtype)[:, None]
        result = result + conv_w[:, taps - 1 - offset][None, :] * moved * matched
    return result


def linked_block_list(series, step_size, b_rows, c_rows, segment, decay_rows):
    length, inner = series.shape
    states_n = b_rows.shape[1]
    block_len = 32
    blocks = length // block_len
    seg_blocks = segment.reshape(blocks, block_len)
    prior = jnp.concatenate([jnp.full((1,), -1, jnp.int32), seg_blocks[:-1, -1]])
    positions = jnp.arange(block_len, dtype=jnp.int32)
    causal = positions[None, :] <= positions[:, None]

    def one_block(state, slices):
        u_now, d_now, b_now, c_now, s_now, p_now = slices
        exponent = jnp.cumsum(d_now, axis=0)[:, None, :] * decay_rows[None, :, :]
        term_list = jnp.exp(-exponent) * (d_now * u_now)[:, None, :] * b_now[:, :, None]
        joined_chain = (causal & (s_now[None, :] == s_now[:, None])).astype(jnp.float32)
        collected_term_list = jnp.einsum(
            "py,yjl->pjl", joined_chain, term_list, precision=maximal_precision
        )
        carried = (s_now == p_now).astype(jnp.float32)[:, None, None]
        states = jnp.exp(exponent) * (collected_term_list + carried * state[None, :, :])
        outputs = jnp.einsum("tne,tn->te", states, c_now, precision=maximal_precision)
        return (states[-1], outputs)

    _, outputs = lax.scan(
        jax.checkpoint(one_block),
        jnp.zeros((states_n, inner), jnp.float32),
        (
            series.reshape(blocks, block_len, inner),
            step_size.reshape(blocks, block_len, inner),
            b_rows.reshape(blocks, block_len, states_n),
            c_rows.reshape(blocks, block_len, states_n),
            seg_blocks,
            prior,
        ),
    )
    return outputs.reshape(length, inner)


def mixer_local(inner_pair, conv_w, conv_b, x_proj, dt_proj, bias_dt, a_log, d_skip, segment):
    inner = conv_w.shape[0]
    rank_dt = dt_proj.shape[1]
    states_n = a_log.shape[1]
    x_part = inner_pair[:, :inner]
    z_part = inner_pair[:, inner:]
    decay_rows = -jnp.exp(a_log).T
    total = jnp.zeros_like(x_part)
    for direction in (1, -1):
        series = jax.nn.silu(conv_series(x_part, segment, conv_w, conv_b, direction))
        projected = jnp.dot(series, x_proj, precision=maximal_precision)
        step_size = jax.nn.softplus(
            jnp.dot(projected[:, :rank_dt], dt_proj.T, precision=maximal_precision)
            + bias_dt[None, :]
        )
        b_rows = projected[:, rank_dt : rank_dt + states_n]
        c_rows = projected[:, rank_dt + states_n :]
        if direction > 0:
            scanned = linked_block_list(series, step_size, b_rows, c_rows, segment, decay_rows)
        else:
            scanned = linked_block_list(
                series[::-1], step_size[::-1], b_rows[::-1], c_rows[::-1], segment[::-1], decay_rows
            )[::-1]
        total = total + scanned + d_skip[None, :] * series
    return total * jax.nn.silu(z_part)


def per_device(
    tokens,
    segment,
    timestep,
    ada_weight,
    ada_bias,
    in_weight,
    conv_weight,
    convolution_bias,
    xproj_weight,
    dtproj_weight,
    dt_bias,
    a_log,
    d_skip,
    out_weight,
    cotangent,
):
    ada_cols, in_cols, out_cols = (
        lax.all_gather(ada_weight, "dp", axis=1, tiled=True),
        lax.all_gather(in_weight, "dp", axis=1, tiled=True),
        lax.all_gather(out_weight, "dp", axis=1, tiled=True),
    )
    ada_full, in_full, out_full = (
        lax.all_gather(ada_cols, "fsdp", axis=0, tiled=True),
        lax.all_gather(in_cols, "fsdp", axis=0, tiled=True),
        lax.all_gather(out_cols, "fsdp", axis=0, tiled=True),
    )
    (
        ada_bias_full,
        conv_full,
        conv_bias_full,
        xproj_full,
        dtproj_full,
        dt_bias_full,
        a_log_full,
        d_skip_full,
    ) = (
        lax.all_gather(ada_bias, ("dp", "fsdp"), axis=0, tiled=True),
        lax.all_gather(conv_weight, ("dp", "fsdp"), axis=0, tiled=True),
        lax.all_gather(convolution_bias, ("dp", "fsdp"), axis=0, tiled=True),
        lax.all_gather(xproj_weight, ("dp", "fsdp"), axis=0, tiled=True),
        lax.all_gather(dtproj_weight, ("dp", "fsdp"), axis=0, tiled=True),
        lax.all_gather(dt_bias, ("dp", "fsdp"), axis=0, tiled=True),
        lax.all_gather(a_log, ("dp", "fsdp"), axis=0, tiled=True),
        lax.all_gather(d_skip, ("dp", "fsdp"), axis=0, tiled=True),
    )
    slots = timestep.shape[0]
    model_width = tokens.shape[1]
    contract_rows = (((0,), (0,)), ((), ()))
    contract_cols = (((1,), (1,)), ((), ()))
    condition = embed_columns(timestep, model_width, model_width).astype(jnp.bfloat16)
    modulation = (
        jnp.dot(condition, ada_full, preferred_element_type=jnp.float32)
        + ada_bias_full.astype(jnp.float32)[None, :]
    )
    picker = (segment[:, None] == jnp.arange(slots, dtype=jnp.int32)[None, :]).astype(jnp.float32)
    per_token = jnp.dot(picker, modulation, precision=maximal_precision)
    shift_mod = per_token[:, :model_width]
    scale_mod = per_token[:, model_width : 2 * model_width]
    gate_mod = per_token[:, 2 * model_width :]
    centered = tokens - jnp.mean(tokens, axis=1, keepdims=True)
    inv_std = lax.rsqrt(jnp.mean(centered * centered, axis=1, keepdims=True) + 1e-06)
    normed = centered * inv_std
    hidden = (normed * (1.0 + scale_mod) + shift_mod).astype(jnp.bfloat16)
    inner_pair = jnp.dot(hidden, in_full, preferred_element_type=jnp.float32)

    def mixer_params(pair_in, conv_w, conv_b, x_proj, dt_proj, bias_dt, a_log_in, d_skip_in):
        return mixer_local(
            pair_in, conv_w, conv_b, x_proj, dt_proj, bias_dt, a_log_in, d_skip_in, segment
        )

    mixer_out, mixer_pull = jax.vjp(
        mixer_params,
        inner_pair,
        conv_full.astype(jnp.float32),
        conv_bias_full.astype(jnp.float32),
        xproj_full.astype(jnp.float32),
        dtproj_full.astype(jnp.float32),
        dt_bias_full.astype(jnp.float32),
        a_log_full.astype(jnp.float32),
        d_skip_full.astype(jnp.float32),
    )
    mixer_low = mixer_out.astype(jnp.bfloat16)
    branch = jnp.dot(mixer_low, out_full, preferred_element_type=jnp.float32)
    layer_out = tokens + gate_mod * branch
    in_back_cols, out_back_cols = (
        lax.all_gather(in_weight, "dp", axis=1, tiled=True),
        lax.all_gather(out_weight, "dp", axis=1, tiled=True),
    )
    in_back, out_back = (
        lax.all_gather(in_back_cols, "fsdp", axis=0, tiled=True),
        lax.all_gather(out_back_cols, "fsdp", axis=0, tiled=True),
    )
    branch_grad = (cotangent * gate_mod).astype(jnp.bfloat16)
    gate_grad = cotangent * branch
    grad_out_w = lax.dot_general(
        mixer_low, branch_grad, contract_rows, preferred_element_type=jnp.float32
    )
    mixer_grad = lax.dot_general(
        branch_grad, out_back, contract_cols, preferred_element_type=jnp.float32
    )
    (
        pair_grad,
        conv_w_grad,
        conv_b_grad,
        xproj_grad,
        dtproj_grad,
        bias_dt_grad,
        a_log_grad,
        d_skip_grad,
    ) = mixer_pull(mixer_grad)
    pair_low = pair_grad.astype(jnp.bfloat16)
    grad_in_w = lax.dot_general(hidden, pair_low, contract_rows, preferred_element_type=jnp.float32)
    hidden_grad = lax.dot_general(
        pair_low, in_back, contract_cols, preferred_element_type=jnp.float32
    )
    normed_grad = hidden_grad * (1.0 + scale_mod)
    grad_tokens = cotangent + inv_std * (
        normed_grad
        - jnp.mean(normed_grad, axis=1, keepdims=True)
        - normed * jnp.mean(normed_grad * normed, axis=1, keepdims=True)
    )
    token_mod_grad = jnp.concatenate([hidden_grad, hidden_grad * normed, gate_grad], axis=1)
    mod_low = lax.dot_general(
        picker, token_mod_grad, contract_rows, precision=maximal_precision
    ).astype(jnp.bfloat16)
    ada_w_term = lax.dot_general(
        condition, mod_low, contract_rows, preferred_element_type=jnp.float32
    )
    ada_b_term = jnp.sum(mod_low.astype(jnp.float32), axis=0)
    row_ada, row_in, row_out = (
        lax.psum_scatter(
            ada_w_term.astype(jnp.bfloat16), "fsdp", scatter_dimension=0, tiled=True
        ).astype(jnp.float32),
        lax.psum_scatter(
            grad_in_w.astype(jnp.bfloat16), "fsdp", scatter_dimension=0, tiled=True
        ).astype(jnp.float32),
        lax.psum_scatter(
            grad_out_w.astype(jnp.bfloat16), "fsdp", scatter_dimension=0, tiled=True
        ).astype(jnp.float32),
    )
    grad_ada_w, grad_in_shard, grad_out_shard = (
        lax.psum_scatter(
            row_ada.astype(jnp.bfloat16), "dp", scatter_dimension=1, tiled=True
        ).astype(jnp.float32),
        lax.psum_scatter(row_in.astype(jnp.bfloat16), "dp", scatter_dimension=1, tiled=True).astype(
            jnp.float32
        ),
        lax.psum_scatter(
            row_out.astype(jnp.bfloat16), "dp", scatter_dimension=1, tiled=True
        ).astype(jnp.float32),
    )
    (
        grad_ada_b,
        grad_conv_w,
        grad_conv_b,
        grad_xproj,
        grad_dtproj,
        grad_bias_dt,
        grad_a_log_shard,
        grad_d_skip_shard,
    ) = (
        lax.psum_scatter(ada_b_term, ("dp", "fsdp"), scatter_dimension=0, tiled=True),
        lax.psum_scatter(conv_w_grad, ("dp", "fsdp"), scatter_dimension=0, tiled=True),
        lax.psum_scatter(conv_b_grad, ("dp", "fsdp"), scatter_dimension=0, tiled=True),
        lax.psum_scatter(xproj_grad, ("dp", "fsdp"), scatter_dimension=0, tiled=True),
        lax.psum_scatter(dtproj_grad, ("dp", "fsdp"), scatter_dimension=0, tiled=True),
        lax.psum_scatter(bias_dt_grad, ("dp", "fsdp"), scatter_dimension=0, tiled=True),
        lax.psum_scatter(a_log_grad, ("dp", "fsdp"), scatter_dimension=0, tiled=True),
        lax.psum_scatter(d_skip_grad, ("dp", "fsdp"), scatter_dimension=0, tiled=True),
    )
    valid = (segment < slots).astype(jnp.float32)[:, None]
    out_sq, grad_sq, counted = lax.psum(
        (
            jnp.sum(layer_out * layer_out * valid),
            jnp.sum(grad_tokens * grad_tokens * valid),
            jnp.sum(valid) * model_width,
        ),
        ("dp", "fsdp"),
    )
    out_rms = jnp.sqrt(out_sq / counted)
    grad_rms = jnp.sqrt(grad_sq / counted)
    return (
        layer_out,
        grad_tokens,
        grad_ada_w,
        grad_ada_b,
        grad_in_shard,
        grad_conv_w,
        grad_conv_b,
        grad_xproj,
        grad_dtproj,
        grad_bias_dt,
        grad_a_log_shard,
        grad_d_skip_shard,
        grad_out_shard,
        out_rms,
        grad_rms,
    )


def solution(mesh):
    return jax.shard_map(
        per_device,
        mesh=mesh,
        in_specs=(
            P(("dp", "fsdp"), None),
            P(("dp", "fsdp")),
            P(("dp", "fsdp")),
            P("fsdp", "dp"),
            P(("dp", "fsdp")),
            P("fsdp", "dp"),
            P(("dp", "fsdp"), None),
            P(("dp", "fsdp")),
            P(("dp", "fsdp"), None),
            P(("dp", "fsdp"), None),
            P(("dp", "fsdp")),
            P(("dp", "fsdp"), None),
            P(("dp", "fsdp")),
            P("fsdp", "dp"),
            P(("dp", "fsdp"), None),
        ),
        out_specs=(
            P(("dp", "fsdp"), None),
            P(("dp", "fsdp"), None),
            P("fsdp", "dp"),
            P(("dp", "fsdp")),
            P("fsdp", "dp"),
            P(("dp", "fsdp"), None),
            P(("dp", "fsdp")),
            P(("dp", "fsdp"), None),
            P(("dp", "fsdp"), None),
            P(("dp", "fsdp")),
            P(("dp", "fsdp"), None),
            P(("dp", "fsdp")),
            P("fsdp", "dp"),
            P(),
            P(),
        ),
        check_vma=False,
    )
```

profile of v0, /device:TPU:0, one launch (start us, length us, event | category | flops | bytes accessed | tf_op | source)
XLA Modules:
  0.0 3546.5 jit_solution(10868932940373456126)
XLA Ops:
  45.4 39.3 %all-gather.13.cloned.1.call-done = bf16[192,6144]{1,0:T(8,128)(2,1)} async-done(((bf16[192,1536]{1,0:T(8,128)(2,1)}), bf16[192,6144]{1,0:T(8,128)(2,1)}) %all-gather.13.cloned.1.call-update) | async-done | bytes 2359312 | tf_op jit(solution)/shard_map/all_gather | solution.py:123
  115.4 44.4 %all-reduce.43 = (bf16[3072]{0:T(1024)(128)(2,1)S(1)}, bf16[4608]{0:T(1024)(128)(2,1)S(1)}, bf16[3072]{0:T(1024)(128)(2,1)S(1)}, bf16[3072]{0:T(1024)(128)(2,1)S(1)}) all-reduce(bf16[3072]{0:T(1024)(128)(2,1)S(1)} %dynamic-update-slice.2, bf16[4608]{0:T(1024)(128)(2,1)S(1)} %dynamic-update-slice, ...), channel_id=1, replica_groups=mesh['dp'=4,'fsdp'=8] {'dp','fsdp'}, use_global_device_ids=true, to_apply=%add.36 | all-reduce | flops 13824 | bytes 55296
  160.9 41.0 %all-gather = bf16[32,96,4]{1,2,0:T(4,128)(2,1)S(1)} all-gather(bf16[1,96,4]{1,2,0:T(4,128)(2,1)S(1)} %bitcast.373), channel_id=1, replica_groups=mesh['dp'=4,'fsdp'=8] {'dp','fsdp'}, dimensions={0}, use_global_device_ids=true | all-gather | bytes 25344 | tf_op jit(solution)/shard_map/all_gather | solution.py:142
  203.9 42.4 %all-gather.1 = bf16[32,96,16]{1,2,0:T(8,128)(2,1)S(1)} all-gather(bf16[1,96,16]{1,2,0:T(8,128)(2,1)S(1)} %bitcast.372), channel_id=1, replica_groups=mesh['dp'=4,'fsdp'=8] {'dp','fsdp'}, dimensions={0}, use_global_device_ids=true | all-gather | bytes 101376 | tf_op jit(solution)/shard_map/all_gather | solution.py:147
  251.1 58.6 %all_gather.54 = bf16[3072,96]{1,0:T(8,128)(2,1)} all-gather(bf16[96,96]{1,0:T(8,128)(2,1)S(1)} %copy-done.55), channel_id=1, replica_groups=mesh['dp'=4,'fsdp'=8] {'dp','fsdp'}, dimensions={0}, use_global_device_ids=true | all-gather | bytes 608256 | tf_op jit(solution)/shard_map/all_gather | solution.py:145
  309.7 54.3 %all_gather.53 = bf16[3072,128]{1,0:T(8,128)(2,1)S(1)} all-gather(bf16[96,128]{1,0:T(8,128)(2,1)} %param.32), channel_id=1, replica_groups=mesh['dp'=4,'fsdp'=8] {'dp','fsdp'}, dimensions={0}, use_global_device_ids=true | all-gather | bytes 811008 | tf_op jit(solution)/shard_map/all_gather | solution.py:144
  381.9 48.0 %all-gather.15.cloned.1.call-done = bf16[1536,6144]{1,0:T(8,128)(2,1)} async-done(((bf16[192,6144]{1,0:T(8,128)(2,1)}), bf16[1536,6144]{1,0:T(8,128)(2,1)}) %all-gather.15.cloned.1.call-update) | async-done | bytes 18874384 | tf_op jit(solution)/shard_map/all_gather | solution.py:128
  456.6 64.0 %all-gather.19.cloned.1.call-done = bf16[3072,1536]{1,0:T(8,128)(2,1)} async-done(((bf16[384,1536]{1,0:T(8,128)(2,1)}), bf16[3072,1536]{1,0:T(8,128)(2,1)}) %all-gather.19.cloned.1.call-update) | async-done | bytes 9437200 | tf_op jit(solution)/shard_map/all_gather | solution.py:129
  552.3 36.8 %rev.35 = f32[384,3072]{1,0:T(8,128)} reverse(f32[384,3072]{1,0:T(8,128)} %get-tuple-element.1465), dimensions={0} | reverse | bytes 9437184 | tf_op jit(solution)/shard_map/jvp()/rev | solution.py:98
  656.6 296.5 %while.81 = (s32[]{:T(128)}, f32[16,3072]{1,0:T(8,128)S(1)}, f32[12,32,3072]{2,1,0:T(8,128)}, f32[12,16,3072]{2,1,0:T(8,128)}, f32[12,32,3072]{2,1,0:T(8,128)}, ...) while((s32[]{:T(128)}, f32[16,3072]{1,0:T(8,128)S(1)}, ...), condition=%wide.region_7.9_spmd.clone, body=%wide.region_5.8_spmd.clone.sunk | while | flops 638585920 | bytes 44057424 | solution.py:62
  995.4 520.1 %while.82 = (s32[]{:T(128)}, f32[16,3072]{1,0:T(8,128)S(1)}, f32[16,3072]{1,0:T(8,128)S(1)}, f32[12,32,3072]{2,1,0:T(8,128)}, f32[12,32,3072]{2,1,0:T(8,128)}, /...) while((s32[]{:T(128)}, f32[16,3072]{1,0:T(8,128)S(1)}, ...), condition=%wide.region_16.18_spmd.clone, body=%wide.region_8.17_spmd.clone.sunk | while | flops 1294471680 | bytes 59021576 | solution.py:62
  1515.5 36.8 %rev.43 = f32[384,3072]{1,0:T(8,128)} reverse(f32[384,3072]{1,0:T(8,128)} %bitcast.339), dimensions={0} | reverse | bytes 9437184 | tf_op jit(solution)/shard_map/transpose(jvp())/rev | solution.py:98
  1567.6 36.7 %rev.40 = f32[384,3072]{1,0:T(8,128)} reverse(f32[384,3072]{1,0:T(8,128)} %bitcast.338), dimensions={0} | reverse | bytes 9437184 | tf_op jit(solution)/shard_map/transpose(jvp())/rev | solution.py:98
  1609.6 297.9 %while.80 = (s32[]{:T(128)}, f32[16,3072]{1,0:T(8,128)S(1)}, f32[12,32,3072]{2,1,0:T(8,128)}, f32[12,16,3072]{2,1,0:T(8,128)}, f32[12,32,3072]{2,1,0:T(8,128)}, ...) while((s32[]{:T(128)}, f32[16,3072]{1,0:T(8,128)S(1)}, ...), condition=%wide.region_4.6_spmd.clone, body=%wide.region_2.5_spmd.clone.sunk | while | flops 638585920 | bytes 44057424 | solution.py:62
  1913.1 520.0 %while.83 = (s32[]{:T(128)}, f32[16,3072]{1,0:T(8,128)S(1)}, f32[16,3072]{1,0:T(8,128)S(1)}, f32[12,32,3072]{2,1,0:T(8,128)}, f32[12,32,3072]{2,1,0:T(8,128)}, /...) while((s32[]{:T(128)}, f32[16,3072]{1,0:T(8,128)S(1)}, ...), condition=%wide.region_25.27_spmd.clone, body=%wide.region_17.26_spmd.clone.sunk | while | flops 1294471680 | bytes 59021576 | solution.py:62
  2445.0 36.7 %rev.38 = f32[384,3072]{1,0:T(8,128)} reverse(f32[384,3072]{1,0:T(8,128)} %bitcast.340), dimensions={0} | reverse | bytes 9437184 | tf_op jit(solution)/shard_map/jvp()/rev | solution.py:97
  2688.7 142.3 %reduce-scatter.19.cloned.1.call-done = bf16[192,4608]{1,0:T(8,128)(2,1)} async-done(((bf16[1536,4608]{1,0:T(8,128)(2,1)}), bf16[192,4608]{1,0:T(8,128)(2,1)}) %reduce-scatter.19.cloned.1.call-update) | async-done | bytes 1769488 | tf_op jit(solution)/shard_map/reduce_scatter | solution.py:235
  2835.1 184.6 %reduce-scatter.21.cloned.1.call-done = bf16[192,6144]{1,0:T(8,128)(2,1)} async-done(((bf16[1536,6144]{1,0:T(8,128)(2,1)}), bf16[192,6144]{1,0:T(8,128)(2,1)}) %reduce-scatter.21.cloned.1.call-update) | async-done | bytes 2359312 | tf_op jit(solution)/shard_map/reduce_scatter | solution.py:238
  3062.0 39.3 %all-reduce.42 = (f32[4608]{0:T(1024)S(1)}, f32[3072]{0:T(1024)S(1)}, f32[3072]{0:T(1024)S(1)}, f32[3072]{0:T(1024)S(1)}, f32[]{:T(128)}, /*index=5*/f32[]{:T(128)}, f32[]{:T(128)}) all-reduce(f32[4608]{0:T(1024)S(1)} %get-tuple-element.1547, f32[3072]{0:T(1024)S(1)} %add_any.195, ...), channel_id=4, replica_groups=mesh['dp'=4,'fsdp'=8] {'dp','fsdp'}, use_global_device_ids=true, to_apply=%region_31.33.clone | all-reduce | flops 13827 | bytes 110616
  3121.6 99.8 %reduce-scatter.35.cloned.1.call-done = f32[96,16]{1,0:T(8,128)} async-done(((f32[3072,16]{1,0:T(8,128)}), f32[96,16]{1,0:T(8,128)}) %reduce-scatter.35.cloned.1.call-update) | async-done | bytes 6160
  3254.4 38.4 %reduce-scatter.31.cloned.1.call-done = bf16[1152,192]{1,0:T(8,128)(2,1)} async-done(((bf16[4608,192]{1,0:T(8,128)(2,1)}), bf16[1152,192]{1,0:T(8,128)(2,1)}) %reduce-scatter.31.cloned.1.call-update) | async-done | bytes 442384
  3295.2 38.0 %reduce-scatter.23.cloned.1.call-done = bf16[192,1536]{1,0:T(8,128)(2,1)} async-done(((bf16[192,6144]{1,0:T(8,128)(2,1)}), bf16[192,1536]{1,0:T(8,128)(2,1)}) %reduce-scatter.23.cloned.1.call-update) | async-done | bytes 589840 | tf_op jit(solution)/shard_map/reduce_scatter | solution.py:249
  3335.4 100.4 %reduce-scatter.27.cloned.1.call-done = f32[96,96]{1,0:T(8,128)} async-done(((f32[3072,96]{1,0:T(8,128)}), f32[96,96]{1,0:T(8,128)}) %reduce-scatter.27.cloned.1.call-update) | async-done | bytes 36880 | tf_op jit(solution)/shard_map/reduce_scatter | solution.py:270
  3435.9 101.7 %reduce-scatter.25.cloned.1.call-done = f32[96,128]{1,0:T(8,128)} async-done(((f32[3072,128]{1,0:T(8,128)}), f32[96,128]{1,0:T(8,128)}) %reduce-scatter.25.cloned.1.call-update) | async-done | bytes 49168 | tf_op jit(solution)/shard_map/reduce_scatter | solution.py:269
  (1247 shorter events, 2236.9 us)
Async XLA Ops:
  7.2 153.2 %copy-start.87 = (s32[4]{0:T(128)S(1)}, s32[4]{0:T(128)}, u32[]{:S(2)}) copy-start(s32[4]{0:T(128)} %param.26) | copy-start | bytes 52
  7.2 153.7 %copy-start.80 = (bf16[96,4]{0,1:T(4,128)(2,1)S(1)}, bf16[96,4]{0,1:T(4,128)(2,1)}, u32[]{:S(2)}) copy-start(bf16[96,4]{0,1:T(4,128)(2,1)} %param.30) | copy-start | bytes 2308
  7.3 196.6 %copy-start.78 = (bf16[96,16]{0,1:T(8,128)(2,1)S(1)}, bf16[96,16]{0,1:T(8,128)(2,1)}, u32[]{:S(2)}) copy-start(bf16[96,16]{0,1:T(8,128)(2,1)} %param.35) | copy-start | bytes 9220
  7.3 240.7 %copy-start.7 = (f32[384,1536]{1,0:T(8,128)S(1)}, f32[384,1536]{1,0:T(8,128)}, u32[]{:S(2)}) copy-start(f32[384,1536]{1,0:T(8,128)} %param.24) | copy-start | bytes 7077892
  7.3 38.0 %all-gather.9.cloned.1.call-start = ((), (), s32[]{:S(2)}) async-start(), calls=%async_computation.10 | async-start | bytes 2211840 | tf_op jit(solution)/shard_map/all_gather | solution.py:122
  8.0 76.6 %all-gather.13.cloned.1.call-start = ((), (), s32[]{:S(2)}) async-start(), calls=%async_computation.12 | async-start | bytes 2949120 | tf_op jit(solution)/shard_map/all_gather | solution.py:123
  8.8 105.3 %all-gather.17.cloned.1.call-start = ((), (), s32[]{:S(2)}) async-start(), calls=%async_computation.14 | async-start | bytes 1474560 | tf_op jit(solution)/shard_map/all_gather | solution.py:124
  9.5 356.9 %all-gather.11.cloned.1.call-start = ((), (), s32[]{:S(2)}) async-start(), calls=%async_computation.11 | async-start | bytes 15925248 | tf_op jit(solution)/shard_map/all_gather | solution.py:127
  45.3 384.6 %all-gather.15.cloned.1.call-start = ((), (), s32[]{:S(2)}) async-start(), calls=%async_computation.13 | async-start | bytes 21233664 | tf_op jit(solution)/shard_map/all_gather | solution.py:128
  84.6 166.4 %copy-start.55 = (bf16[96,96]{1,0:T(8,128)(2,1)S(1)}, bf16[96,96]{1,0:T(8,128)(2,1)}, u32[]{:S(2)}) copy-start(bf16[96,96]{1,0:T(8,128)(2,1)} %param.33) | copy-start | bytes 55300
  84.7 435.9 %all-gather.19.cloned.1.call-start = ((), (), s32[]{:S(2)}) async-start(), calls=%async_computation.15 | async-start | bytes 10616832 | tf_op jit(solution)/shard_map/all_gather | solution.py:129
  114.1 2572.1 %reduce-scatter.29.cloned.1.call-start = ((), (), s32[]{:S(2)}) async-start(), calls=%async_computation.21 | async-start | bytes 10616832 | tf_op jit(solution)/shard_map/reduce_scatter | solution.py:241
  364.0 230.2 %copy-start.9 = (bf16[3072,128]{1,0:T(8,128)(2,1)}, bf16[3072,128]{1,0:T(8,128)(2,1)S(1)}, u32[]{:S(2)}) copy-start(bf16[3072,128]{1,0:T(8,128)(2,1)S(1)} %all_gather.53) | copy-start | bytes 2359300
  2588.1 242.9 %reduce-scatter.19.cloned.1.call-start = ((), (), s32[]{:S(2)}) async-start(), calls=%async_computation.16 | async-start | bytes 15925248 | tf_op jit(solution)/shard_map/reduce_scatter | solution.py:235
  2629.1 390.6 %reduce-scatter.21.cloned.1.call-start = ((), (), s32[]{:S(2)}) async-start(), calls=%async_computation.17 | async-start | bytes 21233664 | tf_op jit(solution)/shard_map/reduce_scatter | solution.py:238
  2647.7 472.5 %reduce-scatter.33.cloned.1.call-start = ((), (), s32[]{:S(2)}) async-start(), calls=%async_computation.23 | async-start | bytes 1622016
  2649.6 571.9 %reduce-scatter.35.cloned.1.call-start = ((), (), s32[]{:S(2)}) async-start(), calls=%async_computation.24 | async-start | bytes 1622016
  2651.3 601.1 %reduce-scatter.37.cloned.1.call-start = ((), (), s32[]{:S(2)}) async-start(), calls=%async_computation.25 | async-start | bytes 1474560
  2688.6 331.1 %copy-start.26 = (f32[384,128]{0,1:T(8,128)S(1)}, f32[384,128]{0,1:T(8,128)}, u32[]{:S(2)}) copy-start(f32[384,128]{0,1:T(8,128)} %copy-done.25) | copy-start | bytes 589828
  2688.6 604.3 %reduce-scatter.31.cloned.1.call-start = ((), (), s32[]{:S(2)}) async-start(), calls=%async_computation.22 | async-start | bytes 2949120
  2835.0 194.5 %copy-start.28 = (f32[384,128]{0,1:T(8,128)S(1)}, f32[384,128]{0,1:T(8,128)}, u32[]{:S(2)}) copy-start(f32[384,128]{0,1:T(8,128)} %copy-done.27) | copy-start | bytes 589828
  2835.0 498.2 %reduce-scatter.23.cloned.1.call-start = ((), (), s32[]{:S(2)}) async-start(), calls=%async_computation.18 | async-start | bytes 2949120 | tf_op jit(solution)/shard_map/reduce_scatter | solution.py:249
  3019.7 416.2 %reduce-scatter.27.cloned.1.call-start = ((), (), s32[]{:S(2)}) async-start(), calls=%async_computation.20 | async-start | bytes 1622016 | tf_op jit(solution)/shard_map/reduce_scatter | solution.py:270
  3040.1 497.5 %reduce-scatter.25.cloned.1.call-start = ((), (), s32[]{:S(2)}) async-start(), calls=%async_computation.19 | async-start | bytes 1622016 | tf_op jit(solution)/shard_map/reduce_scatter | solution.py:269
  (110 other events, 2877.7 us)
Sparse Core Ops, SparseCore 0:
  10.0 35.2 all-gather.8
  47.1 37.4 all-gather.12
  86.5 27.5 all-gather.16
  115.6 131.9 all-gather.10
  249.1 180.7 all-gather.14
  431.4 89.1 all-gather.18
  2588.2 97.9 reduce-scatter.28
  2688.5 142.4 reduce-scatter.18
  2833.3 186.3 reduce-scatter.20
  3024.8 95.3 reduce-scatter.32
  3125.4 95.9 reduce-scatter.34
  3224.8 27.5 reduce-scatter.36
  3255.5 37.3 reduce-scatter.30
  3295.8 37.3 reduce-scatter.22
  3338.9 96.9 reduce-scatter.26
  3441.5 95.9 reduce-scatter.24
where the time goes:
time: 3580 us; the launch traced here: 3550 us
  matrix products  1270 us (35%)
  waiting for transfers between devices  1000 us (28%)
  local copies, waits for them, and re-layouts  586 us (16%)
  other arithmetic  386 us (11%)
  blocking collectives  280 us (8%)
    dot_general x48, matrix products, one_block(): jnp.einsum('tne,tn->te', states, c_now, precision=maximal_precision)  557 us
    dot_general x72, matrix products, one_block(): jnp.einsum('py,yjl->pjl', joined_chain, term_list, precision=maximal_prec...  479 us
    reduce_scatter x1, waiting for transfers between devices, per_device(): lax.psum_scatter(grad_in_w.astype(jnp.bfloat16), 'fsdp', scatter_dimensio...  185 us
    unnamed x20, waiting for transfers between devices  184 us
    reduce_scatter x1, waiting for transfers between devices, per_device(): lax.psum_scatter(ada_w_term.astype(jnp.bfloat16), 'fsdp', scatter_dimensi...  142 us
    reduce_sum x24, other arithmetic, one_block(): exponent = jnp.cumsum(d_now, axis=0)[:, None, :] * decay_rows[None, :, :]  141 us
    squeeze x168, local copies, waits for them, and re-layouts, linked_block_list(): lax.scan(jax.checkpoint(one_block), jnp.zeros((states_n, inner), jnp.floa...  128 us
    reduce_scatter x1, waiting for transfers between devices, per_device(): lax.psum_scatter(xproj_grad, ('dp', 'fsdp'), scatter_dimension=0, tiled=T...  102 us
  transfers between devices with their start and end apart: 16, of which 15 were waited for; matrix products, arithmetic and copies ran while one was open for 5% of the time, Pallas kernels for 0%

commit v1 on v0

v1 whole, which is shorter than its diff:
```python
import math

import jax
import jax.numpy as jnp
from jax import lax
from jax.experimental import pallas as pl
from jax.experimental.pallas import tpu as pltpu
from jax.sharding import PartitionSpec as P

F32 = jnp.float32
BF16 = jnp.bfloat16
LN2 = math.log(2.0)
BOTH = ("dp", "fsdp")
high = lax.Precision.HIGHEST
GROUP = 4


def embed_columns(time_values, column, model_width):
    half_width = model_width // 2
    lower_half = column < half_width
    freq_index = jnp.where(lower_half, column, column - half_width).astype(F32)
    frequency = jnp.exp(freq_index * (-math.log(10000.0) / half_width))
    angles = time_values.astype(F32)[:, None] * frequency[None, :]
    return jax.nn.silu(jnp.where(lower_half[None, :], jnp.cos(angles), jnp.sin(angles)))


def to_rows(v):
    t, e = v.shape
    return v.reshape(t // 8, 8, e // 128, 128).transpose(0, 2, 1, 3).reshape(t * e // 128, 128)


def from_rows(r, t, e):
    return r.reshape(t // 8, e // 128, 8, 128).transpose(0, 2, 1, 3).reshape(t, e)


def fill_columns(proj_ref, bc_ref, tokens, first, group, states):
    def fill(i, _):
        p = proj_ref[pl.ds(pl.multiple_of(i * 8, 8), 8), :]
        for s in range(2):
            for n in range(GROUP):
                col = first + s * states + group * GROUP + n
                row = pl.multiple_of((s * GROUP + n) * tokens + i * 8, 8)
                bc_ref[pl.ds(row, 8), :] = jnp.broadcast_to(p[:, col : col + 1], (8, 128))
        return 0

    lax.fori_loop(0, tokens // 8, fill, 0)


def scan_forward(keep, proj, step, series, decay2, *, rev, tokens, inner, states, rank):
    blocks, tiles, octets = inner // 1024, inner // 128, tokens // 8

    def body(keep_ref, proj_ref, d_ref, u_ref, a_ref, y_ref, bc_ref):
        for ng in range(states // GROUP):
            fill_columns(proj_ref, bc_ref, tokens, rank, ng, states)
            a = [
                [a_ref[pl.ds((ng * GROUP + n) * tiles + c * 8, 8), :] for c in range(blocks)]
                for n in range(GROUP)
            ]

            def octet(i, hs):
                g = (octets - 1 - i) if rev else i
                keep_now = keep_ref[i]
                hs = [h * keep_now for h in hs]
                base = pl.multiple_of(g * (tiles * 8), 8)
                for j in range(8):
                    tt = 7 - j if rev else j
                    t = g * 8 + tt
                    for c in range(blocks):
                        sl = pl.ds(base + c * 64 + tt, 8, stride=8)
                        d = d_ref[sl, :]
                        du = d * u_ref[sl, :]
                        acc = None
                        for n in range(GROUP):
                            b = bc_ref[pl.ds(n * tokens + t, 1), :]
                            cc = bc_ref[pl.ds((GROUP + n) * tokens + t, 1), :]
                            k = n * blocks + c
                            hs[k] = jnp.exp2(d * a[n][c]) * hs[k] + du * b
                            acc = hs[k] * cc if acc is None else acc + hs[k] * cc
                        if ng == 0:
                            y_ref[sl, :] = acc
                        else:
                            y_ref[sl, :] = y_ref[sl, :] + acc
                return hs

            lax.fori_loop(0, octets, octet, [jnp.zeros((8, 128), F32)] * (GROUP * blocks))

    vmem = pl.BlockSpec(memory_space=pltpu.VMEM)
    return pl.pallas_call(
        body,
        out_shape=jax.ShapeDtypeStruct((tokens * tiles, 128), F32),
        in_specs=[pl.BlockSpec(memory_space=pltpu.SMEM)] + [vmem] * 4,
        out_specs=vmem,
        scratch_shapes=[pltpu.VMEM((2 * GROUP * tokens, 128), F32)],
        compiler_params=pltpu.CompilerParams(vmem_limit_bytes=56 << 20),
        cost_estimate=pl.CostEstimate(
            flops=tokens * inner * states * 7,
            bytes_accessed=3 * tokens * inner * 4,
            transcendentals=tokens * inner * states,
        ),
        name="scan_forward",
    )(keep, proj, step, series, decay2)


def scan_backward(keep, proj, step, series, grad, decay2, *, rev, tokens, inner, states, rank):
    blocks, tiles, octets = inner // 1024, inner // 128, tokens // 8
    slots = GROUP * blocks

    def body(
        keep_ref, proj_ref, d_ref, u_ref, g_ref, a_ref, ddu_ref, dd_ref, r_ref, da_ref, bc_ref, h_ref, q_ref
    ):
        zero = jnp.zeros((8, 128), F32)
        for ng in range(states // GROUP):
            fill_columns(proj_ref, bc_ref, tokens, rank, ng, states)
            a = [
                [a_ref[pl.ds((ng * GROUP + n) * tiles + c * 8, 8), :] for c in range(blocks)]
                for n in range(GROUP)
            ]
            for k in range(slots):
                h_ref[pl.ds(k * 8, 8), :] = zero

            def ahead(i, hs):
                g = (octets - 1 - i) if rev else i
                keep_now = keep_ref[i]
                hs = [h * keep_now for h in hs]
                base = pl.multiple_of(g * (tiles * 8), 8)
                for j in range(8):
                    tt = 7 - j if rev else j
                    t = g * 8 + tt
                    hb = pl.multiple_of((i * 8 + j + 1) * (slots * 8), 8)
                    for c in range(blocks):
                        sl = pl.ds(base + c * 64 + tt, 8, stride=8)
                        d = d_ref[sl, :]
                        du = d * u_ref[sl, :]
                        for n in range(GROUP):
                            b = bc_ref[pl.ds(n * tokens + t, 1), :]
                            k = n * blocks + c
                            hs[k] = jnp.exp2(d * a[n][c]) * hs[k] + du * b
                            h_ref[pl.ds(hb + k * 8, 8), :] = hs[k]
                return hs

            lax.fori_loop(0, octets, ahead, [zero] * slots)

            def back(ii, carry):
                gs, das = [list(v) for v in carry]
                i = octets - 1 - ii
                g = (octets - 1 - i) if rev else i
                keep_now = keep_ref[i]
                base = pl.multiple_of(g * (tiles * 8), 8)
                for jj in range(8):
                    j = 7 - jj
                    tt = 7 - j if rev else j
                    t = g * 8 + tt
                    hb = pl.multiple_of((i * 8 + j) * (slots * 8), 8)
                    pb, pc = [None] * GROUP, [None] * GROUP
                    for c in range(blocks):
                        sl = pl.ds(base + c * 64 + tt, 8, stride=8)
                        d = d_ref[sl, :]
                        du = d * u_ref[sl, :]
                        gy = g_ref[sl, :]
                        ddu = dd = None
                        for n in range(GROUP):
                            b = bc_ref[pl.ds(n * tokens + t, 1), :]
                            cc = bc_ref[pl.ds((GROUP + n) * tokens + t, 1), :]
                            k = n * blocks + c
                            before = h_ref[pl.ds(hb + k * 8, 8), :]
                            after = h_ref[pl.ds(hb + (slots + k) * 8, 8), :]
                            adj = gs[k] + cc * gy
                            x = after * gy
                            pc[n] = x if c == 0 else pc[n] + x
                            x = adj * du
                            pb[n] = x if c == 0 else pb[n] + x
                            x = adj * b
                            ddu = x if n == 0 else ddu + x
                            moved = adj * jnp.exp2(d * a[n][c])
                            if j == 0:
                                moved = moved * keep_now
                            gs[k] = moved
                            m = moved * before
                            x = m * a[n][c]
                            dd = x if n == 0 else dd + x
                            das[k] = das[k] + m * d
                        if ng == 0:
                            ddu_ref[sl, :] = ddu
                            dd_ref[sl, :] = dd
                        else:
                            ddu_ref[sl, :] = ddu_ref[sl, :] + ddu
                            dd_ref[sl, :] = dd_ref[sl, :] + dd
                    for n in range(GROUP):
                        q_ref[pl.ds(j * 64 + n * 8, 8), :] = pb[n]
                        q_ref[pl.ds(j * 64 + (GROUP + n) * 8, 8), :] = pc[n]
                for j in range(8):
                    tt = 7 - j if rev else j
                    t = g * 8 + tt
                    s = None
                    for q in range(8):
                        x = q_ref[pl.ds(j * 64 + q, 8, stride=8), :]
                        s = x if s is None else s + x
                    r_ref[pl.ds(pl.multiple_of((ng * tokens + t) * 8, 8), 8), :] = s
                return gs, das

            _, das = lax.fori_loop(0, octets, back, ([zero] * slots, [zero] * slots))
            for n in range(GROUP):
                for c in range(blocks):
                    da_ref[pl.ds((ng * GROUP + n) * tiles + c * 8, 8), :] = das[n * blocks + c]

    vmem = pl.BlockSpec(memory_space=pltpu.VMEM)
    rows = tokens * tiles
    return pl.pallas_call(
        body,
        out_shape=(
            jax.ShapeDtypeStruct((rows, 128), F32),
            jax.ShapeDtypeStruct((rows, 128), F32),
            jax.ShapeDtypeStruct((states // GROUP * tokens * 8, 128), F32),
            jax.ShapeDtypeStruct((states * tiles, 128), F32),
        ),
        in_specs=[pl.BlockSpec(memory_space=pltpu.SMEM)] + [vmem] * 5,
        out_specs=(vmem,) * 4,
        scratch_shapes=[
            pltpu.VMEM((2 * GROUP * tokens, 128), F32),
            pltpu.VMEM((slots * 8 * (tokens + 1), 128), F32),
            pltpu.VMEM((512, 128), F32),
        ],
        compiler_params=pltpu.CompilerParams(vmem_limit_bytes=60 << 20),
        cost_estimate=pl.CostEstimate(
            flops=tokens * inner * states * 20,
            bytes_accessed=5 * tokens * inner * 4,
            transcendentals=2 * tokens * inner * states,
        ),
        name="scan_backward",
    )(keep, proj, step, series, grad, decay2)


def conv_pair(values, segment, conv_w, conv_b):
    length, taps = values.shape[0], conv_w.shape[1]
    results = []
    for direction in (1, -1):
        result = conv_b[None, :] + conv_w[:, taps - 1][None, :] * values
        for offset in range(1, taps):
            zero_rows = jnp.zeros((offset, values.shape[1]), values.dtype)
            edge_seg = jnp.full((offset,), -1, jnp.int32)
            if direction > 0:
                moved = jnp.concatenate([zero_rows, values[: length - offset]], axis=0)
                moved_seg = jnp.concatenate([edge_seg, segment[: length - offset]])
            else:
                moved = jnp.concatenate([values[offset:], zero_rows], axis=0)
                moved_seg = jnp.concatenate([segment[offset:], edge_seg])
            matched = (moved_seg == segment).astype(values.dtype)[:, None]
            result = result + conv_w[:, taps - 1 - offset][None, :] * moved * matched
        results.append(jax.nn.silu(result))
    return tuple(results)


def per_device(
    tokens,
    segment,
    timestep,
    ada_weight,
    ada_bias,
    in_weight,
    conv_weight,
    convolution_bias,
    xproj_weight,
    dtproj_weight,
    dt_bias,
    a_log,
    d_skip,
    out_weight,
    cotangent,
):
    dp, fsdp = lax.axis_size("dp"), lax.axis_size("fsdp")
    devices = dp * fsdp
    slots = timestep.shape[0]
    length, width = tokens.shape
    taps, rank, states = conv_weight.shape[1], dtproj_weight.shape[1], a_log.shape[1]
    own = conv_weight.shape[0]
    inner = own * devices
    contract_rows = (((0,), (0,)), ((), ()))
    contract_cols = (((1,), (1,)), ((), ()))

    def full(w):
        return lax.all_gather(
            lax.all_gather(w, "dp", axis=1, tiled=True), "fsdp", axis=0, tiled=True
        )

    parts = [
        xproj_weight,
        dtproj_weight,
        conv_weight,
        convolution_bias[:, None],
        dt_bias[:, None],
        d_skip[:, None],
        a_log,
    ]
    widths = [p.shape[1] for p in parts]
    total_width = -(-sum(widths) // 128) * 128
    packed = jnp.concatenate(parts, axis=1)
    packed = jnp.pad(packed, ((0, 0), (0, total_width - packed.shape[1])))
    packed = lax.all_gather(packed, BOTH, axis=0, tiled=True).astype(F32)
    pieces, at = [], 0
    for w in widths:
        pieces.append(packed[:, at : at + w])
        at += w
    x_proj, dt_proj, conv_w, conv_b, bias_dt, skip, alog = pieces
    conv_b, bias_dt, skip = conv_b[:, 0], bias_dt[:, 0], skip[:, 0]

    times = lax.all_gather(timestep, BOTH, axis=0, tiled=True)
    ada_rows, ada_cols = ada_weight.shape
    row0 = lax.axis_index("fsdp") * ada_rows
    condition = embed_columns(
        times, row0 + jnp.arange(ada_rows, dtype=jnp.int32), width
    ).astype(BF16)
    bias_cols = ada_bias.shape[0]
    bias_part = lax.dynamic_update_slice(
        jnp.zeros((ada_cols,), F32), ada_bias.astype(F32), (lax.axis_index("fsdp") * bias_cols,)
    )
    partial = jnp.dot(condition, ada_weight, preferred_element_type=F32) + bias_part[None, :]
    swapped = lax.all_to_all(partial, BOTH, 0, 0, tiled=True)
    modulation = (
        swapped.reshape(dp, fsdp, slots, ada_cols).sum(axis=1).transpose(1, 0, 2).reshape(slots, dp * ada_cols)
    )
    picker = (segment[:, None] == jnp.arange(slots, dtype=jnp.int32)[None, :]).astype(F32)
    per_token = jnp.dot(picker, modulation, precision=high)
    shift_mod = per_token[:, :width]
    scale_mod = per_token[:, width : 2 * width]
    gate_mod = per_token[:, 2 * width :]
    centered = tokens - jnp.mean(tokens, axis=1, keepdims=True)
    inv_std = lax.rsqrt(jnp.mean(centered * centered, axis=1, keepdims=True) + 1e-06)
    normed = centered * inv_std
    hidden = (normed * (1.0 + scale_mod) + shift_mod).astype(BF16)

    in_full = full(in_weight)
    x_part = jnp.dot(hidden, in_full[:, :inner], preferred_element_type=F32)
    z_part = jnp.dot(hidden, in_full[:, inner:], preferred_element_type=F32)

    same = (segment[1:] == segment[:-1]).astype(F32)
    same = jnp.concatenate([jnp.zeros((1,), F32), same, jnp.zeros((1,), F32)])
    keeps = (same[0:length:8], same[8 : length + 1 : 8][::-1])

    decay = -jnp.exp(alog)
    decay2 = (decay * (1.0 / LN2)).T.reshape(states * inner // 128, 128)
    sizes = dict(tokens=length, inner=inner, states=states, rank=rank)

    series, conv_pull = jax.vjp(
        lambda v, w, b: conv_pair(v, segment, w, b), x_part, conv_w, conv_b
    )
    proj, step = [], []
    total = skip[None, :] * (series[0] + series[1])
    for k in range(2):
        projected = jnp.dot(series[k], x_proj, precision=high)
        pre = jnp.dot(projected[:, :rank], dt_proj.T, precision=high) + bias_dt[None, :]
        proj.append(projected)
        step.append(jax.nn.softplus(pre))
        scanned = scan_forward(
            keeps[k], projected, to_rows(step[k]), to_rows(series[k]), decay2, rev=k == 1, **sizes
        )
        total = total + from_rows(scanned, length, inner)

    gate = jax.nn.sigmoid(z_part)
    silu_z = z_part * gate
    mixer_low = (total * silu_z).astype(BF16)
    out_full = full(out_weight)
    branch = jnp.dot(mixer_low, out_full, preferred_element_type=F32)
    layer_out = tokens + gate_mod * branch

    branch_grad = (cotangent * gate_mod).astype(BF16)
    gate_grad = cotangent * branch
    grad_out_w = lax.dot_general(
        mixer_low, branch_grad, contract_rows, preferred_element_type=F32
    ).astype(BF16)
    mixer_grad = lax.dot_general(branch_grad, out_full, contract_cols, preferred_element_type=F32)
    total_grad = mixer_grad * silu_z
    z_grad = (mixer_grad * total * (gate * (1.0 + z_part * (1.0 - gate)))).astype(BF16)

    series_grad = []
    xproj_grad = dtproj_grad = bias_grad = alog_grad = 0.0
    for k in range(2):
        ddu, dd, r, da = scan_backward(
            keeps[k],
            proj[k],
            to_rows(step[k]),
            to_rows(series[k]),
            to_rows(total_grad),
            decay2,
            rev=k == 1,
            **sizes,
        )
        ddu, dd = from_rows(ddu, length, inner), from_rows(dd, length, inner)
        bc_grad = (
            jnp.sum(r, axis=-1)
            .reshape(states // GROUP, length, 2, GROUP)
            .transpose(1, 2, 0, 3)
            .reshape(length, 2 * states)
        )
        step_grad = ddu * series[k] + LN2 * dd
        pre_grad = step_grad * (1.0 - jnp.exp(-step[k]))
        proj_grad = jnp.concatenate([jnp.dot(pre_grad, dt_proj, precision=high), bc_grad], axis=1)
        series_grad.append(
            ddu * step[k]
            + skip[None, :] * total_grad
            + lax.dot_general(proj_grad, x_proj, contract_cols, precision=high)
        )
        xproj_grad += lax.dot_general(series[k], proj_grad, contract_rows, precision=high)
        dtproj_grad += lax.dot_general(pre_grad, proj[k][:, :rank], contract_rows, precision=high)
        bias_grad += jnp.sum(pre_grad, axis=0)
        alog_grad += da
    alog_grad = alog_grad.reshape(states, inner).T * decay
    skip_grad = jnp.sum(total_grad * (series[0] + series[1]), axis=0)
    x_grad, conv_w_grad, conv_b_grad = conv_pull(tuple(series_grad))
    x_grad = x_grad.astype(BF16)
    pair_low = jnp.concatenate([x_grad, z_grad], axis=1)

    grad_in_w = lax.dot_general(hidden, pair_low, contract_rows, preferred_element_type=F32).astype(BF16)
    hidden_grad = lax.dot_general(pair_low, in_full, contract_cols, preferred_element_type=F32)
    normed_grad = hidden_grad * (1.0 + scale_mod)
    grad_tokens = cotangent + inv_std * (
        normed_grad
        - jnp.mean(normed_grad, axis=1, keepdims=True)
        - normed * jnp.mean(normed_grad * normed, axis=1, keepdims=True)
    )
    token_mod_grad = jnp.concatenate([hidden_grad, hidden_grad * normed, gate_grad], axis=1)
    mod_low = lax.dot_general(picker, token_mod_grad, contract_rows, precision=high).astype(BF16)
    mod_all = lax.all_gather(mod_low, BOTH, axis=0, tiled=True)
    mod_cols = lax.dynamic_slice_in_dim(mod_all, lax.axis_index("dp") * ada_cols, ada_cols, axis=1)
    grad_ada_w = lax.dot_general(condition, mod_cols, contract_rows, preferred_element_type=F32)
    grad_ada_b = jnp.sum(
        lax.dynamic_slice_in_dim(
            mod_cols, lax.axis_index("fsdp") * bias_cols, bias_cols, axis=1
        ).astype(F32),
        axis=0,
    )

    def scattered(g):
        rows = lax.psum_scatter(g, "fsdp", scatter_dimension=0, tiled=True)
        return lax.psum_scatter(rows, "dp", scatter_dimension=1, tiled=True).astype(F32)

    grad_in_shard = scattered(grad_in_w)
    grad_out_shard = scattered(grad_out_w)
    small = jnp.concatenate(
        [
            xproj_grad,
            dtproj_grad,
            conv_w_grad,
            conv_b_grad[:, None],
            bias_grad[:, None],
            skip_grad[:, None],
            alog_grad,
        ],
        axis=1,
    )
    small = jnp.pad(small, ((0, 0), (0, total_width - small.shape[1])))
    small = lax.psum_scatter(small, BOTH, scatter_dimension=0, tiled=True)
    pieces, at = [], 0
    for w in widths:
        pieces.append(small[:, at : at + w])
        at += w
    g_xproj, g_dtproj, g_conv_w, g_conv_b, g_bias, g_skip, g_alog = pieces

    valid = (segment < slots).astype(F32)[:, None]
    out_sq, grad_sq, counted = lax.psum(
        (
            jnp.sum(layer_out * layer_out * valid),
            jnp.sum(grad_tokens * grad_tokens * valid),
            jnp.sum(valid) * width,
        ),
        BOTH,
    )
    return (
        layer_out,
        grad_tokens,
        grad_ada_w,
        grad_ada_b,
        grad_in_shard,
        g_conv_w,
        g_conv_b[:, 0],
        g_xproj,
        g_dtproj,
        g_bias[:, 0],
        g_alog,
        g_skip[:, 0],
        grad_out_shard,
        jnp.sqrt(out_sq / counted),
        jnp.sqrt(grad_sq / counted),
    )


def solution(mesh):
    rows, flat, block = P(BOTH, None), P(BOTH), P("fsdp", "dp")
    return jax.shard_map(
        per_device,
        mesh=mesh,
        in_specs=(
            rows, flat, flat, block, flat, block, rows, flat, rows, rows, flat, rows, flat, block, rows,
        ),
        out_specs=(
            rows, rows, block, flat, block, rows, flat, rows, rows, flat, rows, flat, block, P(), P(),
        ),
        check_vma=False,
    )
```

time: 3580 us -> 1350 us (0.38)
  matrix products: 1270 us -> 201 us
  local copies, waits for them, and re-layouts: 586 us -> 76.4 us
  waiting for transfers between devices: 1000 us -> 584 us
  other arithmetic: 386 us -> 95.8 us
  Pallas kernels: 0 us -> 284 us
  blocking collectives: 280 us -> 77.6 us
    dot_general x141 -> x22, matrix products: 1260 us -> 193 us  [the longest x2 41.9 us: per_device(): lax.dot_general(proj_grad, x_proj, contract_cols, precision=high)]
    reduce_scatter x6 -> x3, waiting for transfers between devices: 602 us -> 154 us  [the longest x2 115 us: scattered(): rows = lax.psum_scatter(g, 'fsdp', scatter_dimension=0, tiled=True)]
    pallas_call x0 -> x4, Pallas kernels: none -> 284 us  [the longest x2 197 us: scan_backward(): pl.pallas_call(body, out_shape=(jax.ShapeDtypeStruct((rows, 128), F32), j...]
    rev x11 -> x1, local copies, waits for them, and re-layouts: 224 us -> 0.61 us  [per_device(): keeps = (same[0:length:8], same[8:length + 1:8][::-1])]
    all_gather x4 -> x0, blocking collectives: 196 us -> none  [the longest x1 58.6 us: per_device(): lax.all_gather(dtproj_weight, ('dp', 'fsdp'), axis=0, tiled=True)]
    squeeze x168 -> x0, local copies, waits for them, and re-layouts: 128 us -> none  [linked_block_list(): lax.scan(jax.checkpoint(one_block), jnp.zeros((states_n, inner), jnp.floa...]
    reduce_sum x28 -> x7, other arithmetic: 173 us -> 50 us  [the longest x1 25 us: per_device(): bias_grad += jnp.sum(pre_grad, axis=0)]
    all_gather x6, waiting for transfers between devices: 216 us -> 287 us  [the longest x2 208 us: full(): lax.all_gather(lax.all_gather(w, 'dp', axis=1, tiled=True), 'fsdp', axis=...]
  transfers between devices with their start and end apart: 16 -> 12, of which waited for: 15 -> 10; matrix products, arithmetic and copies ran while one was open for 5% -> 19% of each run, Pallas kernels for 0% -> 0%
where the time goes in v1:
time: 1350 us; the launch traced here: 1340 us
  waiting for transfers between devices  584 us (43%)
  Pallas kernels  284 us (21%)
  matrix products  201 us (15%)
  other arithmetic  95.8 us (7%)
  blocking collectives  77.6 us (6%)
  local copies, waits for them, and re-layouts  76.4 us (6%)
  between operations  20.5 us (2%)
    all_gather x2, waiting for transfers between devices, full(): lax.all_gather(lax.all_gather(w, 'dp', axis=1, tiled=True), 'fsdp', axis=...  208 us
    pallas_call x2, Pallas kernels, scan_backward(): pl.pallas_call(body, out_shape=(jax.ShapeDtypeStruct((rows, 128), F32), j...  197 us
    unnamed x13, waiting for transfers between devices  126 us
    reduce_scatter x2, waiting for transfers between devices, scattered(): rows = lax.psum_scatter(g, 'fsdp', scatter_dimension=0, tiled=True)  115 us
    pallas_call x2, Pallas kernels, scan_forward(): pl.pallas_call(body, out_shape=jax.ShapeDtypeStruct((tokens * tiles, 128)...  87.1 us
    all_gather x2, waiting for transfers between devices, full(): lax.all_gather(w, 'dp', axis=1, tiled=True)  65.2 us
    dot_general x2, matrix products, per_device(): lax.dot_general(proj_grad, x_proj, contract_cols, precision=high)  41.9 us
    unnamed x1, blocking collectives  39.4 us
  transfers between devices with their start and end apart: 12, of which 10 were waited for; matrix products, arithmetic and copies ran while one was open for 19% of the time, Pallas kernels for 0%

profile of v1, /device:TPU:0, one launch (start us, length us, event | category | flops | bytes accessed | tf_op | source)
XLA Modules:
  0.0 1344.4 jit_solution(3932940085701567280)
XLA Ops:
  14.3 35.9 %all-gather.10.cloned.1.call-done = bf16[192,6144]{1,0:T(8,128)(2,1)} async-done(((bf16[192,1536]{1,0:T(8,128)(2,1)}), bf16[192,6144]{1,0:T(8,128)(2,1)}) %all-gather.10.cloned.1.call-update) | async-done | bytes 2359312 | tf_op jit(solution)/shard_map/all_gather | solution.py:282
  50.2 29.4 %all-gather.14.cloned.1.call-done = bf16[384,1536]{1,0:T(8,128)(2,1)} async-done(((bf16[384,384]{1,0:T(8,128)(2,1)}), bf16[384,1536]{1,0:T(8,128)(2,1)}) %all-gather.14.cloned.1.call-update) | async-done | bytes 1179664 | tf_op jit(solution)/shard_map/all_gather | solution.py:282
  79.8 39.4 %all-reduce.26 = s32[128]{0:T(128)S(1)} all-reduce(s32[128]{0:T(128)S(1)} %dynamic-update-slice), channel_id=1, replica_groups=mesh['dp'=4,'fsdp'=8] {'dp','fsdp'}, use_global_device_ids=true, to_apply=%add.26 | all-reduce | flops 128 | bytes 1024
  129.8 17.4 %all-to-all-done = f32[32,4,1152]{2,1,0:T(4,128)S(1)} async-done(((f32[32,4,1152]{2,1,0:T(4,128)}), f32[32,4,1152]{2,1,0:T(4,128)S(1)}, u32[]{:S(2)}, u32[]{:S(2)}) %all-to-all-start) | async-done | bytes 589856 | tf_op jit(solution)/shard_map/all_to_all | solution.py:317
  162.0 147.1 %all-gather.12.cloned.1.call-done = bf16[1536,6144]{1,0:T(8,128)(2,1)} async-done(((bf16[192,6144]{1,0:T(8,128)(2,1)}), bf16[1536,6144]{1,0:T(8,128)(2,1)}) %all-gather.12.cloned.1.call-update) | async-done | bytes 18874384 | tf_op jit(solution)/shard_map/all_gather | solution.py:281
  339.2 60.4 %all-gather.16.cloned.1.call-done = bf16[3072,1536]{1,0:T(8,128)(2,1)} async-done(((bf16[384,1536]{1,0:T(8,128)(2,1)}), bf16[3072,1536]{1,0:T(8,128)(2,1)}) %all-gather.16.cloned.1.call-update) | async-done | bytes 9437200 | tf_op jit(solution)/shard_map/all_gather | solution.py:281
  399.6 29.4 %multiply_reduce_fusion = (f32[3072]{0:T(1024)}, f32[384,3072]{1,0:T(8,128)}, f32[384,3072]{1,0:T(8,128)}, f32[384,3072]{1,0:T(8,128)}, f32[384,3072]{1,0:T(8,12...) fusion(f32[384,3072]{1,0:T(8,128)} %fusion, f32[384]{0:T(512)S(1)} %get-tuple-element.154, ...), kind=kOutput, calls=%fused_computation.29 | convolution fusion | flops 3666342912 | bytes 76612608 | tf_op jit(solution)/shard_map/dot_general | solution.py:370
  447.1 43.7 %scan_forward.3 = f32[9216,128]{1,0:T(8,128)} custom-call(f32[48]{0:T(128)} %rev.3.keep_ref, f32[384,128]{1,0:T(8,128)} %copy.55.proj_ref, f32[9216,128]{1,0:T(8,128)} %bitcast.137, f32[9216,128]{1,0:T(8,128)} %bitcast.121, f32[384,128]{1,0:T(8,128)} %reshape.254.a_ref), custom_call_target="tpu_custom_call" | custom-call | flops 132120576 | bytes 14155776 | tf_op jit(solution)/shard_map/scan_forward/pallas_call | solution.py:88
  490.8 98.3 %scan_backward.2 = (f32[9216,128]{1,0:T(8,128)}, f32[9216,128]{1,0:T(8,128)}, f32[12288,128]{1,0:T(8,128)}, f32[384,128]{1,0:T(8,128)}) custom-call(f32[48]{0:T(128)} %rev.3.keep_ref, f32[384,128]{1,0:T(8,128)} %copy.55.proj_ref, f32[9216,128]{1,0:T(8,128)} %bitcast.138, f32[9216,128]{1,0:T(8,128)} %bitcast.122, f32[9216,128]{1,0:T(8,128)} %bitcast.131, ...), custom_call_target="tpu_custom_call" | custom-call | flops 377487360 | bytes 23592960 | tf_op jit(solution)/shard_map/scan_backward/pallas_call | solution.py:208
  595.8 43.4 %scan_forward.2 = f32[9216,128]{1,0:T(8,128)} custom-call(f32[48]{0:T(128)} %slice.149.keep_ref, f32[384,128]{1,0:T(8,128)} %copy.54.proj_ref, f32[9216,128]{1,0:T(8,128)} %bitcast.133, f32[9216,128]{1,0:T(8,128)} %bitcast.127, f32[384,128]{1,0:T(8,128)} %reshape.254.a_ref), custom_call_target="tpu_custom_call" | custom-call | flops 132120576 | bytes 14155776 | tf_op jit(solution)/shard_map/scan_forward/pallas_call | solution.py:88
  639.1 98.3 %scan_backward.3 = (f32[9216,128]{1,0:T(8,128)}, f32[9216,128]{1,0:T(8,128)}, f32[12288,128]{1,0:T(8,128)}, f32[384,128]{1,0:T(8,128)}) custom-call(f32[48]{0:T(128)} %slice.149.keep_ref, f32[384,128]{1,0:T(8,128)} %copy.54.proj_ref, f32[9216,128]{1,0:T(8,128)} %bitcast.134, f32[9216,128]{1,0:T(8,128)} %bitcast.128, f32[9216,128]{1,0:T(8,128)} %bitcast.132, ...), custom_call_target="tpu_custom_call" | custom-call | flops 377487360 | bytes 23592960 | tf_op jit(solution)/shard_map/scan_backward/pallas_call | solution.py:208
  745.2 25.0 %fusion.87 = (f32[3072]{0:T(1024)S(1)}, f32[384,3072]{1,0:T(8,128)}, bf16[384,3072]{1,0:T(8,128)(2,1)}, f32[384,3072]{1,0:T(8,128)}, f32[3072]{0:T(1024)S(1)}, /*index=5*/f32[384,3072]{1,0:T(8,128)}) fusion(f32[384,3072]{1,0:T(8,128)} %compare_select_fusion, f32[384,3072]{1,0:T(8,128)} %bitcast.141, f32[384,3072]{1,0:T(8,128)} %bitcast.139, ...), kind=kLoop, calls=%fused_computation.160 | loop fusion | flops 30664704 | bytes 73175040 | tf_op jit(solution)/shard_map/reduce_sum | solution.py:404
  814.0 20.3 %multiply_reduce_fusion.8 = (f32[3072]{0:T(1024)S(1)}, f32[384,3072]{1,0:T(8,128)}, f32[3072]{0:T(1024)S(1)}, f32[384,3072]{1,0:T(8,128)}, f32[3072]{0:T(1024)S(...) fusion(f32[381,3072]{1,0:T(8,128)} %get-tuple-element.134, f32[384]{0:T(512)S(1)} %get-tuple-element.158, ...), kind=kOutput, calls=%fused_computation.37 | convolution fusion | flops 1837931520 | bytes 52869120 | tf_op jit(solution)/shard_map/dot_general | solution.py:400
  834.3 21.6 %multiply_reduce_fusion.4 = (f32[3072]{0:T(1024)S(1)}, f32[384,3072]{1,0:T(8,128)}, f32[3072]{0:T(1024)S(1)}, f32[384,3072]{1,0:T(8,128)}, f32[3072]{0:T(1024)S(...) fusion(f32[381,3072]{1,0:T(8,128)} %get-tuple-element.135, f32[384]{0:T(512)S(1)} %get-tuple-element.154, ...), kind=kOutput, calls=%fused_computation.33 | convolution fusion | flops 1837931520 | bytes 52869120 | tf_op jit(solution)/shard_map/dot_general | solution.py:400
  880.9 16.2 %fusion.83 = (f32[3072]{0:T(1024)S(1)}, f32[3072]{0:T(1024)S(1)}, f32[3072]{0:T(1024)S(1)}, f32[3072]{0:T(1024)S(1)}, bf16[384,3072]{1,0:T(8,128)(2,1)}) fusion(f32[384,3072]{1,0:T(8,128)} %get-tuple-element.167, f32[384,3072]{1,0:T(8,128)S(1)} %bitcast.120, f32[384,3072]{1,0:T(8,128)} %get-tuple-element.166, f32[383,3072]{1,0:T(8,128)} %get-tuple-element.151, ...), kind=kLoop, calls=%fused_computation.159 | loop fusion | flops 18862080 | bytes 44740608 | tf_op jit(solution)/shard_map/transpose(jvp())/reduce_sum | solution.py:237
  897.1 15.9 %convolution_convert_fusion = bf16[1536,6144]{1,0:T(8,128)(2,1)} fusion(bf16[384,1536]{1,0:T(8,128)(2,1)} %get-tuple-element.115, bf16[384,3072]{1,0:T(8,128)(2,1)S(1)} %copy-done.10, bf16[384,3072]{1,0:T(8,128)(2,1)} %get-tuple-element.113), kind=kOutput, calls=%fused_computation | convolution fusion | flops 7266631680 | bytes 24772608 | tf_op jit(solution)/shard_map/dot_general | solution.py:412
  914.6 15.5 %fusion.82 = (f32[384]{0:T(512)S(1)}, f32[384]{0:T(512)S(1)}, f32[384,1536]{1,0:T(8,128)}) fusion(f32[384,4608]{1,0:T(8,128)} %copy-done.3, f32[384]{0:T(512)S(1)} %copy-done.35, f32[384,1536]{1,0:T(8,128)S(1)} %copy-done.6, f32[384]{0:T(512)S(1)} %copy-done.32, bf16[1536,6144]{1,0:T(8,128)(2,1)} %all-gather.12.cloned.1.call-done, ...), kind=kOutput, calls=%fused_computation.158 | convolution fusion | flops 7261322240 | bytes 30676992 | tf_op jit(solution)/shard_map/dot_general | solution.py:413
  930.1 14.6 %multiply_reduce_fusion.9 = (f32[]{:T(128)}, f32[]{:T(128)}, f32[384,1536]{1,0:T(8,128)}, f32[384,1536]{1,0:T(8,128)}, f32[384,1536]{1,0:T(8,128)S(1)}, /*index=5*/f32[384,1536]{1,0:T(8,128)S(1)}) fusion(f32[384]{0:T(512)S(1)} %copy-done.36, f32[384,1536]{1,0:T(8,128)} %param.29, f32[384]{0:T(512)S(1)} %get-tuple-element.170, ...), kind=kOutput, calls=%fused_computation.60 | convolution fusion | flops 3635085312 | bytes 33037832 | tf_op jit(solution)/shard_map/dot_general | solution.py:362
  984.3 115.5 %reduce-scatter.10.cloned.1.call-done = bf16[192,6144]{1,0:T(8,128)(2,1)} async-done(((bf16[1536,6144]{1,0:T(8,128)(2,1)}), bf16[192,6144]{1,0:T(8,128)(2,1)}) %reduce-scatter.10.cloned.1.call-update) | async-done | bytes 2359312 | tf_op jit(solution)/shard_map/reduce_scatter | solution.py:433
  1101.1 38.2 %all-reduce.27 = (f32[]{:T(128)}, f32[]{:T(128)}, f32[]{:T(128)}) all-reduce(f32[]{:T(128)} %get-tuple-element.83, f32[]{:T(128)S(6)} %mul.567, f32[]{:T(128)} %get-tuple-element.82), channel_id=1, replica_groups=mesh['dp'=4,'fsdp'=8] {'dp','fsdp'}, use_global_device_ids=true, to_apply=%region_27.28 | all-reduce | flops 3 | bytes 24 | tf_op jit(solution)/shard_map/psum | solution.py:459
  1142.0 14.0 %all-gather.18.cloned.1.call-done = bf16[32,4,4608]{2,1,0:T(4,128)(2,1)} async-done(((bf16[1,4,4608]{2,1,0:T(4,128)(2,1)}), bf16[32,4,4608]{2,1,0:T(4,128)(2,1)}) %all-gather.18.cloned.1.call-update) | async-done | bytes 1179664 | tf_op jit(solution)/shard_map/all_gather | solution.py:422
  1159.8 102.0 %reduce-scatter.16.cloned.1.call-done = f32[96,256]{1,0:T(8,128)} async-done(((f32[3072,256]{1,0:T(8,128)}), f32[96,256]{1,0:T(8,128)}) %reduce-scatter.16.cloned.1.call-update) | async-done | bytes 98320
  1270.6 22.1 %reduce-scatter.18.cloned.1.call-done = bf16[384,384]{1,0:T(8,128)(2,1)} async-done(((bf16[1536,384]{1,0:T(8,128)(2,1)}), bf16[384,384]{1,0:T(8,128)(2,1)}) %reduce-scatter.18.cloned.1.call-update) | async-done | bytes 294928
  1294.8 38.5 %reduce-scatter.12.cloned.1.call-done = bf16[192,1536]{1,0:T(8,128)(2,1)} async-done(((bf16[192,6144]{1,0:T(8,128)(2,1)}), bf16[192,1536]{1,0:T(8,128)(2,1)}) %reduce-scatter.12.cloned.1.call-update) | async-done | bytes 589840 | tf_op jit(solution)/shard_map/reduce_scatter | solution.py:434
  (240 shorter events, 222.0 us)
Async XLA Ops:
  7.2 112.7 %copy-start = (bf16[192,1152]{1,0:T(8,128)(2,1)S(1)}, bf16[192,1152]{1,0:T(8,128)(2,1)}, u32[]{:S(2)}) copy-start(bf16[192,1152]{1,0:T(8,128)(2,1)} %param.18) | copy-start | bytes 1327108
  7.2 112.1 %copy-start.43 = (bf16[144]{0:T(256)(128)(2,1)S(1)}, bf16[144]{0:T(256)(128)(2,1)}, u32[]{:S(2)}) copy-start(bf16[144]{0:T(256)(128)(2,1)} %param.19) | copy-start | bytes 868
  7.2 119.7 %copy-start.5 = (f32[384,1536]{1,0:T(8,128)S(1)}, f32[384,1536]{1,0:T(8,128)}, u32[]{:S(2)}) copy-start(f32[384,1536]{1,0:T(8,128)} %param.15) | copy-start | bytes 7077892
  7.2 42.9 %all-gather.10.cloned.1.call-start = ((), (), s32[]{:S(2)}) async-start(), calls=%async_computation.7 | async-start | bytes 2949120 | tf_op jit(solution)/shard_map/all_gather | solution.py:282
  8.0 71.6 %all-gather.14.cloned.1.call-start = ((), (), s32[]{:S(2)}) async-start(), calls=%async_computation.9 | async-start | bytes 1474560 | tf_op jit(solution)/shard_map/all_gather | solution.py:282
  8.7 148.0 %all-gather.8.cloned.1.call-start = ((), (), s32[]{:S(2)}) async-start(), calls=%async_computation.6 | async-start | bytes 1622016 | tf_op jit(solution)/shard_map/all_gather | solution.py:298
  14.2 294.9 %all-gather.12.cloned.1.call-start = ((), (), s32[]{:S(2)}) async-start(), calls=%async_computation.8 | async-start | bytes 21233664 | tf_op jit(solution)/shard_map/all_gather | solution.py:281
  50.1 349.4 %all-gather.16.cloned.1.call-start = ((), (), s32[]{:S(2)}) async-start(), calls=%async_computation.10 | async-start | bytes 10616832 | tf_op jit(solution)/shard_map/all_gather | solution.py:281
  121.6 25.7 %all-to-all-start = ((f32[32,4,1152]{2,1,0:T(4,128)}), f32[32,4,1152]{2,1,0:T(4,128)S(1)}, u32[]{:S(2)}, u32[]{:S(2)}) async-start(f32[32,4,1152]{2,1,0:T(4,128)} %all_to_all.6), calls=%async_computation | async-start | bytes 1179648 | tf_op jit(solution)/shard_map/all_to_all | solution.py:317
  126.8 855.0 %reduce-scatter.14.cloned.1.call-start = ((), (), s32[]{:S(2)}) async-start(), calls=%async_computation.13 | async-start | bytes 10616832 | tf_op jit(solution)/shard_map/reduce_scatter | solution.py:433
  156.7 152.5 %copy-start.17 = (bf16[384,1536]{1,0:T(8,128)(2,1)S(1)}, bf16[384,1536]{1,0:T(8,128)(2,1)}, u32[]{:S(2)}) copy-start(bf16[384,1536]{1,0:T(8,128)(2,1)} %get-tuple-element.115) | copy-start | bytes 3538948
  162.0 237.6 %copy-start.24 = (f32[3072,1]{0,1:T(1,128)}, f32[3072,1]{0,1:T(1,128)S(1)}, u32[]{:S(2)}) copy-start(f32[3072,1]{0,1:T(1,128)S(1)} %get-tuple-element.139) | copy-start | bytes 36868
  162.0 237.6 %copy-start.26 = (f32[3072,1]{0,1:T(1,128)}, f32[3072,1]{0,1:T(1,128)S(1)}, u32[]{:S(2)}) copy-start(f32[3072,1]{0,1:T(1,128)S(1)} %get-tuple-element.141) | copy-start | bytes 36868
  162.0 237.6 %copy-start.28 = (f32[3072,1]{0,1:T(1,128)}, f32[3072,1]{0,1:T(1,128)S(1)}, u32[]{:S(2)}) copy-start(f32[3072,1]{0,1:T(1,128)S(1)} %get-tuple-element.140) | copy-start | bytes 36868
  439.6 149.5 %copy-start.13 = (f32[384,128]{0,1:T(8,128)}, f32[384,128]{0,1:T(8,128)S(1)}, u32[]{:S(2)}) copy-start(f32[384,128]{0,1:T(8,128)S(1)} %fusion.38) | copy-start | bytes 589828
  784.6 315.2 %reduce-scatter.10.cloned.1.call-start = ((), (), s32[]{:S(2)}) async-start(), calls=%async_computation.11 | async-start | bytes 21233664 | tf_op jit(solution)/shard_map/reduce_scatter | solution.py:433
  913.0 243.0 %all-gather.18.cloned.1.call-start = ((), (), s32[]{:S(2)}) async-start(), calls=%async_computation.14 | async-start | bytes 1216512 | tf_op jit(solution)/shard_map/all_gather | solution.py:422
  947.9 313.9 %reduce-scatter.16.cloned.1.call-start = ((), (), s32[]{:S(2)}) async-start(), calls=%async_computation.15 | async-start | bytes 3244032
  981.7 176.3 %copy-start.38 = (f32[192]{0:T(256)S(1)}, f32[192]{0:T(256)}, u32[]{:S(2)}) copy-start(f32[192]{0:T(256)} %copy-done.37) | copy-start | bytes 2308
  981.7 176.3 %copy-start.40 = (f32[128]{0:T(128)S(1)}, f32[128]{0:T(128)}, u32[]{:S(2)}) copy-start(f32[128]{0:T(128)} %copy-done.39) | copy-start | bytes 1540
  981.8 176.3 %copy-start.42 = (pred[192]{0:T(512)(128)(4,1)S(1)}, pred[192]{0:T(512)(128)(4,1)}, u32[]{:S(2)}) copy-start(pred[192]{0:T(512)(128)(4,1)} %copy-done.41) | copy-start | bytes 580
  981.8 311.0 %reduce-scatter.18.cloned.1.call-start = ((), (), s32[]{:S(2)}) async-start(), calls=%async_computation.16 | async-start | bytes 1474560
  984.3 349.0 %reduce-scatter.12.cloned.1.call-start = ((), (), s32[]{:S(2)}) async-start(), calls=%async_computation.12 | async-start | bytes 2949120 | tf_op jit(solution)/shard_map/reduce_scatter | solution.py:434
  1099.8 235.7 %copy-start.1 = (bf16[192,1152]{1,0:T(8,128)(2,1)S(1)}, bf16[192,1152]{1,0:T(8,128)(2,1)}, u32[]{:S(2)}) copy-start(bf16[192,1152]{1,0:T(8,128)(2,1)} %param.18) | copy-start | bytes 1327108
  (44 other events, 493.1 us)
Sparse Core Ops, SparseCore 0:
  9.9 40.1 all-gather.9
  51.9 27.5 all-gather.13
  83.1 56.1 all-gather.7
  140.9 168.2 all-gather.11
  310.6 88.9 all-gather.15
  784.7 97.9 reduce-scatter.13
  913.1 186.6 reduce-scatter.9
  1103.4 52.5 all-gather.17
  1161.4 100.3 reduce-scatter.15
  1265.2 27.5 reduce-scatter.17
  1295.8 37.3 reduce-scatter.11

commit v2 on v1

v2 whole, which is shorter than its diff:
```python
import math

import jax
import jax.numpy as jnp
from jax import lax
from jax.experimental import pallas as pl
from jax.experimental.pallas import tpu as pltpu
from jax.sharding import Mesh, PartitionSpec as P

F32 = jnp.float32
BF16 = jnp.bfloat16
LN2 = math.log(2.0)
ALL = ("dp", "fz", "core")
high = lax.Precision.HIGHEST
GROUP = 4


def embed_columns(time_values, column, model_width):
    half_width = model_width // 2
    lower_half = column < half_width
    freq_index = jnp.where(lower_half, column, column - half_width).astype(F32)
    frequency = jnp.exp(freq_index * (-math.log(10000.0) / half_width))
    angles = time_values.astype(F32)[:, None] * frequency[None, :]
    return jax.nn.silu(jnp.where(lower_half[None, :], jnp.cos(angles), jnp.sin(angles)))


def fill_columns(proj_ref, bc_ref, tokens, first, group, states):
    def fill(i, _):
        p = proj_ref[pl.ds(pl.multiple_of(i * 8, 8), 8), :]
        for s in range(2):
            for n in range(GROUP):
                col = first + s * states + group * GROUP + n
                row = pl.multiple_of((s * GROUP + n) * tokens + i * 8, 8)
                bc_ref[pl.ds(row, 8), :] = jnp.broadcast_to(p[:, col : col + 1], (8, 128))
        return 0

    lax.fori_loop(0, tokens // 8, fill, 0)


VMEM = pl.BlockSpec(memory_space=pltpu.VMEM)
SMEM = pl.BlockSpec(memory_space=pltpu.SMEM)
ANY = pl.BlockSpec(memory_space=pl.ANY)


def dot(a, b):
    return jnp.dot(a, b, preferred_element_type=F32)


def dot_nt(a, b):
    return lax.dot_general(a, b, (((1,), (1,)), ((), ())), preferred_element_type=F32)


def shifted(ext, j, ahead):
    n = ext.shape[0] - 2
    sub = lax.broadcasted_iota(jnp.int32, (n, 8, 128), 1)
    if ahead:
        r = pltpu.roll(ext, 8 - j, 1)
        return jnp.where(sub >= 8 - j, r[2:], r[1:-1])
    r = pltpu.roll(ext, j, 1)
    return jnp.where(sub < j, r[:-2], r[1:-1])


def extended(ref, k, q, size, keep_ref, slots):
    zero = jnp.zeros((1, 8, 128), F32)
    lo, hi = q * size, (q + 1) * size
    before = ref[pl.ds(lo - 1, 1), k] * keep_ref[q] if q else zero
    after = ref[pl.ds(hi, 1), k] * keep_ref[q + 1] if q < slots - 1 else zero
    return jnp.concatenate([before, ref[pl.ds(lo, size), k], after], axis=0)


def convolved(ext, p, taps):
    here = ext[1:-1]
    both, moves = [], []
    for ahead in (False, True):
        c = p[taps : taps + 1][None] + p[taps - 1 : taps][None] * here
        for j in range(1, taps):
            m = shifted(ext, j, ahead)
            moves.append(m)
            c = c + p[taps - 1 - j : taps - j][None] * m
        both.append(c)
    return both, moves


def project(hidden, weight, *, rows, length, inner):
    blocks, owners, _, cols = weight.shape
    tiles = cols // 128

    def body(h_ref, w_ref, o_ref):
        w = w_ref[0].reshape(owners * rows, cols)
        r = dot(h_ref[...], w)
        for k in range(tiles):
            o_ref[:, k] = r[:, k * 128 : (k + 1) * 128].reshape(length // 8, 8, 128)

    return pl.pallas_call(
        body,
        grid=(blocks,),
        out_shape=jax.ShapeDtypeStruct((length // 8, inner // 128, 8, 128), F32),
        in_specs=[
            pl.BlockSpec(hidden.shape, lambda b: (0, 0)),
            pl.BlockSpec((1, owners, rows, cols), lambda b: (b, 0, 0, 0)),
        ],
        out_specs=pl.BlockSpec((length // 8, tiles, 8, 128), lambda b: (0, b, 0, 0)),
        compiler_params=pltpu.CompilerParams(vmem_limit_bytes=40 << 20),
        cost_estimate=pl.CostEstimate(
            flops=2 * length * hidden.shape[1] * inner,
            bytes_accessed=2 * hidden.shape[1] * inner + 4 * length * inner,
            transcendentals=0,
        ),
        name="project",
    )(hidden, weight)


def mixer_forward(keep, bound, x, x_proj, dt_proj, params, decay2, *, tokens, inner, states, rank, taps, slots):
    blocks, tiles, octets = inner // 1024, inner // 128, tokens // 8
    size = octets // slots
    rows = tokens * tiles

    def body(keep_ref, bound_ref, x_ref, xw_ref, dt_ref, p_ref, a_ref, y_ref, sf_ref, sr_ref, df_ref, dr_ref, proj_ref, bc_ref):
        shape4 = (octets, tiles, 8, 128)
        y4 = y_ref.reshape(shape4)
        s4 = (sf_ref.reshape(shape4), sr_ref.reshape(shape4))
        d4 = (df_ref.reshape(shape4), dr_ref.reshape(shape4))

        def conv(k, _):
            p = p_ref[k]
            skip = p[taps + 2 : taps + 3][None]
            for q in range(slots):
                both, _ = convolved(extended(x_ref, k, q, size, bound_ref, slots), p, taps)
                sl = pl.ds(q * size, size)
                series = [c * jax.nn.sigmoid(c) for c in both]
                for ref, v in zip(s4, series):
                    ref[sl, k] = v
                y4[sl, k] = skip * (series[0] + series[1])
            return 0

        lax.fori_loop(0, tiles, conv, 0)
        lanes = lax.broadcasted_iota(jnp.int32, (tokens, 128), 1)
        for s in range(2):
            total = jnp.zeros((tokens, 128), F32)
            for k in range(0, tiles, 2):
                lhs = jnp.concatenate(
                    [s4[s][:, k + i].reshape(tokens, 128).astype(BF16) for i in range(2)], axis=1
                )
                total = total + dot(lhs, xw_ref[pl.ds(k * 128, 256), :])
            proj_ref[s] = total
            low = jnp.where(lanes < rank, total, 0.0).astype(BF16)
            for k in range(0, tiles, 2):
                pre = dot_nt(low, dt_ref[pl.ds(k * 128, 256), :])
                for i in range(2):
                    v = pre[:, i * 128 : (i + 1) * 128] + p_ref[k + i, taps + 1 : taps + 2, :]
                    step = jnp.maximum(v, 0.0) + jnp.log1p(jnp.exp(-jnp.abs(v)))
                    d4[s][:, k + i] = step.reshape(octets, 8, 128)
        for s, (d_ref, u_ref) in enumerate(((df_ref, sf_ref), (dr_ref, sr_ref))):
            rev = s == 1
            for ng in range(states // GROUP):
                fill_columns(proj_ref.at[s], bc_ref, tokens, rank, ng, states)
                a = [
                    [a_ref[pl.ds((ng * GROUP + n) * tiles + c * 8, 8), :] for c in range(blocks)]
                    for n in range(GROUP)
                ]

                def octet(i, hs):
                    g = (octets - 1 - i) if rev else i
                    keep_now = keep_ref[s, i]
                    hs = [h * keep_now for h in hs]
                    base = pl.multiple_of(g * (tiles * 8), 8)
                    for j in range(8):
                        tt = 7 - j if rev else j
                        t = g * 8 + tt
                        for c in range(blocks):
                            sl = pl.ds(base + c * 64 + tt, 8, stride=8)
                            d = d_ref[sl, :]
                            du = d * u_ref[sl, :]
                            acc = None
                            for n in range(GROUP):
                                b = bc_ref[pl.ds(n * tokens + t, 1), :]
                                cc = bc_ref[pl.ds((GROUP + n) * tokens + t, 1), :]
                                k = n * blocks + c
                                hs[k] = jnp.exp2(d * a[n][c]) * hs[k] + du * b
                                acc = hs[k] * cc if acc is None else acc + hs[k] * cc
                            y_ref[sl, :] = y_ref[sl, :] + acc
                    return hs

                lax.fori_loop(0, octets, octet, [jnp.zeros((8, 128), F32)] * (GROUP * blocks))

    big = jax.ShapeDtypeStruct((rows, 128), F32)
    return pl.pallas_call(
        body,
        out_shape=(big,) * 5 + (jax.ShapeDtypeStruct((2, tokens, 128), F32),),
        in_specs=[SMEM, SMEM] + [VMEM] * 5,
        out_specs=(VMEM,) * 6,
        scratch_shapes=[pltpu.VMEM((2 * GROUP * tokens, 128), F32)],
        compiler_params=pltpu.CompilerParams(vmem_limit_bytes=56 << 20),
        cost_estimate=pl.CostEstimate(
            flops=tokens * inner * states * 160,
            bytes_accessed=6 * rows * 512,
            transcendentals=2 * tokens * inner * states,
        ),
        name="mixer_forward",
    )(keep, bound, x, x_proj, dt_proj, params, decay2)


def mixer_middle(place, hidden, weight, out_weight, branch_grad, total, *, rows, length, inner):
    blocks, owners, _, cols = weight.shape[0], weight.shape[1], 0, weight.shape[-1]
    packed = out_weight is None
    dp, per, wide = branch_grad.shape[0], owners // blocks, branch_grad.shape[2]
    tiles, octets = cols // 128, length // 8
    half = rows
    width = hidden.shape[1]

    def body(place_ref, h_ref, wz_ref, wo_ref, bg_ref, t_ref, g_ref, dz_ref, br_ref, *more):
        ml_ref, gz_ref, go_ref, ht_ref, sem = more[-5:]
        b = pl.program_id(0)
        where = place_ref[b]

        def copies():
            if packed:
                return [
                    pltpu.make_async_copy(gz_ref, more[0].at[b, :, 0], sem.at[0]),
                    pltpu.make_async_copy(go_ref, more[0].at[:, pl.ds(where * per, per), 1], sem.at[1]),
                ]
            return [
                pltpu.make_async_copy(gz_ref, more[0].at[b], sem.at[0]),
                pltpu.make_async_copy(go_ref, more[1].at[:, pl.ds(where * per, per)], sem.at[1]),
            ]

        z = dot(h_ref[...], wz_ref[...].reshape(owners * rows, cols))

        def out_rows(d):
            if not packed:
                return wo_ref[d].reshape(cols, wide)
            pieces = []
            for j in range(per):
                for i in range(2):
                    pieces.append(wo_ref[d, j, 0, :, i * wide : (i + 1) * wide])
            return jnp.concatenate(pieces, axis=0)

        mg = dot_nt(bg_ref[0], out_rows(0))
        for d in range(1, dp):
            mg = mg + dot_nt(bg_ref[d], out_rows(d))
        for k in range(tiles):
            sl = slice(k * 128, (k + 1) * 128)
            zk, mk, tk = z[:, sl], mg[:, sl], t_ref[:, k].reshape(length, 128)
            gate = jax.nn.sigmoid(zk)
            silu = zk * gate
            ml_ref[:, sl] = (tk * silu).astype(BF16)
            g_ref[:, k] = (mk * silu).reshape(octets, 8, 128)
            dz_ref[:, sl] = (mk * tk * (gate * (1.0 + zk * (1.0 - gate)))).astype(BF16)
        ml = ml_ref[...]
        ml_t = ml.T

        @pl.when(b == 0)
        def _():
            br_ref[...] = jnp.zeros_like(br_ref)
            ht_ref[...] = h_ref[...].T

        @pl.when(b > 0)
        def _():
            for c in copies():
                c.wait()

        for d in range(dp):
            br_ref[d] = br_ref[d] + dot(ml, out_rows(d))
            go = dot(ml_t, bg_ref[d]).astype(BF16)
            if packed:
                at = 0
                for j in range(per):
                    for i in range(2):
                        go_ref[d, j, :, i * wide : (i + 1) * wide] = go[at : at + half]
                        at += half
            else:
                go_ref[d] = go.reshape(go_ref.shape[1:])
        gz_ref[...] = dot(ht_ref[...], dz_ref[...]).astype(BF16).reshape(owners, rows, cols)
        for c in copies():
            c.start()

        @pl.when(b == blocks - 1)
        def _():
            for c in copies():
                c.wait()

    if packed:
        wz_spec = pl.BlockSpec((1, owners, 1, rows, cols), lambda b, p: (b, 0, 0, 0, 0))
        wo_spec = pl.BlockSpec((dp, per, 1, rows, cols), lambda b, p: (0, p[b], 1, 0, 0))
        extra = (jax.ShapeDtypeStruct((blocks, owners, 2, rows, cols), BF16),)
        go_shape = (dp, per, rows, cols)
        out_weight = weight
    else:
        wz_spec = pl.BlockSpec((1, owners, rows, cols), lambda b, p: (b, 0, 0, 0))
        wo_spec = pl.BlockSpec((dp, per, 2 * rows, wide), lambda b, p: (0, p[b], 0, 0))
        extra = (
            jax.ShapeDtypeStruct((blocks, owners, rows, cols), BF16),
            jax.ShapeDtypeStruct((dp, owners, 2 * rows, wide), BF16),
        )
        go_shape = (dp, per, 2 * rows, wide)
    whole = lambda v: pl.BlockSpec(v.shape, lambda b, p: (0,) * v.ndim)
    tile_spec = pl.BlockSpec((octets, tiles, 8, 128), lambda b, p: (0, b, 0, 0))
    return pl.pallas_call(
        body,
        grid_spec=pltpu.PrefetchScalarGridSpec(
            num_scalar_prefetch=1,
            grid=(blocks,),
            in_specs=[
                whole(hidden),
                wz_spec,
                wo_spec,
                whole(branch_grad),
                tile_spec,
            ],
            out_specs=(
                tile_spec,
                pl.BlockSpec((length, cols), lambda b, p: (0, b)),
                pl.BlockSpec((dp, length, wide), lambda b, p: (0, 0, 0)),
            )
            + (ANY,) * len(extra),
            scratch_shapes=[
                pltpu.VMEM((length, cols), BF16),
                pltpu.VMEM((owners, rows, cols), BF16),
                pltpu.VMEM(go_shape, BF16),
                pltpu.VMEM((width, length), BF16),
                pltpu.SemaphoreType.DMA((2,)),
            ],
        ),
        out_shape=(
            jax.ShapeDtypeStruct((octets, inner // 128, 8, 128), F32),
            jax.ShapeDtypeStruct((length, inner), BF16),
            jax.ShapeDtypeStruct((dp, length, wide), F32),
        )
        + extra,
        compiler_params=pltpu.CompilerParams(vmem_limit_bytes=56 << 20),
        cost_estimate=pl.CostEstimate(
            flops=10 * length * width * inner, bytes_accessed=60 << 20, transcendentals=length * inner
        ),
        name="mixer_middle",
    )(place, hidden, weight, out_weight, branch_grad, total)


def mixer_backward(keep, proj, step, series, grad, decay2, x_proj, dt_proj, params, *, rev, tokens, inner, states, rank, taps):
    blocks, tiles, octets = inner // 1024, inner // 128, tokens // 8
    slots = GROUP * blocks
    rows = tokens * tiles

    def body(
        keep_ref, proj_ref, d_ref, u_ref, g_ref, a_ref, xw_ref, dt_ref, p_ref,
        ddu_ref, small_ref, da_ref, skip_ref,
        dd_ref, bc_ref, h_ref, q_ref, r_ref, cols_ref,
    ):
        zero = jnp.zeros((8, 128), F32)
        cols_ref[...] = jnp.zeros_like(cols_ref)
        for ng in range(states // GROUP):
            fill_columns(proj_ref, bc_ref, tokens, rank, ng, states)
            a = [
                [a_ref[pl.ds((ng * GROUP + n) * tiles + c * 8, 8), :] for c in range(blocks)]
                for n in range(GROUP)
            ]
            for k in range(slots):
                h_ref[pl.ds(k * 8, 8), :] = zero

            def ahead(i, hs):
                g = (octets - 1 - i) if rev else i
                keep_now = keep_ref[i]
                hs = [h * keep_now for h in hs]
                base = pl.multiple_of(g * (tiles * 8), 8)
                for j in range(8):
                    tt = 7 - j if rev else j
                    t = g * 8 + tt
                    hb = pl.multiple_of((i * 8 + j + 1) * (slots * 8), 8)
                    for c in range(blocks):
                        sl = pl.ds(base + c * 64 + tt, 8, stride=8)
                        d = d_ref[sl, :]
                        du = d * u_ref[sl, :]
                        for n in range(GROUP):
                            b = bc_ref[pl.ds(n * tokens + t, 1), :]
                            k = n * blocks + c
                            hs[k] = jnp.exp2(d * a[n][c]) * hs[k] + du * b
                            h_ref[pl.ds(hb + k * 8, 8), :] = hs[k]
                return hs

            lax.fori_loop(0, octets, ahead, [zero] * slots)

            def back(ii, carry):
                gs, das = [list(v) for v in carry]
                i = octets - 1 - ii
                g = (octets - 1 - i) if rev else i
                keep_now = keep_ref[i]
                base = pl.multiple_of(g * (tiles * 8), 8)
                for jj in range(8):
                    j = 7 - jj
                    tt = 7 - j if rev else j
                    t = g * 8 + tt
                    hb = pl.multiple_of((i * 8 + j) * (slots * 8), 8)
                    pb, pc = [None] * GROUP, [None] * GROUP
                    for c in range(blocks):
                        sl = pl.ds(base + c * 64 + tt, 8, stride=8)
                        d = d_ref[sl, :]
                        du = d * u_ref[sl, :]
                        gy = g_ref[sl, :]
                        ddu = dd = None
                        for n in range(GROUP):
                            b = bc_ref[pl.ds(n * tokens + t, 1), :]
                            cc = bc_ref[pl.ds((GROUP + n) * tokens + t, 1), :]
                            k = n * blocks + c
                            before = h_ref[pl.ds(hb + k * 8, 8), :]
                            after = h_ref[pl.ds(hb + (slots + k) * 8, 8), :]
                            adj = gs[k] + cc * gy
                            x = after * gy
                            pc[n] = x if c == 0 else pc[n] + x
                            x = adj * du
                            pb[n] = x if c == 0 else pb[n] + x
                            x = adj * b
                            ddu = x if n == 0 else ddu + x
                            moved = adj * jnp.exp2(d * a[n][c])
                            if j == 0:
                                moved = moved * keep_now
                            gs[k] = moved
                            m = moved * before
                            x = m * a[n][c]
                            dd = x if n == 0 else dd + x
                            das[k] = das[k] + m * d
                        if ng == 0:
                            ddu_ref[sl, :] = ddu
                            dd_ref[sl, :] = dd
                        else:
                            ddu_ref[sl, :] = ddu_ref[sl, :] + ddu
                            dd_ref[sl, :] = dd_ref[sl, :] + dd
                    for n in range(GROUP):
                        q_ref[pl.ds(j * 64 + n * 8, 8), :] = pb[n]
                        q_ref[pl.ds(j * 64 + (GROUP + n) * 8, 8), :] = pc[n]
                for j in range(8):
                    tt = 7 - j if rev else j
                    t = g * 8 + tt
                    s = None
                    for q in range(8):
                        x = q_ref[pl.ds(j * 64 + q, 8, stride=8), :]
                        s = x if s is None else s + x
                    r_ref[pl.ds(pl.multiple_of(t * 8, 8), 8), :] = s
                return gs, das

            _, das = lax.fori_loop(0, octets, back, ([zero] * slots, [zero] * slots))
            for n in range(GROUP):
                for c in range(blocks):
                    da_ref[pl.ds((ng * GROUP + n) * tiles + c * 8, 8), :] = das[n * blocks + c]
            lane = lax.broadcasted_iota(jnp.int32, (128, 128), 1)
            for q in range(2 * GROUP):
                col = rank + (q // GROUP) * states + ng * GROUP + q % GROUP
                one = jnp.where(lane == col, 1.0, 0.0).astype(BF16)
                v = r_ref[pl.ds(q, tokens, stride=8), :]
                high_part = v.astype(BF16)
                low_part = (v - high_part.astype(F32)).astype(BF16)
                cols_ref[...] += dot(high_part, one) + dot(low_part, one)
        shape4 = (octets, tiles, 8, 128)
        d4, u4, g4, ddu4, dd4 = [r.reshape(shape4) for r in (d_ref, u_ref, g_ref, ddu_ref, dd_ref)]
        lanes = lax.broadcasted_iota(jnp.int32, (tokens, 128), 1)
        low = jnp.where(lanes < rank, proj_ref[...], jnp.where(lanes == rank, 1.0, 0.0)).astype(BF16)
        low_t = low.T
        proj_grad = jnp.zeros((tokens, 128), F32)
        for k in range(0, tiles, 2):
            pair = []
            for i in range(2):
                d, u, gy, ddu = d4[:, k + i], u4[:, k + i], g4[:, k + i], ddu4[:, k + i]
                pre = (ddu * u + LN2 * dd4[:, k + i]) * (1.0 - jnp.exp(-d))
                pair.append(pre.reshape(tokens, 128).astype(BF16))
                ddu4[:, k + i] = ddu * d + p_ref[k + i, taps + 2 : taps + 3, :][None] * gy
                skip_ref[k + i] = jnp.sum(gy * u, axis=0)
            pre = jnp.concatenate(pair, axis=1)
            proj_grad = proj_grad + dot(pre, dt_ref[pl.ds(k * 128, 256), :])
            small_ref[128:256, k * 128 : (k + 2) * 128] = dot(low_t, pre)
        proj_grad = jnp.where(lanes < rank, proj_grad, cols_ref[...]).astype(BF16)
        proj_t = proj_grad.T
        for k in range(0, tiles, 2):
            pair = [u4[:, k + i].reshape(tokens, 128).astype(BF16) for i in range(2)]
            small_ref[0:128, k * 128 : (k + 2) * 128] = dot(proj_t, jnp.concatenate(pair, axis=1))
            more = dot_nt(proj_grad, xw_ref[pl.ds(k * 128, 256), :])
            for i in range(2):
                ddu4[:, k + i] = ddu4[:, k + i] + more[:, i * 128 : (i + 1) * 128].reshape(octets, 8, 128)

    return pl.pallas_call(
        body,
        out_shape=(
            jax.ShapeDtypeStruct((rows, 128), F32),
            jax.ShapeDtypeStruct((256, inner), F32),
            jax.ShapeDtypeStruct((states * tiles, 128), F32),
            jax.ShapeDtypeStruct((tiles, 8, 128), F32),
        ),
        in_specs=[SMEM] + [VMEM] * 8,
        out_specs=(VMEM,) * 4,
        scratch_shapes=[
            pltpu.VMEM((rows, 128), F32),
            pltpu.VMEM((2 * GROUP * tokens, 128), F32),
            pltpu.VMEM((slots * 8 * (tokens + 1), 128), F32),
            pltpu.VMEM((512, 128), F32),
            pltpu.VMEM((tokens * 8, 128), F32),
            pltpu.VMEM((tokens, 128), F32),
        ],
        compiler_params=pltpu.CompilerParams(vmem_limit_bytes=60 << 20),
        cost_estimate=pl.CostEstimate(
            flops=tokens * inner * states * 160,
            bytes_accessed=5 * rows * 512,
            transcendentals=2 * tokens * inner * states,
        ),
        name="mixer_backward",
    )(keep, proj, step, series, grad, decay2, x_proj, dt_proj, params)


def mixer_finish(bound, x, grads, params, hidden, z_grad, wx, wz, *, rows, total_rows, length, inner, taps, slots):
    blocks, owners, cols = wx.shape[0], wx.shape[1], wx.shape[-1]
    tiles, octets = cols // 128, length // 8
    size = octets // slots
    width = hidden.shape[1]
    packed = wz.ndim == 5

    def body(bound_ref, x_ref, gf_ref, gr_ref, p_ref, h_ref, dz_ref, wx_ref, wz_ref, gx_ref, hg_ref, gw_ref, cf_ref, cr_ref, dx_ref, ht_ref):
        def first(k, _):
            p = p_ref[k]
            sums = [jnp.zeros((8, 128), F32) for _ in range(taps + 1)]
            for q in range(slots):
                ext = extended(x_ref, k, q, size, bound_ref, slots)
                both, moves = convolved(ext, p, taps)
                sl = pl.ds(q * size, size)
                for s, (c, src, dst) in enumerate(zip(both, (gf_ref, gr_ref), (cf_ref, cr_ref))):
                    gate = jax.nn.sigmoid(c)
                    dc = src[sl, k] * (gate * (1.0 + c * (1.0 - gate)))
                    dst[sl, k] = dc
                    sums[taps] = sums[taps] + jnp.sum(dc, axis=0)
                    sums[taps - 1] = sums[taps - 1] + jnp.sum(dc * ext[1:-1], axis=0)
                    for j in range(1, taps):
                        m = moves[s * (taps - 1) + j - 1]
                        sums[taps - 1 - j] = sums[taps - 1 - j] + jnp.sum(dc * m, axis=0)
            for i, v in enumerate(sums):
                gw_ref[k, i] = v
            return 0

        @pl.when(pl.program_id(0) == 0)
        def _():
            ht_ref[...] = h_ref[...].T

        lax.fori_loop(0, tiles, first, 0)
        for k in range(tiles):
            p = p_ref[k]
            for q in range(slots):
                ef = extended(cf_ref, k, q, size, bound_ref, slots)
                er = extended(cr_ref, k, q, size, bound_ref, slots)
                v = p[taps - 1 : taps][None] * (ef[1:-1] + er[1:-1])
                for j in range(1, taps):
                    v = v + p[taps - 1 - j : taps - j][None] * (shifted(ef, j, True) + shifted(er, j, False))
                dx_ref[pl.ds(q * size * 8, size * 8), k * 128 : (k + 1) * 128] = v.reshape(size * 8, 128).astype(BF16)
        dx = dx_ref[...]
        gx_ref[0] = dot(ht_ref[...], dx).astype(BF16).reshape(owners, rows, cols)
        hg = dot_nt(dx, wx_ref[...].reshape(owners * rows, cols)) + dot_nt(
            dz_ref[...], wz_ref[...].reshape(owners * rows, cols)
        )

        @pl.when(pl.program_id(0) == 0)
        def _():
            hg_ref[...] = hg

        @pl.when(pl.program_id(0) > 0)
        def _():
            hg_ref[...] = hg_ref[...] + hg

    tile_spec = pl.BlockSpec((octets, tiles, 8, 128), lambda b: (0, b, 0, 0))
    w_spec = pl.BlockSpec((1, owners, rows, cols), lambda b: (b, 0, 0, 0))
    z_spec = pl.BlockSpec((1, owners, 1, rows, cols), lambda b: (b, 0, 0, 0, 0)) if packed else w_spec
    return pl.pallas_call(
        body,
        grid=(blocks,),
        in_specs=[
            SMEM,
            tile_spec,
            tile_spec,
            tile_spec,
            pl.BlockSpec((tiles, 8, 128), lambda b: (b, 0, 0)),
            pl.BlockSpec(hidden.shape, lambda b: (0, 0)),
            pl.BlockSpec((length, cols), lambda b: (0, b)),
            w_spec,
            z_spec,
        ],
        out_specs=(
            pl.BlockSpec((1, owners, rows, cols), lambda b: (b, 0, 0, 0)),
            pl.BlockSpec((length, width), lambda b: (0, 0)),
            pl.BlockSpec((tiles, taps + 1, 8, 128), lambda b: (b, 0, 0, 0)),
        ),
        out_shape=(
            jax.ShapeDtypeStruct((blocks, owners, total_rows, cols), BF16),
            jax.ShapeDtypeStruct((length, width), F32),
            jax.ShapeDtypeStruct((inner // 128, taps + 1, 8, 128), F32),
        ),
        scratch_shapes=[
            pltpu.VMEM((octets, tiles, 8, 128), F32),
            pltpu.VMEM((octets, tiles, 8, 128), F32),
            pltpu.VMEM((length, cols), BF16),
            pltpu.VMEM((width, length), BF16),
        ],
        compiler_params=pltpu.CompilerParams(vmem_limit_bytes=56 << 20),
        cost_estimate=pl.CostEstimate(
            flops=6 * length * width * inner, bytes_accessed=45 << 20, transcendentals=2 * length * inner
        ),
        name="mixer_finish",
    )(bound, x, grads[0], grads[1], params, hidden, z_grad, wx, wz)


def swap(v, axis, k):
    return lax.ppermute(v, axis, [(i, i ^ k) for i in range(lax.axis_size(axis))])


def others(v, axis):
    return jnp.stack([v] + [swap(v, axis, k) for k in range(1, lax.axis_size(axis))])


def gather_all(v):
    return others(others(others(v, "dp"), "fz"), "core")


def per_device(
    tokens,
    segment,
    timestep,
    ada_weight,
    ada_bias,
    in_weight,
    conv_weight,
    convolution_bias,
    xproj_weight,
    dtproj_weight,
    dt_bias,
    a_log,
    d_skip,
    out_weight,
    cotangent,
):
    dp, fz, cores = [lax.axis_size(n) for n in ALL]
    my_dp = lax.axis_index("dp")
    my_j = lax.axis_index("fz") * cores + lax.axis_index("core")
    fsdp = fz * cores
    devices = dp * fsdp
    slots = timestep.shape[0]
    length, width = tokens.shape
    taps, rank, states = conv_weight.shape[1], dtproj_weight.shape[1], a_log.shape[1]
    own = conv_weight.shape[0]
    inner = own * devices
    rows, cols = in_weight.shape[0], in_weight.shape[1] // 2
    wide = out_weight.shape[1]
    packs = wide % 128 == 0
    contract_rows = (((0,), (0,)), ((), ()))

    lower = my_dp < dp // 2
    opposite = [(i, (i + dp // 2) % dp) for i in range(dp)]
    left, right = in_weight[:, :cols], in_weight[:, cols:]
    got = lax.ppermute(jnp.where(lower, right, left), "dp", opposite)
    kept = jnp.where(lower, left, right)
    x_cols, z_cols = jnp.where(lower, kept, got), jnp.where(lower, got, kept)
    order = [(b % (dp // 2)) * 2 + b // (dp // 2) for b in range(dp)]

    parts = [
        xproj_weight,
        dtproj_weight,
        conv_weight,
        convolution_bias[:, None],
        dt_bias[:, None],
        d_skip[:, None],
        a_log,
    ]
    packed = jnp.concatenate(parts, axis=1)
    packed = jnp.pad(packed, ((0, 0), (0, 256 - packed.shape[1])))
    tail = own * 256 // cols
    g_x = lax.all_gather(jnp.concatenate([x_cols, packed.reshape(tail, cols)], axis=0), ALL, axis=0, tiled=True)
    g_x = g_x.reshape(dp, fsdp, rows + tail, cols)
    times = gather_all(timestep).reshape(-1)
    ada_rows, ada_cols = ada_weight.shape
    condition = embed_columns(
        times, my_j * ada_rows + jnp.arange(ada_rows, dtype=jnp.int32), width
    ).astype(BF16)
    bias_cols = ada_bias.shape[0]
    bias_part = lax.dynamic_update_slice(
        jnp.zeros((ada_cols,), F32), ada_bias.astype(F32), (my_j * bias_cols,)
    )
    partial = jnp.dot(condition, ada_weight, preferred_element_type=F32) + bias_part[None, :]
    partial = partial.reshape(cores, fz, dp, slots, ada_cols)
    for axis, n in (("core", cores), ("fz", fz)):
        partial = partial[0] + sum(swap(partial[k], axis, k) for k in range(1, n))
    blocks = jnp.stack([partial[0]] + [swap(partial[k], "dp", k) for k in range(1, dp)])
    modulation = jnp.concatenate(
        [lax.dynamic_index_in_dim(blocks, my_dp ^ b, keepdims=False) for b in range(dp)], axis=1
    )
    picker = (segment[:, None] == jnp.arange(slots, dtype=jnp.int32)[None, :]).astype(F32)
    per_token = jnp.dot(picker, modulation, precision=high)
    shift_mod = per_token[:, :width]
    scale_mod = per_token[:, width : 2 * width]
    gate_mod = per_token[:, 2 * width :]
    centered = tokens - jnp.mean(tokens, axis=1, keepdims=True)
    inv_std = lax.rsqrt(jnp.mean(centered * centered, axis=1, keepdims=True) + 1e-06)
    normed = centered * inv_std
    hidden = (normed * (1.0 + scale_mod) + shift_mod).astype(BF16)
    branch_grad = (cotangent * gate_mod).astype(BF16)
    branch_grad = branch_grad.reshape(length, dp, wide).transpose(1, 0, 2)

    if packs:
        out_piece = jnp.concatenate([out_weight[:rows], out_weight[rows:]], axis=1)
        later = jnp.stack([z_cols, out_piece])
        later, g_x, hidden = lax.optimization_barrier((later, g_x, hidden))
        g_z = lax.all_gather(later, ALL, axis=0, tiled=True).reshape(dp, fsdp, 2, rows, cols)
        g_out = None
    else:
        g_z = lax.all_gather(z_cols, ALL, axis=0, tiled=True).reshape(dp, fsdp, rows, cols)
        g_out = lax.all_gather(out_weight, ALL, axis=0, tiled=True).reshape(dp, fsdp, 2 * rows, wide)

    packed = g_x[:, :, rows:, :].reshape(dp, inner // dp, 256)
    packed = jnp.concatenate([packed[o] for o in order], axis=0)
    x_proj, dt_proj = packed[:, :128], packed[:, 128:256]
    rest = packed[:, 128 + rank :].astype(F32).T
    params = rest[:8].reshape(8, inner // 128, 128).transpose(1, 0, 2)
    decay = -jnp.exp(rest[taps + 3 : taps + 3 + states])
    decay2 = (decay * (1.0 / LN2)).reshape(states * inner // 128, 128)

    same = (segment[1:] == segment[:-1]).astype(F32)
    same = jnp.concatenate([jnp.zeros((1,), F32), same, jnp.zeros((1,), F32)])
    keep_f, keep_r = same[0:length:8], same[8 : length + 1 : 8][::-1]
    bound = same[0 : length : length // slots]
    sizes = dict(tokens=length, inner=inner, states=states, rank=rank, taps=taps)

    x = project(hidden, g_x, rows=rows, length=length, inner=inner)
    total, series_f, series_r, step_f, step_r, proj = mixer_forward(
        jnp.stack([keep_f, keep_r]), bound, x, x_proj, dt_proj, params, decay2, slots=slots, **sizes
    )
    tile_shape = (length // 8, inner // 128, 8, 128)
    middle = mixer_middle(
        jnp.asarray(order, jnp.int32),
        hidden,
        g_z,
        g_out,
        branch_grad,
        total.reshape(tile_shape),
        rows=rows,
        length=length,
        inner=inner,
    )
    grad, z_grad, branch = middle[:3]
    branch = branch.transpose(1, 0, 2).reshape(length, width)
    layer_out = tokens + gate_mod * branch
    gate_grad = cotangent * branch

    def scattered(v):
        return lax.psum_scatter(v.reshape(-1, v.shape[-1]), ALL, scatter_dimension=0, tiled=True)

    if packs:
        early = scattered(middle[3])
        z_shard, out_shard = early[:rows], early[rows:]
        out_shard = jnp.concatenate([out_shard[:, :wide], out_shard[:, wide:]], axis=0)
    else:
        z_shard, out_shard = early = scattered(middle[3]), scattered(middle[4])

    grad = grad.reshape(total.shape)
    series_grad, small, da, skip_part = [], 0.0, 0.0, 0.0
    for k, (keep, step, series) in enumerate(((keep_f, step_f, series_f), (keep_r, step_r, series_r))):
        got = mixer_backward(
            keep, proj[k], step, series, grad, decay2, x_proj, dt_proj, params, rev=k == 1, **sizes
        )
        series_grad.append(got[0].reshape(tile_shape))
        small, da, skip_part = small + got[1], da + got[2], skip_part + got[3]

    g_in, hidden_grad, conv_part = mixer_finish(
        bound,
        x,
        series_grad,
        params,
        hidden,
        z_grad,
        g_x,
        g_z,
        rows=rows,
        total_rows=rows + tail,
        length=length,
        inner=inner,
        taps=taps,
        slots=slots,
    )
    conv_rows = conv_part.sum(axis=2).transpose(1, 0, 2).reshape(taps + 1, inner)
    small_t = jnp.concatenate(
        [
            small[: 128 + rank],
            conv_rows,
            small[128 + rank : 128 + rank + 1],
            skip_part.sum(axis=1).reshape(1, inner),
            da.reshape(states, inner) * decay,
            jnp.zeros((256 - 128 - rank - taps - 3 - states, inner), F32),
        ],
        axis=0,
    ).astype(BF16)
    small = small_t.T.reshape(dp, inner // dp, 256)
    small = jnp.concatenate([small[order.index(o)] for o in range(dp)], axis=0)
    g_in = lax.dynamic_update_slice(g_in, small.reshape(dp, fsdp, tail, cols), (0, 0, rows, 0))
    g_in, _ = lax.optimization_barrier((g_in, early))
    got = scattered(g_in)
    x_shard, small = got[:rows], got[rows:].reshape(own, 256).astype(F32)
    got = lax.ppermute(jnp.where(lower, z_shard, x_shard), "dp", opposite)
    grad_in_shard = jnp.where(
        lower,
        jnp.concatenate([x_shard, got], axis=1),
        jnp.concatenate([got, z_shard], axis=1),
    ).astype(F32)

    normed_grad = hidden_grad * (1.0 + scale_mod)
    grad_tokens = cotangent + inv_std * (
        normed_grad
        - jnp.mean(normed_grad, axis=1, keepdims=True)
        - normed * jnp.mean(normed_grad * normed, axis=1, keepdims=True)
    )
    token_mod_grad = jnp.concatenate([hidden_grad, hidden_grad * normed, gate_grad], axis=1)
    mod_low = lax.dot_general(picker, token_mod_grad, contract_rows, precision=high).astype(BF16)
    mod_all = gather_all(mod_low).reshape(devices * slots, dp * ada_cols)
    mod_cols = lax.dynamic_slice_in_dim(mod_all, my_dp * ada_cols, ada_cols, axis=1)
    grad_ada_w = lax.dot_general(condition, mod_cols, contract_rows, preferred_element_type=F32)
    grad_ada_b = jnp.sum(
        lax.dynamic_slice_in_dim(mod_cols, my_j * bias_cols, bias_cols, axis=1).astype(F32), axis=0
    )
    valid = (segment < slots).astype(F32)[:, None]
    sums = jnp.stack(
        [
            jnp.sum(layer_out * layer_out * valid),
            jnp.sum(grad_tokens * grad_tokens * valid),
            jnp.sum(valid) * width,
        ]
    )
    sums = jnp.sum(gather_all(jnp.pad(sums, (0, 125))).reshape(devices, 128), axis=0)
    out_sq, grad_sq, counted = sums[0], sums[1], sums[2]
    at = 128 + rank
    return (
        layer_out,
        grad_tokens,
        grad_ada_w,
        grad_ada_b,
        grad_in_shard,
        small[:, at : at + taps],
        small[:, at + taps],
        small[:, :128],
        small[:, 128:at],
        small[:, at + taps + 1],
        small[:, at + taps + 3 : at + taps + 3 + states],
        small[:, at + taps + 2],
        out_shard.astype(F32),
        jnp.sqrt(out_sq / counted),
        jnp.sqrt(grad_sq / counted),
    )


def solution(mesh):
    dp, fsdp = mesh.devices.shape
    cores = 2 if fsdp % 2 == 0 else 1
    split = Mesh(mesh.devices.reshape(dp, fsdp // cores, cores), ALL)
    rows, flat, block = P(ALL, None), P(ALL), P(("fz", "core"), "dp")
    return jax.shard_map(
        per_device,
        mesh=split,
        in_specs=(
            rows, flat, flat, block, flat, block, rows, flat, rows, rows, flat, rows, flat, block, rows,
        ),
        out_specs=(
            rows, rows, block, flat, block, rows, flat, rows, rows, flat, rows, flat, block, P(), P(),
        ),
        check_vma=False,
    )
```

time: 1350 us -> 716 us (0.53)
  waiting for transfers between devices: 584 us -> 174 us
  matrix products: 201 us -> 10.3 us
  Pallas kernels: 284 us -> 389 us
  blocking collectives: 77.6 us -> 0 us
  other arithmetic: 95.8 us -> 36 us
  local copies, waits for them, and re-layouts: 76.4 us -> 41.8 us
  starting transfers between devices: 5.64 us -> 37.2 us
    all_gather x6 -> x2, waiting for transfers between devices: 287 us -> 55.5 us  [the longest x1 49.8 us: per_device(): lax.all_gather(jnp.concatenate([x_cols, packed.reshape(tail, cols)], axis...]
    dot_general x19 -> x0, matrix products: 192 us -> none  [the longest x2 41.9 us: per_device(): lax.dot_general(proj_grad, x_proj, contract_cols, precision=high)]
    unnamed x13 -> x4, waiting for transfers between devices: 126 us -> 0.07 us
    pallas_call x4 -> x6, Pallas kernels: 284 us -> 389 us  [the longest x2 208 us: mixer_backward(): pl.pallas_call(body, out_shape=(jax.ShapeDtypeStruct((rows, 128), F32), j...]
    reduce_scatter x3 -> x2, waiting for transfers between devices: 154 us -> 77.9 us  [scattered(): lax.psum_scatter(v.reshape(-1, v.shape[-1]), ALL, scatter_dimension=0, ti...]
    ppermute x0 -> x30, waiting for transfers between devices: none -> 40.6 us  [the longest x28 38 us: swap(): lax.ppermute(v, axis, [(i, i ^ k) for i in range(lax.axis_size(axis))])]
    unnamed x1 -> x0, blocking collectives: 39.4 us -> none
    psum x1 -> x0, blocking collectives: 38.2 us -> none  [per_device(): lax.psum((jnp.sum(layer_out * layer_out * valid), jnp.sum(grad_tokens * g...]
  transfers between devices with their start and end apart: 12 -> 34, of which waited for: 10 -> 22; matrix products, arithmetic and copies ran while one was open for 19% -> 10% of each run, Pallas kernels for 0% -> 49%
where the time goes in v2:
time: 716 us; the launch traced here: 709 us
  Pallas kernels  389 us (54%)
  waiting for transfers between devices  174 us (24%)
  local copies, waits for them, and re-layouts  41.8 us (6%)
  starting transfers between devices  37.2 us (5%)
  other arithmetic  36 us (5%)
  between operations  20.9 us (3%)
  matrix products  10.3 us (1%)
    pallas_call x2, Pallas kernels, mixer_backward(): pl.pallas_call(body, out_shape=(jax.ShapeDtypeStruct((rows, 128), F32), j...  208 us
    pallas_call x1, Pallas kernels, mixer_forward(): pl.pallas_call(body, out_shape=(big,) * 5 + (jax.ShapeDtypeStruct((2, tok...  98.5 us
    reduce_scatter x2, waiting for transfers between devices, scattered(): lax.psum_scatter(v.reshape(-1, v.shape[-1]), ALL, scatter_dimension=0, ti...  77.9 us
    all_gather x1, waiting for transfers between devices, per_device(): lax.all_gather(jnp.concatenate([x_cols, packed.reshape(tail, cols)], axis...  49.8 us
    pallas_call x1, Pallas kernels, mixer_middle(): pl.pallas_call(body, grid_spec=pltpu.PrefetchScalarGridSpec(num_scalar_pr...  42.7 us
    ppermute x28, waiting for transfers between devices, swap(): lax.ppermute(v, axis, [(i, i ^ k) for i in range(lax.axis_size(axis))])  38 us
    pallas_call x1, Pallas kernels, mixer_finish(): pl.pallas_call(body, grid=(blocks,), in_specs=[SMEM, tile_spec, tile_spec...  32.7 us
    ppermute x28, starting transfers between devices, swap(): lax.ppermute(v, axis, [(i, i ^ k) for i in range(lax.axis_size(axis))])  32.3 us
  transfers between devices with their start and end apart: 34, of which 22 were waited for; matrix products, arithmetic and copies ran while one was open for 10% of the time, Pallas kernels for 49%

profile of v2, /device:TPU:0, one launch (start us, length us, event | category | flops | bytes accessed | tf_op | source)
XLA Modules:
  0.0 709.4 jit_solution(6577405882284232407)
XLA Ops:
  8.5 3.0 collective-permute-start.14
  29.9 2.6 collective-permute-start.4
  34.5 3.4 collective-permute-done.5
  42.2 4.1 collective-permute-start.9
  46.3 2.5 collective-permute-done.10
  57.0 3.0 fusion.17
  60.0 2.8 copy-done.4
  63.8 49.8 %all-gather.3.cloned.1.call-done = bf16[7168,768]{1,0:T(8,128)(2,1)} async-done(((bf16[224,768]{1,0:T(8,128)(2,1)}), bf16[7168,768]{1,0:T(8,128)(2,1)}) %all-gather.3.cloned.1.call-update) | async-done | bytes 11010064 | tf_op jit(solution)/shard_map/all_gather | solution.py:666
  125.9 7.1 project.1.x_ref
  136.4 98.5 %mixer_forward.1 = (f32[9216,128]{1,0:T(8,128)}, f32[9216,128]{1,0:T(8,128)}, f32[9216,128]{1,0:T(8,128)}, f32[9216,128]{1,0:T(8,128)}, f32[9216,128]{1,0:T(8,128)}, /*index=5*/f32[2,384,128]{2,1,0:T(8,128)}) custom-call(f32[2,48]{1,0:T(2,128)} %pad_maximum_fusion.9.keep_ref, f32[4]{0:T(128)} %slice.203.bound_ref, f32[48,24,8,128]{3,2,1,0:T(8,128)} %copy-done.2, ...), custom_call_target="tpu_custom_call" | custom-call | flops 3019898880 | bytes 28311552 | tf_op jit(solution)/shard_map/mixer_forward/pallas_call | solution.py:187
  234.9 5.7 all-gather.5.cloned.1.call-done
  240.6 42.7 %mixer_middle.1 = (f32[48,24,8,128]{3,2,1,0:T(8,128)}, bf16[384,3072]{1,0:T(8,128)(2,1)}, f32[4,384,384]{2,1,0:T(8,128)}, bf16[4,8,2,192,768]{4,3,2,1,0:T(8,128)(2,1)}) custom-call(s32[4]{0:T(128)} %constant.87.clone.place_ref, bf16[384,1536]{1,0:T(8,128)(2,1)} %copy-done.3, bf16[4,8,2,192,768]{4,3,2,1,0:T(8,128)(2,1)} %bitcast.131, ...), custom_call_target="tpu_custom_call" | custom-call | flops 18119393280 | bytes 62914560 | tf_op jit(solution)/shard_map/mixer_middle/pallas_call | solution.py:298
  285.0 104.5 %mixer_backward.3 = (f32[9216,128]{1,0:T(8,128)}, f32[256,3072]{1,0:T(8,128)}, f32[384,128]{1,0:T(8,128)}, f32[24,8,128]{2,1,0:T(8,128)}) custom-call(f32[48]{0:T(128)} %copy-done.25, f32[384,128]{1,0:T(8,128)} %get-tuple-element.156.proj_ref, f32[9216,128]{1,0:T(8,128)} %get-tuple-element.50.d_ref, f32[9216,128]{1,0:T(8,128)} %get-tuple-element.51.u_ref, ...), custom_call_target="tpu_custom_call" | custom-call | flops 3019898880 | bytes 23592960 | tf_op jit(solution)/shard_map/mixer_backward/pallas_call | solution.py:477
  389.5 103.8 %mixer_backward.2 = (f32[9216,128]{1,0:T(8,128)}, f32[256,3072]{1,0:T(8,128)}, f32[384,128]{1,0:T(8,128)}, f32[24,8,128]{2,1,0:T(8,128)}) custom-call(f32[48]{0:T(128)} %copy-done.24, f32[384,128]{1,0:T(8,128)} %get-tuple-element.157.proj_ref, f32[9216,128]{1,0:T(8,128)} %get-tuple-element.46.d_ref, f32[9216,128]{1,0:T(8,128)} %get-tuple-element.47.u_ref, ...), custom_call_target="tpu_custom_call" | custom-call | flops 3019898880 | bytes 23592960 | tf_op jit(solution)/shard_map/mixer_backward/pallas_call | solution.py:477
  493.4 3.2 add_convert_fusion
  502.1 32.7 %mixer_finish.1 = (bf16[4,8,224,768]{3,2,1,0:T(8,128)(2,1)}, f32[384,1536]{1,0:T(8,128)}, f32[24,5,8,128]{3,2,1,0:T(8,128)}) custom-call(f32[4]{0:T(128)} %slice.203.bound_ref, f32[48,24,8,128]{3,2,1,0:T(8,128)} %copy-done.2, f32[48,24,8,128]{3,2,1,0:T(8,128)} %bitcast.139, f32[48,24,8,128]{3,2,1,0:T(8,128)} %bitcast.138, f32[24,8,128]{2,1,0:T(8,128)} %bitcast.152, ...), custom_call_target="tpu_custom_call" | custom-call | flops 10871635968 | bytes 47185920 | tf_op jit(solution)/shard_map/mixer_finish/pallas_call | solution.py:564
  538.8 2.8 reshape.186
  546.8 4.3 fusion.50
  552.9 5.2 multiply_reduce_fusion.1
  566.4 3.2 collective-permute-start.28
  571.8 4.8 fusion.6
  584.6 3.7 collective-permute-start.19
  591.1 13.1 %collective-permute-done.19 = bf16[4,4,4608]{2,1,0:T(4,128)(2,1)S(1)} collective-permute-done((bf16[4,4,4608]{2,1,0:T(4,128)(2,1)S(1)}, bf16[4,4,4608]{2,1,0:T(4,128)(2,1)S(1)}, u32[]{:S(2)}, u32[]{:S(2)}) %collective-permute-start.19) | collective-permute-done | bytes 147488 | tf_op jit(solution)/shard_map/ppermute | solution.py:603
  613.3 77.9 %reduce-scatter.5.cloned.1.call-done = bf16[224,768]{1,0:T(8,128)(2,1)} async-done(((bf16[7168,768]{1,0:T(8,128)(2,1)}), bf16[224,768]{1,0:T(8,128)(2,1)}) %reduce-scatter.5.cloned.1.call-update) | async-done | bytes 344080 | tf_op jit(solution)/shard_map/reduce_scatter | solution.py:743
  (230 shorter events, 104.0 us)
Async XLA Ops:
  7.2 106.4 %all-gather.3.cloned.1.call-start = ((), (), s32[]{:S(2)}) async-start(), calls=%async_computation.2 | async-start | bytes 11354112 | tf_op jit(solution)/shard_map/all_gather | solution.py:666
  8.5 10.0 %collective-permute-start.14 = (bf16[192,768]{1,0:T(8,128)(2,1)S(1)}, bf16[192,768]{1,0:T(8,128)(2,1)S(1)}, u32[]{:S(2)}, u32[]{:S(2)}) collective-permute-start(bf16[192,768]{1,0:T(8,128)(2,1)S(1)} %broadcast_select_fusion.3), channel_id=1, source_target_pairs={{0,16},{8,24},{16,0},{24,8},{1,17},{9,25},{17,1},{25,9},{2,18},{10... | collective-permute-start | bytes 884744 | tf_op jit(solution)/shard_map/ppermute | solution.py:649
  20.4 220.1 %all-gather.5.cloned.1.call-start = ((), (), s32[]{:S(2)}) async-start(), calls=%async_computation.3 | async-start | bytes 19464192 | tf_op jit(solution)/shard_map/all_gather | solution.py:701
  23.8 4.4 collective-permute-start.2
  28.2 4.5 collective-permute-start.3
  29.9 4.6 collective-permute-start.4
  32.5 5.4 collective-permute-start.5
  41.8 7.0 collective-permute-start.10
  42.2 6.7 collective-permute-start.8
  42.2 8.2 %collective-permute-start.9 = (f32[4,4,1152]{2,1,0:T(4,128)S(1)}, f32[4,4,1152]{2,1,0:T(4,128)S(1)}, u32[]{:S(2)}, u32[]{:S(2)}) collective-permute-start(f32[4,4,1152]{2,1,0:T(4,128)S(1)} %get-tuple-element.159), channel_id=1, source_target_pairs={{0,4},{2,6},{4,0},{6,2},{1,5},{3,7},{5,1},{7,3},{8,12},{10,14},{12... | collective-permute-start | bytes 221192 | tf_op jit(solution)/shard_map/ppermute | solution.py:603
  52.0 5.0 collective-permute-start.13
  113.6 429.4 %reduce-scatter.3.cloned.1.call-start = ((), (), s32[]{:S(2)}) async-start(), calls=%async_computation.4 | async-start | bytes 19464192 | tf_op jit(solution)/shard_map/reduce_scatter | solution.py:743
  283.3 407.8 %reduce-scatter.5.cloned.1.call-start = ((), (), s32[]{:S(2)}) async-start(), calls=%async_computation.5 | async-start | bytes 11354112 | tf_op jit(solution)/shard_map/reduce_scatter | solution.py:743
  559.5 4.9 collective-permute-start.23
  565.1 4.5 collective-permute-start.26
  565.2 4.5 collective-permute-start.27
  566.4 5.4 collective-permute-start.28
  571.8 8.5 %collective-permute-start.29 = (f32[4,4,128]{2,1,0:T(4,128)S(1)}, f32[4,4,128]{2,1,0:T(4,128)S(1)}, u32[]{:S(2)}, u32[]{:S(2)}) collective-permute-start(f32[4,4,128]{2,1,0:T(4,128)S(1)} %pad_maximum_fusion.7), channel_id=1, source_target_pairs={{0,1},{1,0},{2,3},{3,2},{4,5},{5,4},{6,7},{7,6},{8,9},{9,8},{10,11... | collective-permute-start | bytes 24584 | tf_op jit(solution)/shard_map/ppermute | solution.py:603
  576.6 5.0 collective-permute-start.15
  579.3 4.9 collective-permute-start.17
  584.3 6.8 collective-permute-start.18
  584.6 19.7 %collective-permute-start.19 = (bf16[4,4,4608]{2,1,0:T(4,128)(2,1)S(1)}, bf16[4,4,4608]{2,1,0:T(4,128)(2,1)S(1)}, u32[]{:S(2)}, u32[]{:S(2)}) collective-permute-start(bf16[4,4,4608]{2,1,0:T(4,128)(2,1)S(1)} %pad_maximum_fusion.5), channel_id=1, source_target_pairs={{0,4},{2,6},{4,0},{6,2},{1,5},{3,7},{5,1},{7,3},{8,12},{10,14},{12... | collective-permute-start | bytes 442376 | tf_op jit(solution)/shard_map/ppermute | solution.py:603
  588.3 15.9 %collective-permute-start.20 = (bf16[4,4,4608]{2,1,0:T(4,128)(2,1)S(1)}, bf16[4,4,4608]{2,1,0:T(4,128)(2,1)S(1)}, u32[]{:S(2)}, u32[]{:S(2)}) collective-permute-start(bf16[4,4,4608]{2,1,0:T(4,128)(2,1)S(1)} %pad_maximum_fusion.5), channel_id=1, source_target_pairs={{0,6},{2,4},{4,2},{6,0},{1,7},{3,5},{5,3},{7,1},{8,14},{10,12},{12... | collective-permute-start | bytes 442376 | tf_op jit(solution)/shard_map/ppermute | solution.py:603
  692.2 6.8 collective-permute-start.22
  (39 other events, 391.3 us)
Sparse Core Ops, SparseCore 0:
  20.6 93.0 all-gather.2
  117.2 123.3 all-gather.4
  283.4 204.9 reduce-scatter.2
  543.1 147.9 reduce-scatter.4

commit v3 on v2

--- a/solution.py
+++ b/solution.py
@@ -34,7 +34,7 @@
                 bc_ref[pl.ds(row, 8), :] = jnp.broadcast_to(p[:, col : col + 1], (8, 128))
         return 0
 
-    lax.fori_loop(0, tokens // 8, fill, 0)
+    lax.fori_loop(0, tokens // 8, fill, 0, unroll=8)
 
 
 VMEM = pl.BlockSpec(memory_space=pltpu.VMEM)
@@ -79,6 +79,22 @@
             c = c + p[taps - 1 - j : taps - j][None] * m
         both.append(c)
     return both, moves
+
+
+def sublane_sums(vs):
+    sub = lax.broadcasted_iota(jnp.int32, (8, 128), 0)
+    for sh in (4, 2, 1):
+        upper = (sub & sh) != 0
+        half = len(vs) // 2
+        vs = [
+            jnp.where(
+                upper,
+                vs[q + half] + pltpu.roll(vs[q + half], sh, 0),
+                vs[q] + pltpu.roll(vs[q], 8 - sh, 0),
+            )
+            for q in range(half)
+        ]
+    return vs[0]
 
 
 def project(hidden, weight, *, rows, length, inner):
@@ -343,7 +359,7 @@
     def body(
         keep_ref, proj_ref, d_ref, u_ref, g_ref, a_ref, xw_ref, dt_ref, p_ref,
         ddu_ref, small_ref, da_ref, skip_ref,
-        dd_ref, bc_ref, h_ref, q_ref, r_ref, cols_ref,
+        dd_ref, bc_ref, h_ref, r_ref, cols_ref,
     ):
         zero = jnp.zeros((8, 128), F32)
         cols_ref[...] = jnp.zeros_like(cols_ref)
@@ -423,17 +439,7 @@
                         else:
                             ddu_ref[sl, :] = ddu_ref[sl, :] + ddu
                             dd_ref[sl, :] = dd_ref[sl, :] + dd
-                    for n in range(GROUP):
-                        q_ref[pl.ds(j * 64 + n * 8, 8), :] = pb[n]
-                        q_ref[pl.ds(j * 64 + (GROUP + n) * 8, 8), :] = pc[n]
-                for j in range(8):
-                    tt = 7 - j if rev else j
-                    t = g * 8 + tt
-                    s = None
-                    for q in range(8):
-                        x = q_ref[pl.ds(j * 64 + q, 8, stride=8), :]
-                        s = x if s is None else s + x
-                    r_ref[pl.ds(pl.multiple_of(t * 8, 8), 8), :] = s
+                    r_ref[pl.ds(pl.multiple_of(t * 8, 8), 8), :] = sublane_sums(pb + pc)
                 return gs, das
 
             _, das = lax.fori_loop(0, octets, back, ([zero] * slots, [zero] * slots))
@@ -488,7 +494,6 @@
             pltpu.VMEM((rows, 128), F32),
             pltpu.VMEM((2 * GROUP * tokens, 128), F32),
             pltpu.VMEM((slots * 8 * (tokens + 1), 128), F32),
-            pltpu.VMEM((512, 128), F32),
             pltpu.VMEM((tokens * 8, 128), F32),
             pltpu.VMEM((tokens, 128), F32),
         ],
@@ -502,14 +507,15 @@
     )(keep, proj, step, series, grad, decay2, x_proj, dt_proj, params)
 
 
-def mixer_finish(bound, x, grads, params, hidden, z_grad, wx, wz, *, rows, total_rows, length, inner, taps, slots):
-    blocks, owners, cols = wx.shape[0], wx.shape[1], wx.shape[-1]
+def mixer_finish(place, bound, x, grads, params, hidden, *, rows, cols, owners, length, inner, taps, slots):
+    blocks = inner // cols
     tiles, octets = cols // 128, length // 8
     size = octets // slots
     width = hidden.shape[1]
-    packed = wz.ndim == 5
-
-    def body(bound_ref, x_ref, gf_ref, gr_ref, p_ref, h_ref, dz_ref, wx_ref, wz_ref, gx_ref, hg_ref, gw_ref, cf_ref, cr_ref, dx_ref, ht_ref):
+    cores = 2
+    fz = owners // cores
+
+    def body(place_ref, bound_ref, x_ref, gf_ref, gr_ref, p_ref, h_ref, mine_ref, twin_ref, dx_ref, gw_ref, cf_ref, cr_ref, ht_ref):
         def first(k, _):
             p = p_ref[k]
             sums = [jnp.zeros((8, 128), F32) for _ in range(taps + 1)]
@@ -532,7 +538,10 @@
 
         @pl.when(pl.program_id(0) == 0)
         def _():
-            ht_ref[...] = h_ref[...].T
+            ht = h_ref[...].T
+            for j in range(owners):
+                at = ((j % cores) ^ place_ref[2]) * fz + ((j // cores) ^ place_ref[1])
+                ht_ref[pl.ds(pl.multiple_of(at * rows, 16), rows), :] = ht[j * rows : (j + 1) * rows]
 
         lax.fori_loop(0, tiles, first, 0)
         for k in range(tiles):
@@ -545,9 +554,59 @@
                     v = v + p[taps - 1 - j : taps - j][None] * (shifted(ef, j, True) + shifted(er, j, False))
                 dx_ref[pl.ds(q * size * 8, size * 8), k * 128 : (k + 1) * 128] = v.reshape(size * 8, 128).astype(BF16)
         dx = dx_ref[...]
-        gx_ref[0] = dot(ht_ref[...], dx).astype(BF16).reshape(owners, rows, cols)
-        hg = dot_nt(dx, wx_ref[...].reshape(owners * rows, cols)) + dot_nt(
-            dz_ref[...], wz_ref[...].reshape(owners * rows, cols)
+        gx = dot(ht_ref[...], dx).astype(BF16).reshape(cores, fz, rows, cols)
+        mine_ref[:, 0] = gx[0]
+        twin_ref[:, 0] = gx[1]
+
+    tile_spec = pl.BlockSpec((octets, tiles, 8, 128), lambda b, p: (0, b, 0, 0))
+    part_spec = pl.BlockSpec((fz, 1, rows, cols), lambda b, p: (0, b ^ p[0], 0, 0))
+    part = jax.ShapeDtypeStruct((fz, blocks, rows, cols), BF16)
+    return pl.pallas_call(
+        body,
+        grid_spec=pltpu.PrefetchScalarGridSpec(
+            num_scalar_prefetch=1,
+            grid=(blocks,),
+            in_specs=[
+                SMEM,
+                tile_spec,
+                tile_spec,
+                tile_spec,
+                pl.BlockSpec((tiles, 8, 128), lambda b, p: (b, 0, 0)),
+                pl.BlockSpec(hidden.shape, lambda b, p: (0, 0)),
+            ],
+            out_specs=(
+                part_spec,
+                part_spec,
+                pl.BlockSpec((length, cols), lambda b, p: (0, b)),
+                pl.BlockSpec((tiles, taps + 1, 8, 128), lambda b, p: (b, 0, 0, 0)),
+            ),
+            scratch_shapes=[
+                pltpu.VMEM((octets, tiles, 8, 128), F32),
+                pltpu.VMEM((octets, tiles, 8, 128), F32),
+                pltpu.VMEM((width, length), BF16),
+            ],
+        ),
+        out_shape=(
+            part,
+            part,
+            jax.ShapeDtypeStruct((length, inner), BF16),
+            jax.ShapeDtypeStruct((inner // 128, taps + 1, 8, 128), F32),
+        ),
+        compiler_params=pltpu.CompilerParams(vmem_limit_bytes=56 << 20),
+        cost_estimate=pl.CostEstimate(
+            flops=2 * length * width * inner, bytes_accessed=30 << 20, transcendentals=2 * length * inner
+        ),
+        name="mixer_finish",
+    )(place, bound, x, grads[0], grads[1], params, hidden)
+
+
+def hidden_back(x_grad, z_grad, wx, wz, *, rows):
+    blocks, owners, cols = wx.shape[0], wx.shape[1], wx.shape[-1]
+    length, width = x_grad.shape[0], owners * rows
+
+    def body(dx_ref, dz_ref, wx_ref, wz_ref, hg_ref):
+        hg = dot_nt(dx_ref[...], wx_ref[...].reshape(width, cols)) + dot_nt(
+            dz_ref[...], wz_ref[...].reshape(width, cols)
         )
 
         @pl.when(pl.program_id(0) == 0)
@@ -558,45 +617,20 @@
         def _():
             hg_ref[...] = hg_ref[...] + hg
 
-    tile_spec = pl.BlockSpec((octets, tiles, 8, 128), lambda b: (0, b, 0, 0))
     w_spec = pl.BlockSpec((1, owners, rows, cols), lambda b: (b, 0, 0, 0))
-    z_spec = pl.BlockSpec((1, owners, 1, rows, cols), lambda b: (b, 0, 0, 0, 0)) if packed else w_spec
+    z_spec = pl.BlockSpec((1, owners, 1, rows, cols), lambda b: (b, 0, 0, 0, 0)) if wz.ndim == 5 else w_spec
     return pl.pallas_call(
         body,
         grid=(blocks,),
-        in_specs=[
-            SMEM,
-            tile_spec,
-            tile_spec,
-            tile_spec,
-            pl.BlockSpec((tiles, 8, 128), lambda b: (b, 0, 0)),
-            pl.BlockSpec(hidden.shape, lambda b: (0, 0)),
-            pl.BlockSpec((length, cols), lambda b: (0, b)),
-            w_spec,
-            z_spec,
-        ],
-        out_specs=(
-            pl.BlockSpec((1, owners, rows, cols), lambda b: (b, 0, 0, 0)),
-            pl.BlockSpec((length, width), lambda b: (0, 0)),
-            pl.BlockSpec((tiles, taps + 1, 8, 128), lambda b: (b, 0, 0, 0)),
-        ),
-        out_shape=(
-            jax.ShapeDtypeStruct((blocks, owners, total_rows, cols), BF16),
-            jax.ShapeDtypeStruct((length, width), F32),
-            jax.ShapeDtypeStruct((inner // 128, taps + 1, 8, 128), F32),
-        ),
-        scratch_shapes=[
-            pltpu.VMEM((octets, tiles, 8, 128), F32),
-            pltpu.VMEM((octets, tiles, 8, 128), F32),
-            pltpu.VMEM((length, cols), BF16),
-            pltpu.VMEM((width, length), BF16),
-        ],
-        compiler_params=pltpu.CompilerParams(vmem_limit_bytes=56 << 20),
+        in_specs=[pl.BlockSpec((length, cols), lambda b: (0, b))] * 2 + [w_spec, z_spec],
+        out_specs=pl.BlockSpec((length, width), lambda b: (0, 0)),
+        out_shape=jax.ShapeDtypeStruct((length, width), F32),
+        compiler_params=pltpu.CompilerParams(vmem_limit_bytes=40 << 20),
         cost_estimate=pl.CostEstimate(
-            flops=6 * length * width * inner, bytes_accessed=45 << 20, transcendentals=2 * length * inner
-        ),
-        name="mixer_finish",
-    )(bound, x, grads[0], grads[1], params, hidden, z_grad, wx, wz)
+            flops=4 * length * width * blocks * cols, bytes_accessed=24 << 20, transcendentals=0
+        ),
+        name="hidden_back",
+    )(x_grad, z_grad, wx, wz)
 
 
 def swap(v, axis, k):
@@ -608,7 +642,17 @@
 
 
 def gather_all(v):
-    return others(others(others(v, "dp"), "fz"), "core")
+    return others(others(others(v, "fz"), "dp"), "core")
+
+
+def added(v, axis, dim):
+    parts = [lax.index_in_dim(v, k, dim, keepdims=False) for k in range(lax.axis_size(axis))]
+    return sum((swap(p, axis, k) if k else p).astype(F32) for k, p in enumerate(parts))
+
+
+def relative(v, dim, me):
+    n = v.shape[dim]
+    return jnp.concatenate([lax.dynamic_slice_in_dim(v, me ^ k, 1, axis=dim) for k in range(n)], axis=dim)
 
 
 def per_device(
@@ -675,9 +719,9 @@
         jnp.zeros((ada_cols,), F32), ada_bias.astype(F32), (my_j * bias_cols,)
     )
     partial = jnp.dot(condition, ada_weight, preferred_element_type=F32) + bias_part[None, :]
-    partial = partial.reshape(cores, fz, dp, slots, ada_cols)
-    for axis, n in (("core", cores), ("fz", fz)):
-        partial = partial[0] + sum(swap(partial[k], axis, k) for k in range(1, n))
+    partial = partial.reshape(cores, dp, fz, slots, ada_cols)
+    partial = partial[0] + swap(partial[1], "core", 1)
+    partial = partial[:, 0] + sum(swap(partial[:, k], "fz", k) for k in range(1, fz))
     blocks = jnp.stack([partial[0]] + [swap(partial[k], "dp", k) for k in range(1, dp)])
     modulation = jnp.concatenate(
         [lax.dynamic_index_in_dim(blocks, my_dp ^ b, keepdims=False) for b in range(dp)], axis=1
@@ -758,46 +802,56 @@
         series_grad.append(got[0].reshape(tile_shape))
         small, da, skip_part = small + got[1], da + got[2], skip_part + got[3]
 
-    g_in, hidden_grad, conv_part = mixer_finish(
+    my_place = jnp.stack([lax.axis_index(n) for n in ALL]).astype(jnp.int32)
+    mine, twin, x_grad, conv_part = mixer_finish(
+        my_place,
         bound,
         x,
         series_grad,
         params,
         hidden,
-        z_grad,
-        g_x,
-        g_z,
         rows=rows,
-        total_rows=rows + tail,
+        cols=cols,
+        owners=fsdp,
         length=length,
         inner=inner,
         taps=taps,
         slots=slots,
     )
-    conv_rows = conv_part.sum(axis=2).transpose(1, 0, 2).reshape(taps + 1, inner)
     small_t = jnp.concatenate(
         [
-            small[: 128 + rank],
-            conv_rows,
-            small[128 + rank : 128 + rank + 1],
+            small[: 128 + rank + 1],
             skip_part.sum(axis=1).reshape(1, inner),
             da.reshape(states, inner) * decay,
-            jnp.zeros((256 - 128 - rank - taps - 3 - states, inner), F32),
+            jnp.zeros((256 - 128 - rank - 2 - states, inner), F32),
         ],
         axis=0,
     ).astype(BF16)
     small = small_t.T.reshape(dp, inner // dp, 256)
     small = jnp.concatenate([small[order.index(o)] for o in range(dp)], axis=0)
-    g_in = lax.dynamic_update_slice(g_in, small.reshape(dp, fsdp, tail, cols), (0, 0, rows, 0))
-    g_in, _ = lax.optimization_barrier((g_in, early))
-    got = scattered(g_in)
-    x_shard, small = got[:rows], got[rows:].reshape(own, 256).astype(F32)
-    got = lax.ppermute(jnp.where(lower, z_shard, x_shard), "dp", opposite)
-    grad_in_shard = jnp.where(
-        lower,
-        jnp.concatenate([x_shard, got], axis=1),
-        jnp.concatenate([got, z_shard], axis=1),
-    ).astype(F32)
+    cut = cols // 3 // 128 * 128
+    extra = own * 256 // (cols - cut)
+    small = small.reshape(dp, fz, cores, extra, cols - cut)
+    for dim, axis in enumerate(ALL):
+        small = relative(small, dim, lax.axis_index(axis))
+    small_twin = swap(small[:, :, 1], "core", 1)
+    other = swap(twin, "core", 1)
+
+    def both(k, first):
+        if first:
+            a, b = [v[k, :, :, :cut].astype(F32) for v in (mine, other)]
+            return a + b
+        a, b = [v[:, k, :, cut:].astype(F32) for v in (mine, other)]
+        return jnp.concatenate([a + b, small[k, :, 0].astype(F32) + small_twin[k].astype(F32)], axis=1)
+
+    sends = [[both(k, first).astype(BF16) for k in range(1, n)] for first, n in ((True, fz), (False, dp))]
+    sends, x_grad, _ = lax.optimization_barrier((sends, x_grad, early))
+    arrived = [[swap(v, axis, k + 1) for k, v in enumerate(send)] for send, axis in zip(sends, ("fz", "dp"))]
+    arrived[0][0], x_grad = lax.optimization_barrier((arrived[0][0], x_grad))
+    x_first, x_second = [
+        (both(0, first) + sum(v.astype(F32) for v in got)).astype(BF16) for first, got in zip((True, False), arrived)
+    ]
+    hidden_grad = hidden_back(x_grad, z_grad, g_x, g_z, rows=rows)
 
     normed_grad = hidden_grad * (1.0 + scale_mod)
     grad_tokens = cotangent + inv_std * (
@@ -807,12 +861,6 @@
     )
     token_mod_grad = jnp.concatenate([hidden_grad, hidden_grad * normed, gate_grad], axis=1)
     mod_low = lax.dot_general(picker, token_mod_grad, contract_rows, precision=high).astype(BF16)
-    mod_all = gather_all(mod_low).reshape(devices * slots, dp * ada_cols)
-    mod_cols = lax.dynamic_slice_in_dim(mod_all, my_dp * ada_cols, ada_cols, axis=1)
-    grad_ada_w = lax.dot_general(condition, mod_cols, contract_rows, preferred_element_type=F32)
-    grad_ada_b = jnp.sum(
-        lax.dynamic_slice_in_dim(mod_cols, my_j * bias_cols, bias_cols, axis=1).astype(F32), axis=0
-    )
     valid = (segment < slots).astype(F32)[:, None]
     sums = jnp.stack(
         [
@@ -821,8 +869,38 @@
             jnp.sum(valid) * width,
         ]
     )
-    sums = jnp.sum(gather_all(jnp.pad(sums, (0, 125))).reshape(devices, 128), axis=0)
-    out_sq, grad_sq, counted = sums[0], sums[1], sums[2]
+    pieces, rest = [], sums
+    for _ in range(3):
+        pieces.append(lax.optimization_barrier(rest.astype(BF16)))
+        rest = rest - pieces[-1].astype(F32)
+    pieces = jnp.pad(jnp.concatenate(pieces)[None, :], ((0, slots - 1), (0, 128 - 9)))
+    conv_rows = conv_part.sum(axis=2).transpose(1, 0, 2).reshape((taps + 1) * inner)
+    conv_cols = -(-conv_rows.shape[0] // (slots * 128)) * 128
+    conv_rows = jnp.pad(conv_rows, (0, slots * conv_cols - conv_rows.shape[0]))
+    mod_low = jnp.concatenate([mod_low, pieces, conv_rows.reshape(slots, conv_cols).astype(BF16)], axis=1)
+    mod_all = gather_all(mod_low).reshape(devices * slots, -1)
+    row = jnp.arange(devices * slots, dtype=jnp.int32) % slots
+    slot_rows = (row[None, :] == jnp.arange(slots, dtype=jnp.int32)[:, None]).astype(BF16)
+    conv_grad = jnp.dot(slot_rows, mod_all[:, dp * ada_cols + 128 :], preferred_element_type=F32)
+    conv_grad = conv_grad.reshape(-1)[: (taps + 1) * inner].reshape(taps + 1, dp, inner // dp)
+    conv_grad = jnp.stack([conv_grad[:, order.index(o)] for o in range(dp)], axis=1).reshape(taps + 1, inner)
+    conv_grad = lax.dynamic_slice_in_dim(conv_grad, (my_dp * fsdp + my_j) * own, own, axis=1).T
+    mod_cols = lax.dynamic_slice_in_dim(mod_all, my_dp * ada_cols, ada_cols, axis=1)
+    grad_ada_w = lax.dot_general(condition, mod_cols, contract_rows, preferred_element_type=F32)
+    grad_ada_b = jnp.sum(
+        lax.dynamic_slice_in_dim(mod_cols, my_j * bias_cols, bias_cols, axis=1).astype(F32), axis=0
+    )
+    sums = jnp.sum(mod_all[:, dp * ada_cols : dp * ada_cols + 9].astype(F32), axis=0)
+    out_sq, grad_sq, counted = [sums[i] + sums[i + 3] + sums[i + 6] for i in range(3)]
+    x_second = added(x_second, "fz", 0)
+    small = x_second[rows:].reshape(own, 256)
+    x_shard = jnp.concatenate([added(x_first, "dp", 0), x_second[:rows]], axis=1).astype(BF16)
+    got = lax.ppermute(jnp.where(lower, z_shard, x_shard), "dp", opposite)
+    grad_in_shard = jnp.where(
+        lower,
+        jnp.concatenate([x_shard, got], axis=1),
+        jnp.concatenate([got, z_shard], axis=1),
+    ).astype(F32)
     at = 128 + rank
     return (
         layer_out,
@@ -830,13 +908,13 @@
         grad_ada_w,
         grad_ada_b,
         grad_in_shard,
-        small[:, at : at + taps],
-        small[:, at + taps],
+        conv_grad[:, :taps],
+        conv_grad[:, taps],
         small[:, :128],
         small[:, 128:at],
-        small[:, at + taps + 1],
-        small[:, at + taps + 3 : at + taps + 3 + states],
-        small[:, at + taps + 2],
+        small[:, at],
+        small[:, at + 2 : at + 2 + states],
+        small[:, at + 1],
         out_shard.astype(F32),
         jnp.sqrt(out_sq / counted),
         jnp.sqrt(grad_sq / counted),

time: 716 us -> 664 us (0.927)
  Pallas kernels: 389 us -> 345 us
  waiting for transfers between devices: 174 us -> 144 us
  other arithmetic: 36 us -> 49.9 us
    reduce_scatter x2 -> x1, waiting for transfers between devices: 77.9 us -> 0.01 us  [scattered(): lax.psum_scatter(v.reshape(-1, v.shape[-1]), ALL, scatter_dimension=0, ti...]
    ppermute x28 -> x35, waiting for transfers between devices: 38 us -> 64.8 us  [swap(): lax.ppermute(v, axis, [(i, i ^ k) for i in range(lax.axis_size(axis))])]
    pallas_call x2, Pallas kernels: 208 us -> 183 us  [mixer_backward(): pl.pallas_call(body, out_shape=(jax.ShapeDtypeStruct((rows, 128), F32), j...]
    pallas_call x1, Pallas kernels: 98.5 us -> 76.4 us  [mixer_forward(): pl.pallas_call(body, out_shape=(big,) * 5 + (jax.ShapeDtypeStruct((2, tok...]
    all_gather x1, waiting for transfers between devices: 5.65 us -> 27.6 us  [per_device(): lax.all_gather(later, ALL, axis=0, tiled=True)]
    ppermute x28 -> x35, starting transfers between devices: 32.3 us -> 36.6 us  [swap(): lax.ppermute(v, axis, [(i, i ^ k) for i in range(lax.axis_size(axis))])]
    pallas_call x1 -> x2, Pallas kernels: 32.7 us -> 36.1 us  [the longest x1 23.6 us: mixer_finish(): pl.pallas_call(body, grid_spec=pltpu.PrefetchScalarGridSpec(num_scalar_pr...]
  transfers between devices with their start and end apart: 34 -> 40, of which waited for: 22 -> 22; matrix products, arithmetic and copies ran while one was open for 10% -> 12% of each run, Pallas kernels for 49% -> 46%
where the time goes in v3:
time: 664 us; the launch traced here: 657 us
  Pallas kernels  345 us (52%)
  waiting for transfers between devices  144 us (22%)
  other arithmetic  49.9 us (8%)
  starting transfers between devices  41.7 us (6%)
  local copies, waits for them, and re-layouts  41.3 us (6%)
  between operations  23.9 us (4%)
  matrix products  10.3 us (2%)
    pallas_call x2, Pallas kernels, mixer_backward(): pl.pallas_call(body, out_shape=(jax.ShapeDtypeStruct((rows, 128), F32), j...  183 us
    pallas_call x1, Pallas kernels, mixer_forward(): pl.pallas_call(body, out_shape=(big,) * 5 + (jax.ShapeDtypeStruct((2, tok...  76.4 us
    ppermute x35, waiting for transfers between devices, swap(): lax.ppermute(v, axis, [(i, i ^ k) for i in range(lax.axis_size(axis))])  64.8 us
    all_gather x1, waiting for transfers between devices, per_device(): lax.all_gather(jnp.concatenate([x_cols, packed.reshape(tail, cols)], axis...  49.8 us
    pallas_call x1, Pallas kernels, mixer_middle(): pl.pallas_call(body, grid_spec=pltpu.PrefetchScalarGridSpec(num_scalar_pr...  42.8 us
    ppermute x35, starting transfers between devices, swap(): lax.ppermute(v, axis, [(i, i ^ k) for i in range(lax.axis_size(axis))])  36.6 us
    all_gather x1, waiting for transfers between devices, per_device(): lax.all_gather(later, ALL, axis=0, tiled=True)  27.6 us
    pallas_call x1, Pallas kernels, mixer_finish(): pl.pallas_call(body, grid_spec=pltpu.PrefetchScalarGridSpec(num_scalar_pr...  23.6 us
  transfers between devices with their start and end apart: 40, of which 22 were waited for; matrix products, arithmetic and copies ran while one was open for 12% of the time, Pallas kernels for 46%

profile of v3, /device:TPU:0, one launch (start us, length us, event | category | flops | bytes accessed | tf_op | source)
XLA Modules:
  0.0 656.7 jit_solution(14831049457161728692)
XLA Ops:
  8.5 3.0 collective-permute-start.14
  26.8 3.5 collective-permute-done.2
  42.3 4.1 collective-permute-start.9
  57.1 3.0 fusion.36
  63.8 49.8 %all-gather.3.cloned.1.call-done = bf16[7168,768]{1,0:T(8,128)(2,1)} async-done(((bf16[224,768]{1,0:T(8,128)(2,1)}), bf16[7168,768]{1,0:T(8,128)(2,1)}) %all-gather.3.cloned.1.call-update) | async-done | bytes 11010064 | tf_op jit(solution)/shard_map/all_gather | solution.py:710
  126.0 7.1 %project.1.x_ref = f32[48,24,8,128]{3,2,1,0:T(8,128)S(1)} custom-call(bf16[384,1536]{1,0:T(8,128)(2,1)S(1)} %get-tuple-element.49.h_ref, bf16[4,8,224,768]{3,2,1,0:T(8,128)(2,1)} %bitcast.236), custom_call_target="tpu_custom_call" | custom-call | flops 3623878656 | bytes 14155776 | tf_op jit(solution)/shard_map/project/pallas_call | solution.py:110
  136.4 76.4 %mixer_forward.1 = (f32[9216,128]{1,0:T(8,128)}, f32[9216,128]{1,0:T(8,128)}, f32[9216,128]{1,0:T(8,128)}, f32[9216,128]{1,0:T(8,128)}, f32[9216,128]{1,0:T(8,128)}, /*index=5*/f32[2,384,128]{2,1,0:T(8,128)}) custom-call(f32[2,48]{1,0:T(2,128)} %pad_maximum_fusion.11.keep_ref, f32[4]{0:T(128)} %slice.332.bound_ref, f32[48,24,8,128]{3,2,1,0:T(8,128)} %copy-done.2, ...), custom_call_target="tpu_custom_call" | custom-call | flops 3019898880 | bytes 28311552 | tf_op jit(solution)/shard_map/mixer_forward/pallas_call | solution.py:203
  212.8 27.6 %all-gather.5.cloned.1.call-done = bf16[64,192,768]{2,1,0:T(8,128)(2,1)} async-done(((bf16[2,192,768]{2,1,0:T(8,128)(2,1)}), bf16[64,192,768]{2,1,0:T(8,128)(2,1)}) %all-gather.5.cloned.1.call-update) | async-done | bytes 18874384 | tf_op jit(solution)/shard_map/all_gather | solution.py:745
  240.4 42.8 %mixer_middle.1 = (f32[48,24,8,128]{3,2,1,0:T(8,128)}, bf16[384,3072]{1,0:T(8,128)(2,1)}, f32[4,384,384]{2,1,0:T(8,128)}, bf16[4,8,2,192,768]{4,3,2,1,0:T(8,128)(2,1)}) custom-call(s32[4]{0:T(128)} %constant.105.clone.place_ref, bf16[384,1536]{1,0:T(8,128)(2,1)} %copy-done.3, bf16[4,8,2,192,768]{4,3,2,1,0:T(8,128)(2,1)} %bitcast.239, ...), custom_call_target="tpu_custom_call" | custom-call | flops 18119393280 | bytes 62914560 | tf_op jit(solution)/shard_map/mixer_middle/pallas_call | solution.py:314
  285.0 92.0 %mixer_backward.3 = (f32[9216,128]{1,0:T(8,128)}, f32[256,3072]{1,0:T(8,128)}, f32[384,128]{1,0:T(8,128)}, f32[24,8,128]{2,1,0:T(8,128)}) custom-call(f32[48]{0:T(128)} %copy-done.37, f32[384,128]{1,0:T(8,128)} %get-tuple-element.135.proj_ref, f32[9216,128]{1,0:T(8,128)} %get-tuple-element.59.d_ref, f32[9216,128]{1,0:T(8,128)} %get-tuple-element.60.u_ref, ...), custom_call_target="tpu_custom_call" | custom-call | flops 3019898880 | bytes 23592960 | tf_op jit(solution)/shard_map/mixer_backward/pallas_call | solution.py:483
  377.0 91.1 %mixer_backward.2 = (f32[9216,128]{1,0:T(8,128)}, f32[256,3072]{1,0:T(8,128)}, f32[384,128]{1,0:T(8,128)}, f32[24,8,128]{2,1,0:T(8,128)}) custom-call(f32[48]{0:T(128)} %copy-done.36, f32[384,128]{1,0:T(8,128)} %get-tuple-element.136.proj_ref, f32[9216,128]{1,0:T(8,128)} %get-tuple-element.55.d_ref, f32[9216,128]{1,0:T(8,128)} %get-tuple-element.56.u_ref, ...), custom_call_target="tpu_custom_call" | custom-call | flops 3019898880 | bytes 23592960 | tf_op jit(solution)/shard_map/mixer_backward/pallas_call | solution.py:483
  468.2 23.6 %mixer_finish.1 = (bf16[4,4,192,768]{3,2,1,0:T(8,128)(2,1)}, bf16[4,4,192,768]{3,2,1,0:T(8,128)(2,1)}, bf16[384,3072]{1,0:T(8,128)(2,1)}, f32[24,5,8,128]{3,2,1,0:T(8,128)}) custom-call(s32[3]{0:T(128)} %pad_add_fusion.2.place_ref, f32[4]{0:T(128)} %slice.332.bound_ref, f32[48,24,8,128]{3,2,1,0:T(8,128)} %copy-done.2, f32[48,24,8,128]{3,2,1,0:T(8,128)} %bitcast.246, ...), custom_call_target="tpu_custom_call" | custom-call | flops 3623878656 | bytes 31457280 | tf_op jit(solution)/shard_map/mixer_finish/pallas_call | solution.py:564
  496.1 3.0 fusion.9
  506.4 3.5 copy.151
  511.5 3.1 fusion.20
  522.7 3.4 collective-permute-start.26
  528.2 9.2 %collective-permute-done.17 = bf16[4,192,256]{2,1,0:T(8,128)(2,1)S(1)} collective-permute-done((bf16[4,192,256]{2,1,0:T(8,128)(2,1)}, bf16[4,192,256]{2,1,0:T(8,128)(2,1)S(1)}, u32[]{:S(2)}, u32[]{:S(2)}) %collective-permute-start.17) | collective-permute-done | bytes 393248 | tf_op jit(solution)/shard_map/ppermute | solution.py:637
  537.4 12.4 %hidden_back.1 = f32[384,1536]{1,0:T(8,128)S(1)} custom-call(bf16[384,3072]{1,0:T(8,128)(2,1)S(1)} %copy-done.5, bf16[384,3072]{1,0:T(8,128)(2,1)S(1)} %copy-done.4, bf16[4,8,224,768]{3,2,1,0:T(8,128)(2,1)} %bitcast.237, bf16[4,8,2,192,768]{4,3,2,1,0:T(8,128)(2,1)} %bitcast.241), custom_call_target="tpu_custom_call" | custom-call | flops 7247757312 | bytes 25165824 | tf_op jit(solution)/shard_map/hidden_back/pallas_call | solution.py:622
  552.9 4.5 multiply_reduce_fusion.1
  562.8 3.2 collective-permute-start.20
  571.7 21.2 %collective-permute-done.27 = bf16[192,256]{1,0:T(8,128)(2,1)S(1)} collective-permute-done((bf16[192,256]{1,0:T(8,128)(2,1)S(1)}, bf16[192,256]{1,0:T(8,128)(2,1)S(1)}, u32[]{:S(2)}, u32[]{:S(2)}) %collective-permute-start.27) | collective-permute-done | bytes 98336 | tf_op jit(solution)/shard_map/ppermute | solution.py:637
  595.2 4.2 collective-permute-done.29
  606.4 4.6 collective-permute-done.22
  613.0 5.9 collective-permute-done.34
  (292 shorter events, 130.6 us)
Async XLA Ops:
  7.2 106.4 %all-gather.3.cloned.1.call-start = ((), (), s32[]{:S(2)}) async-start(), calls=%async_computation.1 | async-start | bytes 11354112 | tf_op jit(solution)/shard_map/all_gather | solution.py:710
  8.5 10.0 %collective-permute-start.14 = (bf16[192,768]{1,0:T(8,128)(2,1)S(1)}, bf16[192,768]{1,0:T(8,128)(2,1)S(1)}, u32[]{:S(2)}, u32[]{:S(2)}) collective-permute-start(bf16[192,768]{1,0:T(8,128)(2,1)S(1)} %broadcast_select_fusion.2), channel_id=1, source_target_pairs={{0,16},{8,24},{16,0},{24,8},{1,17},{9,25},{17,1},{25,9},{2,18},{10... | collective-permute-start | bytes 884744 | tf_op jit(solution)/shard_map/ppermute | solution.py:693
  20.4 220.0 %all-gather.5.cloned.1.call-start = ((), (), s32[]{:S(2)}) async-start(), calls=%async_computation.2 | async-start | bytes 19464192 | tf_op jit(solution)/shard_map/all_gather | solution.py:745
  41.9 7.0 %collective-permute-start.10 = (f32[4,4,1152]{2,1,0:T(4,128)S(1)}, f32[4,4,1152]{2,1,0:T(4,128)S(1)}, u32[]{:S(2)}, u32[]{:S(2)}) collective-permute-start(f32[4,4,1152]{2,1,0:T(4,128)S(1)} %get-tuple-element.139), channel_id=1, source_target_pairs={{0,6},{2,4},{4,2},{6,0},{1,7},{3,5},{5,3},{7,1},{8,14},{10,12},{12... | collective-permute-start | bytes 221192 | tf_op jit(solution)/shard_map/ppermute | solution.py:637
  42.3 9.0 %collective-permute-start.9 = (f32[4,4,1152]{2,1,0:T(4,128)S(1)}, f32[4,4,1152]{2,1,0:T(4,128)S(1)}, u32[]{:S(2)}, u32[]{:S(2)}) collective-permute-start(f32[4,4,1152]{2,1,0:T(4,128)S(1)} %get-tuple-element.137), channel_id=1, source_target_pairs={{0,4},{2,6},{4,0},{6,2},{1,5},{3,7},{5,1},{7,3},{8,12},{10,14},{12... | collective-permute-start | bytes 221192 | tf_op jit(solution)/shard_map/ppermute | solution.py:637
  113.7 406.3 %reduce-scatter.2.cloned.1.call-start = ((), (), s32[]{:S(2)}) async-start(), calls=%async_computation.3 | async-start | bytes 19464192 | tf_op jit(solution)/shard_map/reduce_scatter | solution.py:787
  491.8 19.7 %collective-permute-start.15 = (bf16[4,4,192,768]{3,2,1,0:T(8,128)(2,1)}, bf16[4,4,192,768]{3,2,1,0:T(8,128)(2,1)}, u32[]{:S(2)}, u32[]{:S(2)}) collective-permute-start(bf16[4,4,192,768]{3,2,1,0:T(8,128)(2,1)} %get-tuple-element.63), channel_id=1, source_target_pairs={{0,1},{1,0},{2,3},{3,2},{4,5},{5,4},{6,7},{7,6},{8,9},{9,8},{10,11... | collective-permute-start | bytes 14155784 | tf_op jit(solution)/shard_map/ppermute | solution.py:637
  519.9 17.4 %collective-permute-start.17 = (bf16[4,192,256]{2,1,0:T(8,128)(2,1)}, bf16[4,192,256]{2,1,0:T(8,128)(2,1)S(1)}, u32[]{:S(2)}, u32[]{:S(2)}) collective-permute-start(bf16[4,192,256]{2,1,0:T(8,128)(2,1)} %get-tuple-element.72), channel_id=1, source_target_pairs={{0,2},{2,0},{4,6},{6,4},{1,3},{3,1},{5,7},{7,5},{8,10},{10,8},{12,... | collective-permute-start | bytes 1179656 | tf_op jit(solution)/shard_map/ppermute | solution.py:637
  521.8 39.8 %collective-permute-start.25 = (bf16[4,192,256]{2,1,0:T(8,128)(2,1)}, bf16[4,192,256]{2,1,0:T(8,128)(2,1)S(1)}, u32[]{:S(2)}, u32[]{:S(2)}) collective-permute-start(bf16[4,192,256]{2,1,0:T(8,128)(2,1)} %get-tuple-element.78), channel_id=1, source_target_pairs={{0,4},{2,6},{4,0},{6,2},{1,5},{3,7},{5,1},{7,3},{8,12},{10,14},{12... | collective-permute-start | bytes 1179656 | tf_op jit(solution)/shard_map/ppermute | solution.py:637
  522.7 40.1 %collective-permute-start.26 = (bf16[4,192,256]{2,1,0:T(8,128)(2,1)}, bf16[4,192,256]{2,1,0:T(8,128)(2,1)}, u32[]{:S(2)}, u32[]{:S(2)}) collective-permute-start(bf16[4,192,256]{2,1,0:T(8,128)(2,1)} %get-tuple-element.79), channel_id=1, source_target_pairs={{0,6},{2,4},{4,2},{6,0},{1,7},{3,5},{5,3},{7,1},{8,14},{10,12},{12... | collective-permute-start | bytes 1179656 | tf_op jit(solution)/shard_map/ppermute | solution.py:637
  526.1 74.0 %collective-permute-start.30 = (bf16[4,240,512]{2,1,0:T(8,128)(2,1)}, bf16[4,240,512]{2,1,0:T(8,128)(2,1)S(1)}, u32[]{:S(2)}, u32[]{:S(2)}) collective-permute-start(bf16[4,240,512]{2,1,0:T(8,128)(2,1)} %get-tuple-element.80), channel_id=1, source_target_pairs={{0,8},{8,0},{16,24},{24,16},{1,9},{9,1},{17,25},{25,17},{2,10},{10... | collective-permute-start | bytes 2949128 | tf_op jit(solution)/shard_map/ppermute | solution.py:637
  527.0 74.3 %collective-permute-start.31 = (bf16[4,240,512]{2,1,0:T(8,128)(2,1)}, bf16[4,240,512]{2,1,0:T(8,128)(2,1)S(1)}, u32[]{:S(2)}, u32[]{:S(2)}) collective-permute-start(bf16[4,240,512]{2,1,0:T(8,128)(2,1)} %get-tuple-element.81), channel_id=1, source_target_pairs={{0,16},{8,24},{16,0},{24,8},{1,17},{9,25},{17,1},{25,9},{2,18},{10... | collective-permute-start | bytes 2949128 | tf_op jit(solution)/shard_map/ppermute | solution.py:637
  561.6 8.2 %collective-permute-start.19 = (bf16[4,8576]{1,0:T(4,128)(2,1)S(1)}, bf16[4,8576]{1,0:T(4,128)(2,1)S(1)}, u32[]{:S(2)}, u32[]{:S(2)}) collective-permute-start(bf16[4,8576]{1,0:T(4,128)(2,1)S(1)} %fusion.57), channel_id=1, source_target_pairs={{0,4},{2,6},{4,0},{6,2},{1,5},{3,7},{5,1},{7,3},{8,12},{10,14},{12... | collective-permute-start | bytes 205832 | tf_op jit(solution)/shard_map/ppermute | solution.py:637
  562.8 8.4 %collective-permute-start.20 = (bf16[4,8576]{1,0:T(4,128)(2,1)S(1)}, bf16[4,8576]{1,0:T(4,128)(2,1)S(1)}, u32[]{:S(2)}, u32[]{:S(2)}) collective-permute-start(bf16[4,8576]{1,0:T(4,128)(2,1)S(1)} %fusion.57), channel_id=1, source_target_pairs={{0,6},{2,4},{4,2},{6,0},{1,7},{3,5},{5,3},{7,1},{8,14},{10,12},{12... | collective-permute-start | bytes 205832 | tf_op jit(solution)/shard_map/ppermute | solution.py:637
  567.5 33.8 %collective-permute-start.32 = (bf16[4,240,512]{2,1,0:T(8,128)(2,1)S(1)}, bf16[4,240,512]{2,1,0:T(8,128)(2,1)S(1)}, u32[]{:S(2)}, u32[]{:S(2)}) collective-permute-start(bf16[4,240,512]{2,1,0:T(8,128)(2,1)S(1)} %copy-done.17), channel_id=1, source_target_pairs={{0,24},{8,16},{16,8},{24,0},{1,25},{9,17},{17,9},{25,1},{2,26},{10... | collective-permute-start | bytes 2949128 | tf_op jit(solution)/shard_map/ppermute | solution.py:637
  569.7 23.2 %collective-permute-start.27 = (bf16[192,256]{1,0:T(8,128)(2,1)S(1)}, bf16[192,256]{1,0:T(8,128)(2,1)S(1)}, u32[]{:S(2)}, u32[]{:S(2)}) collective-permute-start(bf16[192,256]{1,0:T(8,128)(2,1)S(1)} %get-tuple-element.132), channel_id=1, source_target_pairs={{0,8},{8,0},{16,24},{24,16},{1,9},{9,1},{17,25},{25,17},{2,10},{10... | collective-permute-start | bytes 294920 | tf_op jit(solution)/shard_map/ppermute | solution.py:637
  571.1 23.4 %collective-permute-start.28 = (bf16[192,256]{1,0:T(8,128)(2,1)S(1)}, bf16[192,256]{1,0:T(8,128)(2,1)S(1)}, u32[]{:S(2)}, u32[]{:S(2)}) collective-permute-start(bf16[192,256]{1,0:T(8,128)(2,1)S(1)} %get-tuple-element.134), channel_id=1, source_target_pairs={{0,16},{8,24},{16,0},{24,8},{1,17},{9,25},{17,1},{25,9},{2,18},{10... | collective-permute-start | bytes 294920 | tf_op jit(solution)/shard_map/ppermute | solution.py:637
  594.5 9.9 %collective-permute-start.21 = (bf16[4,4,8576]{2,1,0:T(4,128)(2,1)S(1)}, bf16[4,4,8576]{2,1,0:T(4,128)(2,1)S(1)}, u32[]{:S(2)}, u32[]{:S(2)}) collective-permute-start(bf16[4,4,8576]{2,1,0:T(4,128)(2,1)S(1)} %pad_maximum_fusion.9), channel_id=1, source_target_pairs={{0,8},{8,0},{16,24},{24,16},{1,9},{9,1},{17,25},{25,17},{2,10},{10... | collective-permute-start | bytes 823304 | tf_op jit(solution)/shard_map/ppermute | solution.py:637
  599.5 11.5 %collective-permute-start.22 = (bf16[4,4,8576]{2,1,0:T(4,128)(2,1)S(1)}, bf16[4,4,8576]{2,1,0:T(4,128)(2,1)S(1)}, u32[]{:S(2)}, u32[]{:S(2)}) collective-permute-start(bf16[4,4,8576]{2,1,0:T(4,128)(2,1)S(1)} %pad_maximum_fusion.9), channel_id=1, source_target_pairs={{0,16},{8,24},{16,0},{24,8},{1,17},{9,25},{17,1},{25,9},{2,18},{10... | collective-permute-start | bytes 823304 | tf_op jit(solution)/shard_map/ppermute | solution.py:637
  600.1 10.9 %collective-permute-start.23 = (bf16[4,4,8576]{2,1,0:T(4,128)(2,1)S(1)}, bf16[4,4,8576]{2,1,0:T(4,128)(2,1)S(1)}, u32[]{:S(2)}, u32[]{:S(2)}) collective-permute-start(bf16[4,4,8576]{2,1,0:T(4,128)(2,1)S(1)} %pad_maximum_fusion.9), channel_id=1, source_target_pairs={{0,24},{8,16},{16,8},{24,0},{1,25},{9,17},{17,9},{25,1},{2,26},{10... | collective-permute-start | bytes 823304 | tf_op jit(solution)/shard_map/ppermute | solution.py:637
  601.9 11.1 %collective-permute-start.33 = (bf16[240,512]{1,0:T(8,128)(2,1)S(1)}, bf16[240,512]{1,0:T(8,128)(2,1)S(1)}, u32[]{:S(2)}, u32[]{:S(2)}) collective-permute-start(bf16[240,512]{1,0:T(8,128)(2,1)S(1)} %get-tuple-element.121), channel_id=1, source_target_pairs={{0,2},{2,0},{4,6},{6,4},{1,3},{3,1},{5,7},{7,5},{8,10},{10,8},{12,... | collective-permute-start | bytes 737288 | tf_op jit(solution)/shard_map/ppermute | solution.py:637
  602.0 16.9 %collective-permute-start.34 = (bf16[240,512]{1,0:T(8,128)(2,1)S(1)}, bf16[240,512]{1,0:T(8,128)(2,1)S(1)}, u32[]{:S(2)}, u32[]{:S(2)}) collective-permute-start(bf16[240,512]{1,0:T(8,128)(2,1)S(1)} %get-tuple-element.123), channel_id=1, source_target_pairs={{0,4},{2,6},{4,0},{6,2},{1,5},{3,7},{5,1},{7,3},{8,12},{10,14},{12... | collective-permute-start | bytes 737288 | tf_op jit(solution)/shard_map/ppermute | solution.py:637
  604.4 14.5 %collective-permute-start.35 = (bf16[240,512]{1,0:T(8,128)(2,1)S(1)}, bf16[240,512]{1,0:T(8,128)(2,1)S(1)}, u32[]{:S(2)}, u32[]{:S(2)}) collective-permute-start(bf16[240,512]{1,0:T(8,128)(2,1)S(1)} %get-tuple-element.122), channel_id=1, source_target_pairs={{0,6},{2,4},{4,2},{6,0},{1,7},{3,5},{5,3},{7,1},{8,14},{10,12},{12... | collective-permute-start | bytes 737288 | tf_op jit(solution)/shard_map/ppermute | solution.py:637
  613.0 14.1 %collective-permute-start.24 = (bf16[4,4,4,8576]{3,2,1,0:T(4,128)(2,1)}, bf16[4,4,4,8576]{3,2,1,0:T(4,128)(2,1)S(1)}, u32[]{:S(2)}, u32[]{:S(2)}) collective-permute-start(bf16[4,4,4,8576]{3,2,1,0:T(4,128)(2,1)} %pad_maximum_fusion.3), channel_id=1, source_target_pairs={{0,1},{1,0},{2,3},{3,2},{4,5},{5,4},{6,7},{7,6},{8,9},{9,8},{10,11... | collective-permute-start | bytes 3293192 | tf_op jit(solution)/shard_map/ppermute | solution.py:637
  (56 other events, 538.3 us)
Sparse Core Ops, SparseCore 0:
  20.6 93.0 all-gather.2
  117.2 123.1 all-gather.4
  283.4 204.8 reduce-scatter.1

commit v4 on v3

--- a/solution.py
+++ b/solution.py
@@ -446,14 +446,16 @@
             for n in range(GROUP):
                 for c in range(blocks):
                     da_ref[pl.ds((ng * GROUP + n) * tiles + c * 8, 8), :] = das[n * blocks + c]
-            lane = lax.broadcasted_iota(jnp.int32, (128, 128), 1)
+            lane = lax.broadcasted_iota(jnp.int32, (256, 128), 1)
+            total = cols_ref[...]
             for q in range(2 * GROUP):
                 col = rank + (q // GROUP) * states + ng * GROUP + q % GROUP
                 one = jnp.where(lane == col, 1.0, 0.0).astype(BF16)
                 v = r_ref[pl.ds(q, tokens, stride=8), :]
                 high_part = v.astype(BF16)
                 low_part = (v - high_part.astype(F32)).astype(BF16)
-                cols_ref[...] += dot(high_part, one) + dot(low_part, one)
+                total = total + dot(jnp.concatenate([high_part, low_part], axis=1), one)
+            cols_ref[...] = total
         shape4 = (octets, tiles, 8, 128)
         d4, u4, g4, ddu4, dd4 = [r.reshape(shape4) for r in (d_ref, u_ref, g_ref, ddu_ref, dd_ref)]
         lanes = lax.broadcasted_iota(jnp.int32, (tokens, 128), 1)
@@ -555,12 +557,12 @@
                 dx_ref[pl.ds(q * size * 8, size * 8), k * 128 : (k + 1) * 128] = v.reshape(size * 8, 128).astype(BF16)
         dx = dx_ref[...]
         gx = dot(ht_ref[...], dx).astype(BF16).reshape(cores, fz, rows, cols)
-        mine_ref[:, 0] = gx[0]
-        twin_ref[:, 0] = gx[1]
+        mine_ref[0] = gx[0]
+        twin_ref[0] = gx[1]
 
     tile_spec = pl.BlockSpec((octets, tiles, 8, 128), lambda b, p: (0, b, 0, 0))
-    part_spec = pl.BlockSpec((fz, 1, rows, cols), lambda b, p: (0, b ^ p[0], 0, 0))
-    part = jax.ShapeDtypeStruct((fz, blocks, rows, cols), BF16)
+    part_spec = pl.BlockSpec((1, fz, rows, cols), lambda b, p: (b ^ p[0], 0, 0, 0))
+    part = jax.ShapeDtypeStruct((blocks, fz, rows, cols), BF16)
     return pl.pallas_call(
         body,
         grid_spec=pltpu.PrefetchScalarGridSpec(
@@ -829,28 +831,21 @@
     ).astype(BF16)
     small = small_t.T.reshape(dp, inner // dp, 256)
     small = jnp.concatenate([small[order.index(o)] for o in range(dp)], axis=0)
-    cut = cols // 3 // 128 * 128
-    extra = own * 256 // (cols - cut)
-    small = small.reshape(dp, fz, cores, extra, cols - cut)
+    small = small.reshape(dp, fz, cores, tail, cols)
     for dim, axis in enumerate(ALL):
         small = relative(small, dim, lax.axis_index(axis))
     small_twin = swap(small[:, :, 1], "core", 1)
     other = swap(twin, "core", 1)
 
-    def both(k, first):
-        if first:
-            a, b = [v[k, :, :, :cut].astype(F32) for v in (mine, other)]
-            return a + b
-        a, b = [v[:, k, :, cut:].astype(F32) for v in (mine, other)]
-        return jnp.concatenate([a + b, small[k, :, 0].astype(F32) + small_twin[k].astype(F32)], axis=1)
-
-    sends = [[both(k, first).astype(BF16) for k in range(1, n)] for first, n in ((True, fz), (False, dp))]
+    def both(k):
+        a = mine[k].astype(F32) + other[k].astype(F32)
+        return jnp.concatenate([a, small[k, :, 0].astype(F32) + small_twin[k].astype(F32)], axis=1)
+
+    sends = [both(k).astype(BF16) for k in range(1, dp)]
     sends, x_grad, _ = lax.optimization_barrier((sends, x_grad, early))
-    arrived = [[swap(v, axis, k + 1) for k, v in enumerate(send)] for send, axis in zip(sends, ("fz", "dp"))]
-    arrived[0][0], x_grad = lax.optimization_barrier((arrived[0][0], x_grad))
-    x_first, x_second = [
-        (both(0, first) + sum(v.astype(F32) for v in got)).astype(BF16) for first, got in zip((True, False), arrived)
-    ]
+    arrived = [swap(v, "dp", k + 1) for k, v in enumerate(sends)]
+    arrived[0], x_grad = lax.optimization_barrier((arrived[0], x_grad))
+    half_way = (both(0) + sum(v.astype(F32) for v in arrived)).astype(BF16)
     hidden_grad = hidden_back(x_grad, z_grad, g_x, g_z, rows=rows)
 
     normed_grad = hidden_grad * (1.0 + scale_mod)
@@ -878,23 +873,43 @@
     conv_cols = -(-conv_rows.shape[0] // (slots * 128)) * 128
     conv_rows = jnp.pad(conv_rows, (0, slots * conv_cols - conv_rows.shape[0]))
     mod_low = jnp.concatenate([mod_low, pieces, conv_rows.reshape(slots, conv_cols).astype(BF16)], axis=1)
-    mod_all = gather_all(mod_low).reshape(devices * slots, -1)
-    row = jnp.arange(devices * slots, dtype=jnp.int32) % slots
-    slot_rows = (row[None, :] == jnp.arange(slots, dtype=jnp.int32)[:, None]).astype(BF16)
-    conv_grad = jnp.dot(slot_rows, mod_all[:, dp * ada_cols + 128 :], preferred_element_type=F32)
-    conv_grad = conv_grad.reshape(-1)[: (taps + 1) * inner].reshape(taps + 1, dp, inner // dp)
-    conv_grad = jnp.stack([conv_grad[:, order.index(o)] for o in range(dp)], axis=1).reshape(taps + 1, inner)
-    conv_grad = lax.dynamic_slice_in_dim(conv_grad, (my_dp * fsdp + my_j) * own, own, axis=1).T
-    mod_cols = lax.dynamic_slice_in_dim(mod_all, my_dp * ada_cols, ada_cols, axis=1)
-    grad_ada_w = lax.dot_general(condition, mod_cols, contract_rows, preferred_element_type=F32)
-    grad_ada_b = jnp.sum(
-        lax.dynamic_slice_in_dim(mod_cols, my_j * bias_cols, bias_cols, axis=1).astype(F32), axis=0
-    )
-    sums = jnp.sum(mod_all[:, dp * ada_cols : dp * ada_cols + 9].astype(F32), axis=0)
+    base = dp * ada_cols
+    near = others(mod_low, "fz")
+    conv_sum = near[:, :, base + 128 :].astype(F32).sum(axis=0).reshape(-1)[: (taps + 1) * inner]
+    conv_sum = conv_sum.reshape(taps + 1, dp, inner // dp)
+    conv_sum = jnp.stack([conv_sum[:, order.index(o)] for o in range(dp)]).reshape(dp, -1)
+    conv_cols = -(-conv_sum.shape[1] // (fz * slots * 128)) * 128
+    conv_sum = jnp.pad(conv_sum, ((0, 0), (0, fz * slots * conv_cols - conv_sum.shape[1]))).astype(BF16)
+    conv_sum = conv_sum.reshape(dp, fz, slots, conv_cols)
+
+    def part(k):
+        return jnp.concatenate(
+            [
+                lax.dynamic_slice_in_dim(near, (my_dp ^ k) * ada_cols, ada_cols, axis=2),
+                near[:, :, base : base + 128],
+                lax.dynamic_index_in_dim(conv_sum, my_dp ^ k, keepdims=False),
+            ],
+            axis=2,
+        )
+
+    near = jnp.stack([part(0)] + [swap(part(k), "dp", k) for k in range(1, dp)])
+    near = near.reshape(dp * fz * slots, -1)
+    sides = (near, swap(near, "core", 1))
+    conditions = condition.reshape(cores, dp * fz * slots, ada_rows)
+    grad_ada_w, grad_ada_b, sums, conv_grad = 0.0, 0.0, 0.0, 0.0
+    for side, cond in zip(sides, conditions):
+        mod_cols = side[:, :ada_cols]
+        grad_ada_w += lax.dot_general(cond, mod_cols, contract_rows, preferred_element_type=F32)
+        mine_cols = lax.dynamic_slice_in_dim(mod_cols, my_j * bias_cols, bias_cols, axis=1)
+        grad_ada_b += jnp.sum(mine_cols.astype(F32), axis=0)
+        sums += jnp.sum(side[:, ada_cols : ada_cols + 9].astype(F32), axis=0)
+        conv_grad += side[:, ada_cols + 128 :].astype(F32).reshape(dp, -1).sum(axis=0)
+    conv_grad = conv_grad[: (taps + 1) * inner // dp].reshape(taps + 1, inner // dp)
+    conv_grad = lax.dynamic_slice_in_dim(conv_grad, my_j * own, own, axis=1).T
     out_sq, grad_sq, counted = [sums[i] + sums[i + 3] + sums[i + 6] for i in range(3)]
-    x_second = added(x_second, "fz", 0)
-    small = x_second[rows:].reshape(own, 256)
-    x_shard = jnp.concatenate([added(x_first, "dp", 0), x_second[:rows]], axis=1).astype(BF16)
+    half_way = added(half_way, "fz", 0)
+    small = half_way[rows:].reshape(own, 256)
+    x_shard = half_way[:rows].astype(BF16)
     got = lax.ppermute(jnp.where(lower, z_shard, x_shard), "dp", opposite)
     grad_in_shard = jnp.where(
         lower,

time: 664 us -> 648 us (0.976)
    another operation x8 -> x4, other arithmetic: 7.5 us -> 0.3 us  [others(): jnp.stack([v] + [swap(v, axis, k) for k in range(1, lax.axis_size(axis))])]
    ppermute x35 -> x29, waiting for transfers between devices: 64.8 us -> 58.8 us  [swap(): lax.ppermute(v, axis, [(i, i ^ k) for i in range(lax.axis_size(axis))])]
    ppermute x35 -> x29, starting transfers between devices: 36.6 us -> 32.9 us  [swap(): lax.ppermute(v, axis, [(i, i ^ k) for i in range(lax.axis_size(axis))])]
  transfers between devices with their start and end apart: 40 -> 34, of which waited for: 22 -> 20; matrix products, arithmetic and copies ran while one was open for 12% -> 12% of each run, Pallas kernels for 46% -> 47%
where the time goes in v4:
time: 648 us; the launch traced here: 639 us
  Pallas kernels  344 us (53%)
  waiting for transfers between devices  141 us (22%)
  other arithmetic  44.2 us (7%)
  local copies, waits for them, and re-layouts  40.9 us (6%)
  starting transfers between devices  36.7 us (6%)
  between operations  24.1 us (4%)
  matrix products  7.67 us (1%)
    pallas_call x2, Pallas kernels, mixer_backward(): pl.pallas_call(body, out_shape=(jax.ShapeDtypeStruct((rows, 128), F32), j...  183 us
    pallas_call x1, Pallas kernels, mixer_forward(): pl.pallas_call(body, out_shape=(big,) * 5 + (jax.ShapeDtypeStruct((2, tok...  76.3 us
    ppermute x29, waiting for transfers between devices, swap(): lax.ppermute(v, axis, [(i, i ^ k) for i in range(lax.axis_size(axis))])  58.8 us
    all_gather x1, waiting for transfers between devices, per_device(): lax.all_gather(jnp.concatenate([x_cols, packed.reshape(tail, cols)], axis...  49.9 us
    pallas_call x1, Pallas kernels, mixer_middle(): pl.pallas_call(body, grid_spec=pltpu.PrefetchScalarGridSpec(num_scalar_pr...  42.7 us
    ppermute x29, starting transfers between devices, swap(): lax.ppermute(v, axis, [(i, i ^ k) for i in range(lax.axis_size(axis))])  32.9 us
    all_gather x1, waiting for transfers between devices, per_device(): lax.all_gather(later, ALL, axis=0, tiled=True)  27.7 us
    pallas_call x1, Pallas kernels, mixer_finish(): pl.pallas_call(body, grid_spec=pltpu.PrefetchScalarGridSpec(num_scalar_pr...  23.4 us
  transfers between devices with their start and end apart: 34, of which 20 were waited for; matrix products, arithmetic and copies ran while one was open for 12% of the time, Pallas kernels for 47%

profile of v4, /device:TPU:0, one launch (start us, length us, event | category | flops | bytes accessed | tf_op | source)
XLA Modules:
  0.0 639.1 jit_solution(661946919999801221)
XLA Ops:
  8.5 3.0 collective-permute-start.14
  26.8 3.5 collective-permute-done.2
  42.2 4.1 collective-permute-start.9
  51.5 3.4 collective-permute-start.13
  57.0 3.0 fusion.25
  63.7 49.9 %all-gather.3.cloned.1.call-done = bf16[7168,768]{1,0:T(8,128)(2,1)} async-done(((bf16[224,768]{1,0:T(8,128)(2,1)}), bf16[7168,768]{1,0:T(8,128)(2,1)}) %all-gather.3.cloned.1.call-update) | async-done | bytes 11010064 | tf_op jit(solution)/shard_map/all_gather | solution.py:712
  126.0 7.1 %project.1.x_ref = f32[48,24,8,128]{3,2,1,0:T(8,128)S(1)} custom-call(bf16[384,1536]{1,0:T(8,128)(2,1)S(1)} %get-tuple-element.46.h_ref, bf16[4,8,224,768]{3,2,1,0:T(8,128)(2,1)} %bitcast.207), custom_call_target="tpu_custom_call" | custom-call | flops 3623878656 | bytes 14155776 | tf_op jit(solution)/shard_map/project/pallas_call | solution.py:110
  136.5 76.3 %mixer_forward.1 = (f32[9216,128]{1,0:T(8,128)}, f32[9216,128]{1,0:T(8,128)}, f32[9216,128]{1,0:T(8,128)}, f32[9216,128]{1,0:T(8,128)}, f32[9216,128]{1,0:T(8,128)}, /*index=5*/f32[2,384,128]{2,1,0:T(8,128)}) custom-call(f32[2,48]{1,0:T(2,128)} %pad_maximum_fusion.14.keep_ref, f32[4]{0:T(128)} %slice.326.bound_ref, f32[48,24,8,128]{3,2,1,0:T(8,128)} %copy-done.2, ...), custom_call_target="tpu_custom_call" | custom-call | flops 3019898880 | bytes 28311552 | tf_op jit(solution)/shard_map/mixer_forward/pallas_call | solution.py:203
  212.8 27.7 %all-gather.5.cloned.1.call-done = bf16[64,192,768]{2,1,0:T(8,128)(2,1)} async-done(((bf16[2,192,768]{2,1,0:T(8,128)(2,1)}), bf16[64,192,768]{2,1,0:T(8,128)(2,1)}) %all-gather.5.cloned.1.call-update) | async-done | bytes 18874384 | tf_op jit(solution)/shard_map/all_gather | solution.py:747
  240.5 42.7 %mixer_middle.1 = (f32[48,24,8,128]{3,2,1,0:T(8,128)}, bf16[384,3072]{1,0:T(8,128)(2,1)}, f32[4,384,384]{2,1,0:T(8,128)}, bf16[4,8,2,192,768]{4,3,2,1,0:T(8,128)(2,1)}) custom-call(s32[4]{0:T(128)} %constant.90.clone.place_ref, bf16[384,1536]{1,0:T(8,128)(2,1)} %copy-done.3, bf16[4,8,2,192,768]{4,3,2,1,0:T(8,128)(2,1)} %bitcast.210, ...), custom_call_target="tpu_custom_call" | custom-call | flops 18119393280 | bytes 62914560 | tf_op jit(solution)/shard_map/mixer_middle/pallas_call | solution.py:314
  284.9 92.1 %mixer_backward.3 = (f32[9216,128]{1,0:T(8,128)}, f32[256,3072]{1,0:T(8,128)}, f32[384,128]{1,0:T(8,128)}, f32[24,8,128]{2,1,0:T(8,128)}) custom-call(f32[48]{0:T(128)} %copy-done.27, f32[384,128]{1,0:T(8,128)} %get-tuple-element.125.proj_ref, f32[9216,128]{1,0:T(8,128)} %get-tuple-element.56.d_ref, f32[9216,128]{1,0:T(8,128)} %get-tuple-element.57.u_ref, ...), custom_call_target="tpu_custom_call" | custom-call | flops 3019898880 | bytes 23592960 | tf_op jit(solution)/shard_map/mixer_backward/pallas_call | solution.py:485
  377.0 91.0 %mixer_backward.2 = (f32[9216,128]{1,0:T(8,128)}, f32[256,3072]{1,0:T(8,128)}, f32[384,128]{1,0:T(8,128)}, f32[24,8,128]{2,1,0:T(8,128)}) custom-call(f32[48]{0:T(128)} %copy-done.26, f32[384,128]{1,0:T(8,128)} %get-tuple-element.126.proj_ref, f32[9216,128]{1,0:T(8,128)} %get-tuple-element.52.d_ref, f32[9216,128]{1,0:T(8,128)} %get-tuple-element.53.u_ref, ...), custom_call_target="tpu_custom_call" | custom-call | flops 3019898880 | bytes 23592960 | tf_op jit(solution)/shard_map/mixer_backward/pallas_call | solution.py:485
  468.1 23.4 %mixer_finish.1 = (bf16[4,4,192,768]{3,2,1,0:T(8,128)(2,1)}, bf16[4,4,192,768]{3,2,1,0:T(8,128)(2,1)}, bf16[384,3072]{1,0:T(8,128)(2,1)}, f32[24,5,8,128]{3,2,1,0:T(8,128)}) custom-call(s32[3]{0:T(128)} %pad_add_fusion.2.place_ref, f32[4]{0:T(128)} %slice.326.bound_ref, f32[48,24,8,128]{3,2,1,0:T(8,128)} %copy-done.2, f32[48,24,8,128]{3,2,1,0:T(8,128)} %bitcast.217, ...), custom_call_target="tpu_custom_call" | custom-call | flops 3623878656 | bytes 31457280 | tf_op jit(solution)/shard_map/mixer_finish/pallas_call | solution.py:566
  495.7 3.0 fusion.9
  508.2 5.5 add_bitcast_fusion
  519.4 3.6 copy.124
  527.7 22.2 %collective-permute-done.17 = bf16[4,224,768]{2,1,0:T(8,128)(2,1)} collective-permute-done((bf16[4,224,768]{2,1,0:T(8,128)(2,1)}, bf16[4,224,768]{2,1,0:T(8,128)(2,1)}, u32[]{:S(2)}, u32[]{:S(2)}) %collective-permute-start.17) | collective-permute-done | bytes 1376288 | tf_op jit(solution)/shard_map/ppermute | solution.py:639
  551.6 11.9 %hidden_back.1 = f32[384,1536]{1,0:T(8,128)S(1)} custom-call(bf16[384,3072]{1,0:T(8,128)(2,1)S(1)} %copy-done.5, bf16[384,3072]{1,0:T(8,128)(2,1)S(1)} %copy-done.4, bf16[4,8,224,768]{3,2,1,0:T(8,128)(2,1)} %bitcast.208, bf16[4,8,2,192,768]{4,3,2,1,0:T(8,128)(2,1)} %bitcast.212), custom_call_target="tpu_custom_call" | custom-call | flops 7247757312 | bytes 25165824 | tf_op jit(solution)/shard_map/hidden_back/pallas_call | solution.py:624
  566.6 6.1 multiply_reduce_fusion.1
  577.5 3.5 collective-permute-start.20
  581.1 4.9 collective-permute-done.25
  594.7 3.1 collective-permute-start.29
  608.9 11.5 %collective-permute-done.28 = bf16[224,768]{1,0:T(8,128)(2,1)} collective-permute-done((bf16[224,768]{1,0:T(8,128)(2,1)}, bf16[224,768]{1,0:T(8,128)(2,1)}, u32[]{:S(2)}, u32[]{:S(2)}) %collective-permute-start.28) | collective-permute-done | bytes 344096 | tf_op jit(solution)/shard_map/ppermute | solution.py:639
  625.5 3.1 collective-permute-done.30
  (265 shorter events, 109.6 us)
Async XLA Ops:
  7.2 106.4 %all-gather.3.cloned.1.call-start = ((), (), s32[]{:S(2)}) async-start(), calls=%async_computation.1 | async-start | bytes 11354112 | tf_op jit(solution)/shard_map/all_gather | solution.py:712
  8.5 10.0 %collective-permute-start.14 = (bf16[192,768]{1,0:T(8,128)(2,1)S(1)}, bf16[192,768]{1,0:T(8,128)(2,1)S(1)}, u32[]{:S(2)}, u32[]{:S(2)}) collective-permute-start(bf16[192,768]{1,0:T(8,128)(2,1)S(1)} %broadcast_select_fusion.3), channel_id=1, source_target_pairs={{0,16},{8,24},{16,0},{24,8},{1,17},{9,25},{17,1},{25,9},{2,18},{10... | collective-permute-start | bytes 884744 | tf_op jit(solution)/shard_map/ppermute | solution.py:695
  20.4 220.0 %all-gather.5.cloned.1.call-start = ((), (), s32[]{:S(2)}) async-start(), calls=%async_computation.2 | async-start | bytes 19464192 | tf_op jit(solution)/shard_map/all_gather | solution.py:747
  20.5 5.2 collective-permute-start
  25.0 5.3 collective-permute-start.2
  41.8 7.0 %collective-permute-start.10 = (f32[4,4,1152]{2,1,0:T(4,128)S(1)}, f32[4,4,1152]{2,1,0:T(4,128)S(1)}, u32[]{:S(2)}, u32[]{:S(2)}) collective-permute-start(f32[4,4,1152]{2,1,0:T(4,128)S(1)} %get-tuple-element.129), channel_id=1, source_target_pairs={{0,6},{2,4},{4,2},{6,0},{1,7},{3,5},{5,3},{7,1},{8,14},{10,12},{12... | collective-permute-start | bytes 221192 | tf_op jit(solution)/shard_map/ppermute | solution.py:639
  42.2 6.8 %collective-permute-start.8 = (f32[4,4,1152]{2,1,0:T(4,128)S(1)}, f32[4,4,1152]{2,1,0:T(4,128)S(1)}, u32[]{:S(2)}, u32[]{:S(2)}) collective-permute-start(f32[4,4,1152]{2,1,0:T(4,128)S(1)} %get-tuple-element.128), channel_id=1, source_target_pairs={{0,2},{2,0},{4,6},{6,4},{1,3},{3,1},{5,7},{7,5},{8,10},{10,8},{12,... | collective-permute-start | bytes 221192 | tf_op jit(solution)/shard_map/ppermute | solution.py:639
  42.2 9.0 %collective-permute-start.9 = (f32[4,4,1152]{2,1,0:T(4,128)S(1)}, f32[4,4,1152]{2,1,0:T(4,128)S(1)}, u32[]{:S(2)}, u32[]{:S(2)}) collective-permute-start(f32[4,4,1152]{2,1,0:T(4,128)S(1)} %get-tuple-element.127), channel_id=1, source_target_pairs={{0,4},{2,6},{4,0},{6,2},{1,5},{3,7},{5,1},{7,3},{8,12},{10,14},{12... | collective-permute-start | bytes 221192 | tf_op jit(solution)/shard_map/ppermute | solution.py:639
  51.5 5.4 collective-permute-start.13
  113.7 402.9 %reduce-scatter.2.cloned.1.call-start = ((), (), s32[]{:S(2)}) async-start(), calls=%async_computation.3 | async-start | bytes 19464192 | tf_op jit(solution)/shard_map/reduce_scatter | solution.py:789
  491.5 16.8 %collective-permute-start.15 = (bf16[4,4,192,768]{3,2,1,0:T(8,128)(2,1)}, bf16[4,4,192,768]{3,2,1,0:T(8,128)(2,1)}, u32[]{:S(2)}, u32[]{:S(2)}) collective-permute-start(bf16[4,4,192,768]{3,2,1,0:T(8,128)(2,1)} %get-tuple-element.60), channel_id=1, source_target_pairs={{0,1},{1,0},{2,3},{3,2},{4,5},{5,4},{6,7},{7,6},{8,9},{9,8},{10,11... | collective-permute-start | bytes 14155784 | tf_op jit(solution)/shard_map/ppermute | solution.py:639
  516.6 33.3 %collective-permute-start.17 = (bf16[4,224,768]{2,1,0:T(8,128)(2,1)}, bf16[4,224,768]{2,1,0:T(8,128)(2,1)}, u32[]{:S(2)}, u32[]{:S(2)}) collective-permute-start(bf16[4,224,768]{2,1,0:T(8,128)(2,1)} %get-tuple-element.69), channel_id=1, source_target_pairs={{0,8},{8,0},{16,24},{24,16},{1,9},{9,1},{17,25},{25,17},{2,10},{10... | collective-permute-start | bytes 4128776 | tf_op jit(solution)/shard_map/ppermute | solution.py:639
  524.2 61.8 %collective-permute-start.25 = (bf16[4,224,768]{2,1,0:T(8,128)(2,1)}, bf16[4,224,768]{2,1,0:T(8,128)(2,1)S(1)}, u32[]{:S(2)}, u32[]{:S(2)}) collective-permute-start(bf16[4,224,768]{2,1,0:T(8,128)(2,1)} %get-tuple-element.75), channel_id=1, source_target_pairs={{0,16},{8,24},{16,0},{24,8},{1,17},{9,25},{17,1},{25,9},{2,18},{10... | collective-permute-start | bytes 4128776 | tf_op jit(solution)/shard_map/ppermute | solution.py:639
  524.5 61.5 %collective-permute-start.26 = (bf16[4,224,768]{2,1,0:T(8,128)(2,1)}, bf16[4,224,768]{2,1,0:T(8,128)(2,1)S(1)}, u32[]{:S(2)}, u32[]{:S(2)}) collective-permute-start(bf16[4,224,768]{2,1,0:T(8,128)(2,1)} %pad_maximum_fusion.4), channel_id=1, source_target_pairs={{0,24},{8,16},{16,8},{24,0},{1,25},{9,17},{17,9},{25,1},{2,26},{10... | collective-permute-start | bytes 4128776 | tf_op jit(solution)/shard_map/ppermute | solution.py:639
  576.6 11.6 %collective-permute-start.18 = (bf16[4,8576]{1,0:T(4,128)(2,1)S(1)}, bf16[4,8576]{1,0:T(4,128)(2,1)S(1)}, u32[]{:S(2)}, u32[]{:S(2)}) collective-permute-start(bf16[4,8576]{1,0:T(4,128)(2,1)S(1)} %fusion.46), channel_id=1, source_target_pairs={{0,2},{2,0},{4,6},{6,4},{1,3},{3,1},{5,7},{7,5},{8,10},{10,8},{12,... | collective-permute-start | bytes 205832 | tf_op jit(solution)/shard_map/ppermute | solution.py:639
  576.7 11.5 %collective-permute-start.19 = (bf16[4,8576]{1,0:T(4,128)(2,1)S(1)}, bf16[4,8576]{1,0:T(4,128)(2,1)S(1)}, u32[]{:S(2)}, u32[]{:S(2)}) collective-permute-start(bf16[4,8576]{1,0:T(4,128)(2,1)S(1)} %fusion.46), channel_id=1, source_target_pairs={{0,4},{2,6},{4,0},{6,2},{1,5},{3,7},{5,1},{7,3},{8,12},{10,14},{12... | collective-permute-start | bytes 205832 | tf_op jit(solution)/shard_map/ppermute | solution.py:639
  577.5 10.6 %collective-permute-start.20 = (bf16[4,8576]{1,0:T(4,128)(2,1)S(1)}, bf16[4,8576]{1,0:T(4,128)(2,1)S(1)}, u32[]{:S(2)}, u32[]{:S(2)}) collective-permute-start(bf16[4,8576]{1,0:T(4,128)(2,1)S(1)} %fusion.46), channel_id=1, source_target_pairs={{0,6},{2,4},{4,2},{6,0},{1,7},{3,5},{5,3},{7,1},{8,14},{10,12},{12... | collective-permute-start | bytes 205832 | tf_op jit(solution)/shard_map/ppermute | solution.py:639
  588.9 5.8 collective-permute-start.21
  590.0 7.8 %collective-permute-start.22 = (bf16[4,4,1536]{2,1,0:T(4,128)(2,1)S(1)}, bf16[4,4,1536]{2,1,0:T(4,128)(2,1)S(1)}, u32[]{:S(2)}, u32[]{:S(2)}) collective-permute-start(bf16[4,4,1536]{2,1,0:T(4,128)(2,1)S(1)} %get-tuple-element.156), channel_id=1, source_target_pairs={{0,16},{8,24},{16,0},{24,8},{1,17},{9,25},{17,1},{25,9},{2,18},{10... | collective-permute-start | bytes 147464 | tf_op jit(solution)/shard_map/ppermute | solution.py:639
  591.1 6.8 %collective-permute-start.23 = (bf16[4,4,1536]{2,1,0:T(4,128)(2,1)S(1)}, bf16[4,4,1536]{2,1,0:T(4,128)(2,1)S(1)}, u32[]{:S(2)}, u32[]{:S(2)}) collective-permute-start(bf16[4,4,1536]{2,1,0:T(4,128)(2,1)S(1)} %get-tuple-element.157), channel_id=1, source_target_pairs={{0,24},{8,16},{16,8},{24,0},{1,25},{9,17},{17,9},{25,1},{2,26},{10... | collective-permute-start | bytes 147464 | tf_op jit(solution)/shard_map/ppermute | solution.py:639
  593.4 15.5 %collective-permute-start.27 = (bf16[224,768]{1,0:T(8,128)(2,1)}, bf16[224,768]{1,0:T(8,128)(2,1)}, u32[]{:S(2)}, u32[]{:S(2)}) collective-permute-start(bf16[224,768]{1,0:T(8,128)(2,1)} %get-tuple-element.115), channel_id=1, source_target_pairs={{0,2},{2,0},{4,6},{6,4},{1,3},{3,1},{5,7},{7,5},{8,10},{10,8},{12,... | collective-permute-start | bytes 1032200 | tf_op jit(solution)/shard_map/ppermute | solution.py:639
  593.4 27.0 %collective-permute-start.28 = (bf16[224,768]{1,0:T(8,128)(2,1)}, bf16[224,768]{1,0:T(8,128)(2,1)}, u32[]{:S(2)}, u32[]{:S(2)}) collective-permute-start(bf16[224,768]{1,0:T(8,128)(2,1)} %get-tuple-element.117), channel_id=1, source_target_pairs={{0,4},{2,6},{4,0},{6,2},{1,5},{3,7},{5,1},{7,3},{8,12},{10,14},{12... | collective-permute-start | bytes 1032200 | tf_op jit(solution)/shard_map/ppermute | solution.py:639
  594.7 25.7 %collective-permute-start.29 = (bf16[224,768]{1,0:T(8,128)(2,1)}, bf16[224,768]{1,0:T(8,128)(2,1)}, u32[]{:S(2)}, u32[]{:S(2)}) collective-permute-start(bf16[224,768]{1,0:T(8,128)(2,1)} %get-tuple-element.116), channel_id=1, source_target_pairs={{0,6},{2,4},{4,2},{6,0},{1,7},{3,5},{5,3},{7,1},{8,14},{10,12},{12... | collective-permute-start | bytes 1032200 | tf_op jit(solution)/shard_map/ppermute | solution.py:639
  621.9 6.8 %collective-permute-start.30 = (bf16[192,768]{1,0:T(8,128)(2,1)S(1)}, bf16[192,768]{1,0:T(8,128)(2,1)S(1)}, u32[]{:S(2)}, u32[]{:S(2)}) collective-permute-start(bf16[192,768]{1,0:T(8,128)(2,1)S(1)} %get-tuple-element.83), channel_id=1, source_target_pairs={{0,16},{8,24},{16,0},{24,8},{1,17},{9,25},{17,1},{25,9},{2,18},{10... | collective-permute-start | bytes 884744 | tf_op jit(solution)/shard_map/ppermute | solution.py:913
  (38 other events, 398.0 us)
Sparse Core Ops, SparseCore 0:
  20.6 93.0 all-gather.2
  117.3 123.1 all-gather.4
  283.3 204.9 reduce-scatter.1
